TPU v7x, 32 devices: a whole 2x2x4 slice. The times are simulated.
32 devices in a mesh: depth: 2 (over x), sky: 16 (over z, y, core).
Axes of the slice: x: 2, y: 2, z: 4, core: 2. Of those that a mesh axis runs over, the one named last changes fastest.
Arguments:
- potential: float32 [24, 512, 2048], P('depth', 'sky'), may hold values from -6 to 6
- widths: int32 [24], P('depth'), may hold values from 1 to 8, as said below
- plane_slot: int32 [24], P('depth'), may hold values from 0 to 15
- ratio_near: float32 [16], replicated, may hold values from 1 to 1.6
- ratio_lens: float32 [16], replicated, may hold values from 0.5 to 1.5
Outputs:
- convergence: float32 [24, 512, 2048], P('depth', 'sky')
Inputs may be any that keep to these rules, and one draw needn't show every extreme that they name: `widths`: some plane has half-width 8.
All inputs are finite; a program needn't handle non-finite values.
Results may differ from a plain program's by a relative error of at most 0.0003.
Values sent between devices are 32-bit elements; how exact they have to be, the bound alone decides.
No kernel may reach another device: no remote copies, remote signals or barrier semaphores. Data moves between devices by JAX's collectives and lax.ppermute only.
A program may use at most 64 MiB of HBM per device.

v0:
```python
import jax
import jax.numpy as jnp
from jax import lax
from jax.sharding import PartitionSpec as P

WMAX = 8


def padded_2(x, sides, width):
    for axis, dim in sides:
        devices, length = (lax.axis_size(axis), x.shape[dim])
        up = [(i, (i + 1) % devices) for i in range(devices - 1)]
        down = [(j, i) for i, j in up]
        last = lax.slice_in_dim(x, length - width, length, axis=dim)
        first = lax.slice_in_dim(x, 0, width, axis=dim)
        before = lax.ppermute(last, axis, up)
        after = lax.ppermute(first, axis, down)
        x = jnp.concatenate([before, x, after], axis=dim)
    return x


def passed_along(value, axis, steps):
    count = lax.axis_size(axis)
    first, last = (max(0, -steps), min(count, count - steps))
    return lax.ppermute(value, axis, [(source, source + steps) for source in range(first, last)])


def box_filter(values, half_width, axis_index, length):
    summed = None
    for displace in range(-WMAX, WMAX + 1):
        window = lax.slice_in_dim(
            values, WMAX + displace, WMAX + displace + length, axis=axis_index
        )
        active = jnp.where(abs(displace) <= half_width, 1.0, 0.0).astype(jnp.float32)
        term = active * window
        summed = term if summed is None else summed + term
    return summed / (2.0 * half_width.astype(jnp.float32) + 1.0)


def hessian(padded, half_width, row_count, col_count):
    along = box_filter(padded, half_width, 0, row_count + 2)
    smooth = box_filter(along, half_width, 1, col_count + 2)
    centre = smooth[1:-1, 1:-1]
    along_cols = smooth[1:-1, 2:] - 2.0 * centre + smooth[1:-1, :-2]
    along_rows = smooth[2:, 1:-1] - 2.0 * centre + smooth[:-2, 1:-1]
    mixed_term = 0.25 * (smooth[2:, 2:] - smooth[2:, :-2] - smooth[:-2, 2:] + smooth[:-2, :-2])
    return (along_cols, along_rows, mixed_term)


def advance(carried, along_cols, along_rows, mixed_term, near_factor, lens_factor):
    entry_xx = near_factor - lens_factor * along_cols
    entry_yy = near_factor - lens_factor * along_rows
    entry_xy = -lens_factor * mixed_term
    retained = 1.0 - near_factor
    upper = carried[0:2]
    lower = carried[2:4]
    row_first = entry_xx * upper[0] + entry_xy * upper[1] + retained * lower[0]
    row_second = entry_xy * upper[0] + entry_yy * upper[1] + retained * lower[1]
    advanced = jnp.stack([row_first, row_second, upper[0], upper[1]])
    convergence = 1.0 - 0.5 * (row_first[0] + row_second[1])
    return (advanced, convergence)


def identity_state(row_count, col_count):
    pattern = jnp.array([[1.0, 0.0], [0.0, 1.0], [1.0, 0.0], [0.0, 1.0]], dtype=jnp.float32)
    return jnp.broadcast_to(pattern[:, :, None, None], (4, 2, row_count, col_count))


def propagate(carried, curvatures, near_factor, lens_factor):

    def plane(loop_state, inputs):
        along_cols, along_rows, mixed_term, near_one, lens_one = inputs
        return advance(loop_state, along_cols, along_rows, mixed_term, near_one, lens_one)

    return lax.scan(
        plane, carried, (curvatures[0], curvatures[1], curvatures[2], near_factor, lens_factor)
    )


def factors_of(slots, ratio_near, ratio_lens):
    table_ids = jnp.arange(ratio_near.shape[0], dtype=jnp.int32)
    chosen = (slots[:, None] == table_ids[None, :]).astype(jnp.float32)
    near_factor = jnp.sum(chosen * ratio_near[None, :], axis=1)
    lens_factor = jnp.sum(chosen * ratio_lens[None, :], axis=1)
    return (near_factor, lens_factor)


def per_device(potential, widths, plane_slot, ratio_near, ratio_lens):
    row_count = potential.shape[1]
    col_count = potential.shape[2]
    rim_rows = WMAX + 1
    extended = padded_2(potential, (("sky", 1),), rim_rows)
    depth_index = lax.axis_index("depth")
    depth_count = lax.axis_size("depth")
    is_first = depth_index == 0

    def curvature(inputs):
        plane_map, half_width = inputs
        padded = jnp.pad(plane_map, ((0, 0), (rim_rows, rim_rows)))
        return hessian(padded, half_width, row_count, col_count)

    curvatures = lax.map(curvature, (extended, widths))
    near_factor, lens_factor = factors_of(plane_slot, ratio_near, ratio_lens)
    initial = identity_state(row_count, col_count)

    def relay_round(round_index, incoming):
        outgoing, unused = propagate(incoming, curvatures, near_factor, lens_factor)
        received = passed_along(outgoing, "depth", 1)
        return jnp.where(is_first, initial, received)

    incoming = lax.fori_loop(0, depth_count - 1, relay_round, initial)
    final_state, convergence = propagate(incoming, curvatures, near_factor, lens_factor)
    return convergence


def solution(mesh):
    return jax.shard_map(
        per_device,
        mesh=mesh,
        in_specs=(P("depth", "sky", None), P("depth"), P("depth"), P(), P()),
        out_specs=P("depth", "sky", None),
        check_vma=False,
    )
```

profile of v0, /device:TPU:6, one launch (start us, length us, event | category | flops | bytes accessed | tf_op | source)
XLA Modules:
  0.0 433.5 jit_solution(1381082132436083739)
XLA Ops:
  0.0 2.3 fusion.49
  3.9 1.9 collective-permute-start
  7.3 3.9 collective-permute-start.1
  11.5 22.9 %collective-permute-done = f32[12,9,2048]{2,0,1:T(8,128)} collective-permute-done((f32[12,9,2048]{2,0,1:T(8,128)}, f32[12,9,2048]{2,0,1:T(8,128)}, u32[]{:S(2)}, u32[]{:S(2)}) %collective-permute-start) | collective-permute-done | bytes 884768 | tf_op jit(solution)/shard_map/ppermute | solution.py:16
  34.4 1.8 copy.13
  36.2 1.8 copy.14
  38.1 3.3 pad_maximum_fusion.2
  41.8 2.1 broadcast.59.clone.1
  43.8 2.0 broadcast.59.clone.2
  45.9 150.6 %while.45 = (s32[]{:T(128)}, f32[12,32,2048]{2,1,0:T(8,128)S(1)}, f32[12,32,2048]{2,1,0:T(8,128)}, f32[12,32,2048]{2,1,0:T(8,128)}, s32[12]{0:T(128)S(1)}, /*ind...) while((s32[]{:T(128)}, f32[12,32,2048]{2,1,0:T(8,128)S(1)}, ...), condition=%wide.region_1.2_spmd, body=%wide.region_0.1_spmd.sunk | while | flops 5347943 | bytes 9674915 | solution.py:102
  196.4 1.6 copy-done.1
  198.3 90.9 %while.46 = (s32[]{:T(128)}, f32[4,2,32,2048]{3,2,1,0:T(8,128)S(1)}, f32[12]{0:T(128)S(1)}, f32[12]{0:T(128)S(1)}, f32[12,32,2048]{2,1,0:T(8,128)}, /*index=5*/f...) while((s32[]{:T(128)}, f32[4,2,32,2048]{3,2,1,0:T(8,128)S(1)}, f32[12]{0:T(128)S(1)}, ...), condition=%wide.region_5.6_spmd, body=%wide.region_4.5_spmd.sunk | while | flops 2686980 | bytes 11796649 | solution.py:75
  200.1 2.3 subtract_bitcast_fusion.8
  202.5 2.2 subtract_bitcast_fusion.9
  207.7 2.3 subtract_bitcast_fusion.8
  210.1 2.2 subtract_bitcast_fusion.9
  215.3 2.3 subtract_bitcast_fusion.8
  217.6 2.2 subtract_bitcast_fusion.9
  222.9 2.3 subtract_bitcast_fusion.8
  225.2 2.2 subtract_bitcast_fusion.9
  230.4 2.3 subtract_bitcast_fusion.8
  232.8 2.2 subtract_bitcast_fusion.9
  238.0 2.3 subtract_bitcast_fusion.8
  240.4 2.2 subtract_bitcast_fusion.9
  245.6 2.3 subtract_bitcast_fusion.8
  247.9 2.2 subtract_bitcast_fusion.9
  253.2 2.3 subtract_bitcast_fusion.8
  255.5 2.2 subtract_bitcast_fusion.9
  260.7 2.3 subtract_bitcast_fusion.8
  263.1 2.2 subtract_bitcast_fusion.9
  268.3 2.3 subtract_bitcast_fusion.8
  270.6 2.2 subtract_bitcast_fusion.9
  275.9 2.3 subtract_bitcast_fusion.8
  278.2 2.2 subtract_bitcast_fusion.9
  283.5 2.3 subtract_bitcast_fusion.8
  285.8 2.2 subtract_bitcast_fusion.9
  290.5 40.1 %collective-permute-done.2 = f32[4,2,32,2048]{3,2,1,0:T(8,128)} collective-permute-done((f32[4,2,32,2048]{3,2,1,0:T(8,128)S(1)}, f32[4,2,32,2048]{3,2,1,0:T(8,128)}, u32[]{:S(2)}, u32[]{:S(2)}) %collective-permute-start.2) | collective-permute-done | bytes 2097184 | tf_op jit(solution)/shard_map/while/body/eval_jaxpr/ppermute | solution.py:25
  330.6 1.9 broadcast_select_fusion
  332.5 2.0 broadcast.59
  334.5 99.0 %while.47 = (s32[]{:T(128)}, f32[4,2,32,2048]{3,2,1,0:T(8,128)S(1)}, f32[12,32,2048]{2,1,0:T(8,128)}, f32[12]{0:T(128)S(1)}, f32[12]{0:T(128)S(1)}, /*index=5*/f...) while((s32[]{:T(128)}, ...), condition=%wide.region_7.8_spmd, body=%wide.region_6.7_spmd.sunk | while | flops 3407876 | bytes 16515761 | solution.py:75
  336.3 2.2 subtract_bitcast_fusion.10
  338.5 2.2 subtract_bitcast_fusion.11
  344.6 2.2 subtract_bitcast_fusion.10
  346.8 2.2 subtract_bitcast_fusion.11
  352.8 2.2 subtract_bitcast_fusion.10
  355.1 2.2 subtract_bitcast_fusion.11
  361.1 2.2 subtract_bitcast_fusion.10
  363.3 2.2 subtract_bitcast_fusion.11
  369.3 2.2 subtract_bitcast_fusion.10
  371.6 2.2 subtract_bitcast_fusion.11
  377.6 2.2 subtract_bitcast_fusion.10
  379.8 2.2 subtract_bitcast_fusion.11
  385.8 2.2 subtract_bitcast_fusion.10
  388.1 2.2 subtract_bitcast_fusion.11
  394.1 2.2 subtract_bitcast_fusion.10
  396.3 2.2 subtract_bitcast_fusion.11
  402.3 2.2 subtract_bitcast_fusion.10
  404.6 2.2 subtract_bitcast_fusion.11
  410.6 2.2 subtract_bitcast_fusion.10
  412.8 2.2 subtract_bitcast_fusion.11
  418.8 2.2 subtract_bitcast_fusion.10
  421.1 2.2 subtract_bitcast_fusion.11
  427.1 2.2 subtract_bitcast_fusion.10
  429.3 2.2 subtract_bitcast_fusion.11
  (212 shorter events, 129.3 us)
Async XLA Ops:
  2.3 8.9 %copy-start.3 = (f32[16]{0:T(128)S(1)}, f32[16]{0:T(128)}, u32[]{:S(2)}) copy-start(f32[16]{0:T(128)} %param.16) | copy-start | bytes 196
  2.3 8.9 %copy-start.4 = (s32[12]{0:T(128)S(1)}, s32[12]{0:T(128)}, u32[]{:S(2)}) copy-start(s32[12]{0:T(128)} %param.14) | copy-start | bytes 148
  2.3 8.9 %copy-start.5 = (f32[16]{0:T(128)S(1)}, f32[16]{0:T(128)}, u32[]{:S(2)}) copy-start(f32[16]{0:T(128)} %param.15) | copy-start | bytes 196
  3.9 30.5 %collective-permute-start = (f32[12,9,2048]{2,0,1:T(8,128)}, f32[12,9,2048]{2,0,1:T(8,128)}, u32[]{:S(2)}, u32[]{:S(2)}) collective-permute-start(f32[12,9,2048]{2,0,1:T(8,128)} %copy.15), channel_id=1, source_target_pairs={{0,1},{1,2},{2,3},{3,4},{4,5},{5,6},{6,7},{7,8},{8,9},{9,10},{10,1... | collective-permute-start | bytes 2654216 | tf_op jit(solution)/shard_map/ppermute | solution.py:16
  7.3 30.7 %copy-start = (f32[12,32,2048]{2,1,0:T(8,128)S(1)}, f32[12,32,2048]{2,1,0:T(8,128)}, u32[]{:S(2)}) copy-start(f32[12,32,2048]{2,1,0:T(8,128)} %param.12) | copy-start | bytes 9437188
  7.3 28.9 %collective-permute-start.1 = (f32[12,9,2048]{2,0,1:T(8,128)}, f32[12,9,2048]{2,0,1:T(8,128)}, u32[]{:S(2)}, u32[]{:S(2)}) collective-permute-start(f32[12,9,2048]{2,0,1:T(8,128)} %copy.16), channel_id=1, source_target_pairs={{1,0},{2,1},{3,2},{4,3},{5,4},{6,5},{7,6},{8,7},{9,8},{10,9},{11,1... | collective-permute-start | bytes 2654216 | tf_op jit(solution)/shard_map/ppermute | solution.py:17
  41.7 4.1 copy-start.6
  45.9 152.2 %copy-start.2 = (f32[4,2]{1,0:T(4,128)S(1)}, f32[4,2]{1,0:T(4,128)}, u32[]{:S(2)}) copy-start(f32[4,2]{1,0:T(4,128)} %constant.157.clone) | copy-start | bytes 100
  196.4 1.6 copy-start.1
  289.2 41.4 %collective-permute-start.2 = (f32[4,2,32,2048]{3,2,1,0:T(8,128)S(1)}, f32[4,2,32,2048]{3,2,1,0:T(8,128)}, u32[]{:S(2)}, u32[]{:S(2)}) collective-permute-start(f32[4,2,32,2048]{3,2,1,0:T(8,128)S(1)} %get-tuple-element.193), channel_id=1, source_target_pairs={{0,16},{1,17},{2,18},{3,19},{4,20},{5,21},{6,22},{7,23},{8,24},{9,... | collective-permute-start | bytes 6291464 | tf_op jit(solution)/shard_map/while/body/eval_jaxpr/ppermute | solution.py:25
where the time goes:
time: 438 us; the launch traced here: 434 us
  other arithmetic  186 us (42%)
  loops' own time  109 us (25%)
  local copies, waits for them, and re-layouts  68.2 us (16%)
  waiting for transfers between devices  63 us (14%)
  starting transfers between devices  7.1 us (2%)
    another operation x1, loops' own time, per_device(): curvatures = lax.map(curvature, (extended, widths))  78.1 us
    mul x36, other arithmetic, advance(): row_first = entry_xx * upper[0] + entry_xy * upper[1] + retained * lower[0]  56.2 us
    mul x24, other arithmetic, advance(): row_second = entry_xy * upper[0] + entry_yy * upper[1] + retained * lower[1]  54.9 us
    ppermute x1, waiting for transfers between devices, passed_along(): lax.ppermute(value, axis, [(source, source + steps) for source in range(f...  40.1 us
    div x24, other arithmetic, box_filter(): return summed / (2.0 * half_width.astype(jnp.float32) + 1.0)  37.6 us
    another operation x2, loops' own time, propagate(): lax.scan(plane, carried, (curvatures[0], curvatures[1], curvatures[2], ne...  30.6 us
    dynamic_slice x48, local copies, waits for them, and re-layouts, propagate(): lax.scan(plane, carried, (curvatures[0], curvatures[1], curvatures[2], ne...  29.5 us
    dynamic_update_slice x24, other arithmetic, per_device(): curvatures = lax.map(curvature, (extended, widths))  25.9 us
  transfers between devices with their start and end apart: 3, of which 2 were waited for; matrix products, arithmetic and copies ran while one was open for 1% of the time, Pallas kernels for 0%

commit v1 on v0

v1 whole, which is shorter than its diff:
```python
import functools

import jax
import jax.numpy as jnp
from jax import lax
from jax.experimental import pallas as pl
from jax.experimental.pallas import tpu as pltpu
from jax.sharding import PartitionSpec as P

WMAX = 8
RIM = WMAX + 1
LANES = 128
SUB = 8
EDGES = (RIM, 5, 0)
VMEM_LIMIT = 16 * 1024 * 1024
F32 = jnp.float32


def row_groups(row_count):
    groups = [((RIM, row_count - RIM),)]
    for outer, inner in zip(EDGES[:-1], EDGES[1:]):
        groups.append(((inner, outer), (row_count - outer, row_count - inner)))
    return groups


def rows_in(group):
    return sum(stop - start for start, stop in group)


class ShiftLeft:
    def __init__(self, lane, distance):
        self.lane, self.distance, self.held = lane, distance, None

    def __call__(self, block):
        zero = jnp.zeros((SUB, LANES), F32)
        rolled = zero if block is None else pltpu.roll(block, LANES - self.distance, 1)
        held = zero if self.held is None else self.held
        self.held = rolled
        return jnp.where(self.lane < LANES - self.distance, rolled, held)


class ShiftRight:
    def __init__(self, lane, distance):
        self.lane, self.distance, self.held = lane, distance, None

    def __call__(self, block):
        rolled = pltpu.roll(block, self.distance, 1) if self.distance else block
        held, self.held = self.held, rolled
        if held is None:
            return None
        return jnp.where(self.lane >= self.distance, held, rolled) if self.distance else held


def window_sums(lane, half_width):
    shift = lambda distance: ShiftLeft(lane, distance)
    plus = lambda a, b: b if a is None else a + b
    s = [shift(d) for d in {1: (1, 2), 2: (1, 2, 4), 3: (1, 2, 3, 6), 4: (1, 2, 3, 6), 5: (1, 2, 4, 2, 8),
                            6: (1, 2, 3, 6, 12), 7: (1, 2, 3, 5, 10), 8: (1, 2, 4, 8, 16)}[half_width]]

    def sums(x):
        p2 = plus(x, s[0](x))
        if half_width in (2, 5, 8):
            p4 = p2 + s[1](p2)
            if half_width == 2:
                return p4 + s[2](x)
            p8 = p4 + s[2](p4)
            if half_width == 5:
                return p8 + s[4](p2 + s[3](x))
            return p8 + s[3](p8) + s[4](x)
        p3 = p2 + s[1](x)
        if half_width == 1:
            return p3
        if half_width == 7:
            p5 = p3 + s[2](p2)
            return p5 + s[3](p5) + s[4](p5)
        p6 = p3 + s[2](p3)
        if half_width == 3:
            return p6 + s[3](x)
        if half_width == 4:
            return p6 + s[3](p3)
        return p6 + s[3](p6) + s[4](x)

    return sums


def column_stage(blocks, half_width, load, store):
    lane = lax.broadcasted_iota(jnp.int32, (SUB, LANES), 1)
    sums = window_sums(lane, half_width)
    right = [ShiftRight(lane, half_width + step) for step in (0, -1, 1)]
    for block in range(blocks - 1, -2, -1):
        total = sums(load(block) if block >= 0 else None)
        centre, after, before = [shift(total) for shift in right]
        if centre is not None:
            store(block + 1, (centre, after + before - 2.0 * centre, after - before))


def for_each_width(half_width, body):
    for candidate in range(1, WMAX + 1):

        @pl.when(half_width == candidate)
        def _(candidate=candidate):
            body(candidate)


def own_columns(k, half_width, rows, blocks, x_ref, field_ref):
    def with_width(static_width):
        def tile(index, carry):
            base = index * (SUB * blocks)

            def load(block):
                return x_ref[k, pl.ds(pl.multiple_of(base + block * SUB, SUB), SUB), :]

            def store(block, values):
                start = base + RIM * blocks + block
                for field, value in enumerate(values):
                    field_ref[k, field, pl.ds(start, SUB, stride=blocks), :] = value

            column_stage(blocks, static_width, load, store)
            return carry

        lax.fori_loop(0, rows // SUB, tile, 0)

    for_each_width(half_width, with_width)


def halo_columns(k, half_width, rows, blocks, sides, tile_ref, stage_ref, field_ref):
    places = []
    for ref, first, count in sides:
        for i in range(count):
            slot = len(places)
            places.append(first + i)
            for half in range(blocks // SUB):
                start = (slot // SUB) * SUB * blocks + half * SUB * SUB + slot % SUB
                tile_ref[pl.ds(start, SUB, stride=SUB), :] = ref[k, pl.ds(i * blocks + half * SUB, SUB), :]
    tiles = -(-len(places) // SUB)

    def with_width(static_width):
        for index in range(tiles):
            base = index * (SUB * blocks)

            def load(block):
                return tile_ref[pl.ds(base + block * SUB, SUB), :]

            def store(block, values):
                for field, value in enumerate(values):
                    stage_ref[field, pl.ds(base + block, SUB, stride=blocks), :] = value

            column_stage(blocks, static_width, load, store)

    for_each_width(half_width, with_width)
    for slot, row in enumerate(places):
        for field in range(3):
            field_ref[k, field, pl.ds((row + RIM) * blocks, blocks), :] = stage_ref[
                field, pl.ds(slot * blocks, blocks), :
            ]


def row_stage(k, half_width, near, scale, group, blocks, field_ref, entry_ref):
    def row(field, index):
        return field_ref[k, field, pl.ds(pl.multiple_of(index * blocks, blocks), blocks), :]

    place = 0
    for start, stop in group:
        first = start + RIM
        along = lax.fori_loop(
            0, 2 * half_width + 1, lambda i, total: total + row(1, first - half_width + i),
            jnp.zeros((blocks, LANES), F32),
        )
        for at in range(first, stop + RIM):
            high, low = at + half_width, at - half_width
            across = (row(0, high + 1) - row(0, high)) - (row(0, low) - row(0, low - 1))
            mixed = (row(2, high + 1) + row(2, high)) - (row(2, low) + row(2, low - 1))
            where = pl.ds(place * blocks, blocks)
            entry_ref[k, 0, where, :] = near - scale * along
            entry_ref[k, 1, where, :] = near - scale * across
            entry_ref[k, 2, where, :] = (-0.25 * scale) * mixed
            if at + 1 < stop + RIM:
                along = along + (row(1, high + 1) - row(1, low))
            place += 1


def sweep(planes, length, near_of, entry_ref, conv_ref, start, finish):
    step = 4 * SUB if length % (4 * SUB) == 0 else SUB

    def part(index, carry):
        where = pl.ds(pl.multiple_of(index * step, step), step)
        state = start(where, (step, LANES))
        now, then = state[:4], state[4:]
        for k in range(planes):
            xx, yy, xy = [entry_ref[k, i, where, :] for i in range(3)]
            kept = 1.0 - near_of(k)
            new = [
                xx * now[0] + xy * now[2] + kept * then[0],
                xx * now[1] + xy * now[3] + kept * then[1],
                xy * now[0] + yy * now[2] + kept * then[2],
                xy * now[1] + yy * now[3] + kept * then[3],
            ]
            now, then = new, now
            conv_ref[k, where, :] = 1.0 - 0.5 * (new[0] + new[3])
        finish(where, now + then)
        return carry

    lax.fori_loop(0, length // step, part, 0)


def identity_state(where, shape):
    one, zero = jnp.ones(shape, F32), jnp.zeros(shape, F32)
    return [one, zero, zero, one] * 2


def writer(state_ref):
    def finish(where, state):
        for i, value in enumerate(state):
            state_ref[i, where, :] = value

    return finish


def scalars_of(k, widths, slots, near, lens):
    half_width = widths[k]
    count = (2 * half_width + 1).astype(F32)
    return half_width, near[slots[k]], lens[slots[k]] / (count * count)


def first_kernel(sizes, widths, slots, near, lens, x_hbm, field_ref, entry_ref, conv_ref, state_ref, *rest):
    planes, rows, blocks, groups = sizes
    sends, (x_ref, sems) = rest[:-2], rest[-2:]
    copies = [pltpu.make_async_copy(x_hbm.at[k], x_ref.at[k], sems.at[k]) for k in range(planes)]
    for copy in copies:
        copy.start()
    group = groups[0]

    def plane(k, carry):
        pltpu.make_async_copy(x_hbm.at[k], x_ref.at[k], sems.at[k]).wait()
        half_width, near_k, scale = scalars_of(k, widths, slots, near, lens)
        own_columns(k, half_width, rows, blocks, x_ref, field_ref)
        row_stage(k, half_width, near_k, scale, group, blocks, field_ref, entry_ref)
        for part, (outer, inner) in enumerate(zip(EDGES[:-1], EDGES[1:])):
            begin, count = RIM - outer, outer - inner
            for ref, first in ((sends[2 * part], rows - begin - count), (sends[2 * part + 1], begin)):
                for i in range(count):
                    row = first + i
                    for half in range(blocks // SUB):
                        start = (row // SUB) * SUB * blocks + half * SUB * SUB + row % SUB
                        ref[k, pl.ds(i * blocks + half * SUB, SUB), :] = x_ref[k, pl.ds(start, SUB, stride=SUB), :]
        return carry

    lax.fori_loop(0, planes, plane, 0)

    @pl.when(lax.axis_index("depth") == 0)
    def _():
        sweep(planes, rows_in(group) * blocks, lambda k: near[slots[k]], entry_ref, conv_ref, identity_state,
              writer(state_ref))


def later_kernel(sizes, part, widths, slots, near, lens, field_in, before, after, field_ref, entry_ref, conv_ref,
                 state_ref, tile_ref, stage_ref):
    planes, rows, blocks, groups = sizes
    group = groups[part + 1]
    outer, inner = EDGES[part], EDGES[part + 1]
    begin, count = RIM - outer, outer - inner

    def plane(k, carry):
        half_width, near_k, scale = scalars_of(k, widths, slots, near, lens)
        sides = ((before, -begin - count, count), (after, rows + begin, count))
        halo_columns(k, half_width, rows, blocks, sides, tile_ref, stage_ref, field_ref)
        row_stage(k, half_width, near_k, scale, group, blocks, field_ref, entry_ref)
        return carry

    lax.fori_loop(0, planes, plane, 0)

    @pl.when(lax.axis_index("depth") == 0)
    def _():
        sweep(planes, rows_in(group) * blocks, lambda k: near[slots[k]], entry_ref, conv_ref, identity_state,
              writer(state_ref))


def resume_kernel(sizes, part, turn, slots, near, entry_ref, incoming, conv_in, conv_ref, *state_ref):
    planes, rows, blocks, groups = sizes

    @pl.when(lax.axis_index("depth") == turn)
    def _():
        sweep(planes, rows_in(groups[part]) * blocks, lambda k: near[slots[k]], entry_ref, conv_ref,
              lambda where, shape: [incoming[i, where, :] for i in range(8)],
              writer(state_ref[0]) if state_ref else lambda where, state: None)


def gather_kernel(sizes, *refs):
    planes, rows, blocks, groups = sizes
    out_ref = refs[-1]
    k = pl.program_id(0)
    for group, conv_ref in zip(groups, refs):
        place = 0
        for start, stop in group:
            for row in range(start, stop):
                for half in range(blocks // SUB):
                    to = (row // SUB) * SUB * blocks + half * SUB * SUB + row % SUB
                    out_ref[0, pl.ds(to, SUB, stride=SUB), :] = conv_ref[k, pl.ds(place * blocks + half * SUB, SUB), :]
                place += 1


def per_device(potential, widths, plane_slot, ratio_near, ratio_lens):
    planes, rows, cols = potential.shape
    blocks = cols // LANES
    groups = row_groups(rows)
    sizes = (planes, rows, blocks, groups)
    depth_count, sky_count = lax.axis_size("depth"), lax.axis_size("sky")
    up = [(i, i + 1) for i in range(sky_count - 1)]
    down = [(j, i) for i, j in up]
    ahead = [(i, i + 1) for i in range(depth_count - 1)]
    tiled = potential.reshape(planes, rows // SUB, SUB, blocks, LANES).transpose(0, 1, 3, 2, 4)
    tiled = tiled.reshape(planes, rows * blocks, LANES)
    smem = pl.BlockSpec(memory_space=pltpu.SMEM)
    vmem = pl.BlockSpec(memory_space=pltpu.VMEM)
    params = pltpu.CompilerParams(vmem_limit_bytes=VMEM_LIMIT)
    scalars = (widths, plane_slot, ratio_near, ratio_lens)

    def held(*shape):
        return pltpu.VMEM(shape, F32)

    def moved(*shape):
        return jax.ShapeDtypeStruct(shape, F32)

    field_shape = held(planes, 3, (rows + 2 * RIM) * blocks, LANES)

    def group_shapes(part):
        length = rows_in(groups[part]) * blocks
        return [held(planes, 3, length, LANES), held(planes, length, LANES), moved(8, length, LANES)]

    sends = []
    for outer, inner in zip(EDGES[:-1], EDGES[1:]):
        sends += [moved(planes, (outer - inner) * blocks, LANES)] * 2
    field, entry, conv, state, *packed = pl.pallas_call(
        functools.partial(first_kernel, sizes),
        out_shape=[field_shape, *group_shapes(0), *sends],
        in_specs=[smem] * 4 + [pl.BlockSpec(memory_space=pl.ANY)],
        out_specs=[vmem] * (4 + len(sends)),
        scratch_shapes=[pltpu.VMEM((planes, rows * blocks, LANES), F32), pltpu.SemaphoreType.DMA((planes,))],
        compiler_params=params,
        name="interior",
    )(*scalars, tiled)
    entries, convs, states = [entry], [conv], [state]
    for part, (outer, inner) in enumerate(zip(EDGES[:-1], EDGES[1:])):
        before = lax.ppermute(packed[2 * part], "sky", up)
        after = lax.ppermute(packed[2 * part + 1], "sky", down)
        slots = -(-2 * (outer - inner) // SUB) * SUB
        field, entry, conv, state = pl.pallas_call(
            functools.partial(later_kernel, sizes, part),
            out_shape=[field_shape, *group_shapes(part + 1)],
            in_specs=[smem] * 4 + [vmem] * 3,
            out_specs=[vmem] * 4,
            scratch_shapes=[held(slots * blocks, LANES), held(3, slots * blocks, LANES)],
            input_output_aliases={4: 0},
            compiler_params=params,
            name="border",
        )(*scalars, pltpu.with_memory_space_constraint(field, pltpu.VMEM), before, after)
        entries.append(entry)
        convs.append(conv)
        states.append(state)

    for turn in range(1, depth_count):
        last = turn == depth_count - 1
        for part in range(len(groups)):
            incoming = lax.ppermute(states[part], "depth", ahead)
            conv, *state = pl.pallas_call(
                functools.partial(resume_kernel, sizes, part, turn),
                out_shape=group_shapes(part)[1:2] + ([] if last else group_shapes(part)[2:3]),
                in_specs=[smem] * 2 + [vmem] * 3,
                out_specs=[vmem] * (1 if last else 2),
                input_output_aliases={4: 0},
                compiler_params=params,
                name="resume",
            )(plane_slot, ratio_near, pltpu.with_memory_space_constraint(entries[part], pltpu.VMEM), incoming,
              pltpu.with_memory_space_constraint(convs[part], pltpu.VMEM))
            convs[part] = conv
            if state:
                states[part] = state[0]

    out = pl.pallas_call(
        functools.partial(gather_kernel, sizes),
        grid=(planes,),
        out_shape=moved(planes, rows * blocks, LANES),
        in_specs=[vmem] * len(groups),
        out_specs=pl.BlockSpec((1, rows * blocks, LANES), lambda k: (k, 0, 0)),
        compiler_params=params,
        name="gather",
    )(*[pltpu.with_memory_space_constraint(conv, pltpu.VMEM) for conv in convs])
    out = out.reshape(planes, rows // SUB, blocks, SUB, LANES).transpose(0, 1, 3, 2, 4)
    return out.reshape(planes, rows, cols)


def solution(mesh):
    return jax.shard_map(
        per_device,
        mesh=mesh,
        in_specs=(P("depth", "sky", None), P("depth"), P("depth"), P(), P()),
        out_specs=P("depth", "sky", None),
        check_vma=False,
    )
```

time: 438 us -> 101 us (0.23); the launches traced: 434 us -> 101 us
  other arithmetic: 186 us -> 0 us
  loops' own time: 109 us -> 0 us
  local copies, waits for them, and re-layouts: 68.2 us -> 4.51 us
  Pallas kernels: 0 us -> 45.9 us
  waiting for transfers between devices: 63 us -> 35.8 us
  starting transfers between devices: 7.1 us -> 15 us
    mul x60 -> x0, other arithmetic: 111 us -> none  [the longest x36 56.2 us: advance(): row_first = entry_xx * upper[0] + entry_xy * upper[1] + retained * lower[0]]
    another operation x3 -> x0, loops' own time: 109 us -> none  [the longest x1 78.1 us: per_device(): curvatures = lax.map(curvature, (extended, widths))]
    pallas_call x0 -> x7, Pallas kernels: none -> 45.9 us  [the longest x1 19.5 us: per_device(): pl.pallas_call(functools.partial(first_kernel, sizes), out_shape=[field_s...]
    div x24 -> x0, other arithmetic: 37.6 us -> none  [box_filter(): return summed / (2.0 * half_width.astype(jnp.float32) + 1.0)]
    dynamic_slice x60 -> x0, local copies, waits for them, and re-layouts: 36.5 us -> none  [the longest x48 29.5 us: propagate(): lax.scan(plane, carried, (curvatures[0], curvatures[1], curvatures[2], ne...]
    ppermute x3 -> x7, waiting for transfers between devices: 63 us -> 35.8 us  [the longest x3 24.4 us: per_device(): incoming = lax.ppermute(states[part], 'depth', ahead)]
    dynamic_update_slice x24 -> x0, other arithmetic: 25.9 us -> none  [per_device(): curvatures = lax.map(curvature, (extended, widths))]
    squeeze x12 -> x0, local copies, waits for them, and re-layouts: 12.7 us -> none  [per_device(): curvatures = lax.map(curvature, (extended, widths))]
  transfers between devices with their start and end apart: 3 -> 7, of which waited for: 2 -> 2; matrix products, arithmetic and copies ran while one was open for 1% -> 0% of each run, Pallas kernels for 0% -> 20%
where the time goes in v1:
time: 101 us
  Pallas kernels  45.9 us (45%)
  waiting for transfers between devices  35.8 us (35%)
  starting transfers between devices  15 us (15%)
  local copies, waits for them, and re-layouts  4.51 us (4%)
    ppermute x3, waiting for transfers between devices, per_device(): incoming = lax.ppermute(states[part], 'depth', ahead)  24.4 us
    pallas_call x1, Pallas kernels, per_device(): pl.pallas_call(functools.partial(first_kernel, sizes), out_shape=[field_s...  19.5 us
    pallas_call x2, Pallas kernels, per_device(): pl.pallas_call(functools.partial(later_kernel, sizes, part), out_shape=[f...  17.7 us
    ppermute x2, waiting for transfers between devices, per_device(): before = lax.ppermute(packed[2 * part], 'sky', up)  11.4 us
    ppermute x2, starting transfers between devices, per_device(): after = lax.ppermute(packed[2 * part + 1], 'sky', down)  7.28 us
    pallas_call x1, Pallas kernels, per_device(): pl.pallas_call(functools.partial(gather_kernel, sizes), grid=(planes,), o...  4.58 us
    unnamed x12, local copies, waits for them, and re-layouts  4.51 us
    pallas_call x3, Pallas kernels, per_device(): pl.pallas_call(functools.partial(resume_kernel, sizes, part, turn), out_s...  4.11 us
  transfers between devices with their start and end apart: 7, of which 2 were waited for; matrix products, arithmetic and copies ran while one was open for 0% of the time, Pallas kernels for 20%

profile of v1, /device:TPU:6, one launch (start us, length us, event | category | flops | bytes accessed | tf_op | source)
XLA Modules:
  0.0 101.4 jit_solution(4012697831298386828)
XLA Ops:
  0.0 0.0 copy-start
  0.0 1.9 %copy-done = f32[12,32,2048]{2,1,0:T(8,128)S(1)} copy-done((f32[12,32,2048]{2,1,0:T(8,128)S(1)}, f32[12,32,2048]{2,1,0:T(8,128)}, u32[]{:S(2)}) %copy-start) | copy-done | bytes 3145752
  1.9 0.0 copy-start.1
  1.9 0.7 copy-done.1
  2.5 0.0 copy-start.3
  2.5 0.7 copy-done.3
  3.2 0.0 copy-start.4
  3.2 0.7 copy-done.4
  3.9 0.0 copy-start.5
  3.9 0.7 copy-done.5
  4.5 19.5 %interior.1 = (f32[12,3,800,128]{3,2,1,0:T(8,128)S(1)}, f32[12,3,224,128]{3,2,1,0:T(8,128)S(1)}, f32[12,224,128]{2,1,0:T(8,128)S(1)}, f32[8,224,128]{2,1,0:T(8,1...) custom-call(s32[12]{0:T(128)S(1)} %copy-done.4, ...), custom_call_target="tpu_custom_call" | custom-call | tf_op jit(solution)/shard_map/interior/pallas_call | solution.py:333
  24.0 1.9 %collective-permute-start.4 = (f32[12,80,128]{2,1,0:T(8,128)S(1)}, f32[12,80,128]{2,1,0:T(8,128)S(1)}, u32[]{:S(2)}, u32[]{:S(2)}) collective-permute-start(f32[12,80,128]{2,1,0:T(8,128)S(1)} %get-tuple-element.30), channel_id=1, source_target_pairs={{0,1},{1,2},{2,3},{3,4},{4,5},{5,6},{6,7},{7,8},{8,9},{9,10},{10,1... | collective-permute-start | bytes 1474568 | tf_op jit(solution)/shard_map/ppermute | solution.py:344
  26.0 3.6 %collective-permute-start.5 = (f32[12,80,128]{2,1,0:T(8,128)S(1)}, f32[12,80,128]{2,1,0:T(8,128)S(1)}, u32[]{:S(2)}, u32[]{:S(2)}) collective-permute-start(f32[12,80,128]{2,1,0:T(8,128)S(1)} %get-tuple-element.31), channel_id=1, source_target_pairs={{1,0},{2,1},{3,2},{4,3},{5,4},{6,5},{7,6},{8,7},{9,8},{10,9},{11,1... | collective-permute-start | bytes 1474568 | tf_op jit(solution)/shard_map/ppermute | solution.py:345
  29.6 1.9 %collective-permute-start.1 = (f32[12,64,128]{2,1,0:T(8,128)S(1)}, f32[12,64,128]{2,1,0:T(8,128)S(1)}, u32[]{:S(2)}, u32[]{:S(2)}) collective-permute-start(f32[12,64,128]{2,1,0:T(8,128)S(1)} %get-tuple-element.24), channel_id=1, source_target_pairs={{0,1},{1,2},{2,3},{3,4},{4,5},{5,6},{6,7},{7,8},{8,9},{9,10},{10,1... | collective-permute-start | bytes 1179656 | tf_op jit(solution)/shard_map/ppermute | solution.py:344
  31.5 3.6 %collective-permute-start.2 = (f32[12,64,128]{2,1,0:T(8,128)S(1)}, f32[12,64,128]{2,1,0:T(8,128)S(1)}, u32[]{:S(2)}, u32[]{:S(2)}) collective-permute-start(f32[12,64,128]{2,1,0:T(8,128)S(1)} %get-tuple-element.25), channel_id=1, source_target_pairs={{1,0},{2,1},{3,2},{4,3},{5,4},{6,5},{7,6},{8,7},{9,8},{10,9},{11,1... | collective-permute-start | bytes 1179656 | tf_op jit(solution)/shard_map/ppermute | solution.py:345
  35.2 1.3 %collective-permute-start = (f32[8,224,128]{2,1,0:T(8,128)S(1)}, f32[8,224,128]{2,1,0:T(8,128)S(1)}, u32[]{:S(2)}, u32[]{:S(2)}) collective-permute-start(f32[8,224,128]{2,1,0:T(8,128)S(1)} %get-tuple-element.21), channel_id=1, source_target_pairs={{0,16},{1,17},{2,18},{3,19},{4,20},{5,21},{6,22},{7,23},{8,24},{9,... | collective-permute-start | bytes 2752520 | tf_op jit(solution)/shard_map/ppermute | solution.py:364
  36.5 11.4 %collective-permute-done.1.before = f32[12,64,128]{2,1,0:T(8,128)S(1)} collective-permute-done((f32[12,64,128]{2,1,0:T(8,128)S(1)}, f32[12,64,128]{2,1,0:T(8,128)S(1)}, u32[]{:S(2)}, u32[]{:S(2)}) %collective-permute-start.1) | collective-permute-done | bytes 393248 | tf_op jit(solution)/shard_map/ppermute | solution.py:344
  47.9 0.0 collective-permute-done.2.after
  47.9 7.4 %border.2 = (f32[12,3,800,128]{3,2,1,0:T(8,128)S(1)}, f32[12,3,128,128]{3,2,1,0:T(8,128)S(1)}, f32[12,128,128]{2,1,0:T(8,128)S(1)}, f32[8,128,128]{2,1,0:T(8,128)S(1)}) custom-call(s32[12]{0:T(128)S(1)} %copy-done.4, s32[12]{0:T(128)S(1)} %copy-done.1, f32[16]{0:T(128)S(1)} %copy-done.3, f32[16]{0:T(128)S(1)} %copy-done.5, ...), custom_call_target="tpu_custom_call", output_to_operand_aliasing={{0}: (4, {})} | custom-call | tf_op jit(solution)/shard_map/border/pallas_call | solution.py:347
  55.3 0.0 collective-permute-done.4.before
  55.3 0.0 collective-permute-done.5.after
  55.3 0.0 copy-start.2
  55.4 10.3 %border.3 = (f32[12,3,800,128]{3,2,1,0:T(8,128)S(1)}, f32[12,3,160,128]{3,2,1,0:T(8,128)S(1)}, f32[12,160,128]{2,1,0:T(8,128)S(1)}, f32[8,160,128]{2,1,0:T(8,128)S(1)}) custom-call(s32[12]{0:T(128)S(1)} %copy-done.4, s32[12]{0:T(128)S(1)} %copy-done.1, f32[16]{0:T(128)S(1)} %copy-done.3, f32[16]{0:T(128)S(1)} %copy-done.5, ...), custom_call_target="tpu_custom_call", output_to_operand_aliasing={{0}: (4, {})} | custom-call | tf_op jit(solution)/shard_map/border/pallas_call | solution.py:347
  65.6 1.3 %collective-permute-start.6 = (f32[8,160,128]{2,1,0:T(8,128)S(1)}, f32[8,160,128]{2,1,0:T(8,128)S(1)}, u32[]{:S(2)}, u32[]{:S(2)}) collective-permute-start(f32[8,160,128]{2,1,0:T(8,128)S(1)} %get-tuple-element.33), channel_id=1, source_target_pairs={{0,16},{1,17},{2,18},{3,19},{4,20},{5,21},{6,22},{7,23},{8,24},{9,... | collective-permute-start | bytes 1966088 | tf_op jit(solution)/shard_map/ppermute | solution.py:364
  66.9 1.3 %collective-permute-start.3 = (f32[8,128,128]{2,1,0:T(8,128)S(1)}, f32[8,128,128]{2,1,0:T(8,128)S(1)}, u32[]{:S(2)}, u32[]{:S(2)}) collective-permute-start(f32[8,128,128]{2,1,0:T(8,128)S(1)} %get-tuple-element.27), channel_id=1, source_target_pairs={{0,16},{1,17},{2,18},{3,19},{4,20},{5,21},{6,22},{7,23},{8,24},{9,... | collective-permute-start | bytes 1572872 | tf_op jit(solution)/shard_map/ppermute | solution.py:364
  68.2 0.0 collective-permute-done.incoming
  68.2 0.0 copy-done.2
  68.3 1.6 %resume.3.refs_0_ = f32[12,224,128]{2,1,0:T(8,128)S(1)} custom-call(s32[12]{0:T(128)S(1)} %copy-done.2, f32[16]{0:T(128)S(1)} %copy-done.3, f32[12,3,224,128]{3,2,1,0:T(8,128)S(1)} %get-tuple-element.20.entry_ref, f32[8,224,128]{2,1,0:T(8,128)S(1)} %collective-permute-done.incoming, ...), custom_call_target="tpu_custom_call", output_to_operand_aliasing={{}: (4, {})} | custom-call | tf_op jit(solution)/shard_map/resume/pallas_call | solution.py:365
  69.9 24.4 %collective-permute-done.3.incoming = f32[8,128,128]{2,1,0:T(8,128)S(1)} collective-permute-done((f32[8,128,128]{2,1,0:T(8,128)S(1)}, f32[8,128,128]{2,1,0:T(8,128)S(1)}, u32[]{:S(2)}, u32[]{:S(2)}) %collective-permute-start.3) | collective-permute-done | bytes 524320 | tf_op jit(solution)/shard_map/ppermute | solution.py:364
  94.3 1.2 %resume.4.refs_1_ = f32[12,128,128]{2,1,0:T(8,128)S(1)} custom-call(s32[12]{0:T(128)S(1)} %copy-done.2, f32[16]{0:T(128)S(1)} %copy-done.3, f32[12,3,128,128]{3,2,1,0:T(8,128)S(1)} %get-tuple-element.26.entry_ref, f32[8,128,128]{2,1,0:T(8,128)S(1)} %collective-permute-done.3.incoming, ...), custom_call_target="tpu_custom_call", output_to_operand_aliasing={{}: (4, {})} | custom-call | tf_op jit(solution)/shard_map/resume/pallas_call | solution.py:365
  95.5 0.0 collective-permute-done.6.incoming
  95.5 1.3 %resume.5.refs_2_ = f32[12,160,128]{2,1,0:T(8,128)S(1)} custom-call(s32[12]{0:T(128)S(1)} %copy-done.2, f32[16]{0:T(128)S(1)} %copy-done.3, f32[12,3,160,128]{3,2,1,0:T(8,128)S(1)} %get-tuple-element.32.entry_ref, f32[8,160,128]{2,1,0:T(8,128)S(1)} %collective-permute-done.6.incoming, ...), custom_call_target="tpu_custom_call", output_to_operand_aliasing={{}: (4, {})} | custom-call | tf_op jit(solution)/shard_map/resume/pallas_call | solution.py:365
  96.8 4.6 %gather.1 = f32[12,512,128]{2,1,0:T(8,128)} custom-call(f32[12,224,128]{2,1,0:T(8,128)S(1)} %resume.3.refs_0_, f32[12,128,128]{2,1,0:T(8,128)S(1)} %resume.4.refs_1_, f32[12,160,128]{2,1,0:T(8,128)S(1)} %resume.5.refs_2_), custom_call_target="tpu_custom_call" | custom-call | tf_op jit(solution)/shard_map/gather/pallas_call | solution.py:379
Async XLA Ops:
  0.0 1.9 %copy-start = (f32[12,32,2048]{2,1,0:T(8,128)S(1)}, f32[12,32,2048]{2,1,0:T(8,128)}, u32[]{:S(2)}) copy-start(f32[12,32,2048]{2,1,0:T(8,128)} %param.5) | copy-start | bytes 9437188
  1.9 0.7 copy-start.1
  2.5 0.7 copy-start.3
  3.2 0.7 copy-start.4
  3.9 0.7 copy-start.5
  24.0 31.3 %collective-permute-start.4 = (f32[12,80,128]{2,1,0:T(8,128)S(1)}, f32[12,80,128]{2,1,0:T(8,128)S(1)}, u32[]{:S(2)}, u32[]{:S(2)}) collective-permute-start(f32[12,80,128]{2,1,0:T(8,128)S(1)} %get-tuple-element.30), channel_id=1, source_target_pairs={{0,1},{1,2},{2,3},{3,4},{4,5},{5,6},{6,7},{7,8},{8,9},{9,10},{10,1... | collective-permute-start | bytes 1474568 | tf_op jit(solution)/shard_map/ppermute | solution.py:344
  26.0 29.4 %collective-permute-start.5 = (f32[12,80,128]{2,1,0:T(8,128)S(1)}, f32[12,80,128]{2,1,0:T(8,128)S(1)}, u32[]{:S(2)}, u32[]{:S(2)}) collective-permute-start(f32[12,80,128]{2,1,0:T(8,128)S(1)} %get-tuple-element.31), channel_id=1, source_target_pairs={{1,0},{2,1},{3,2},{4,3},{5,4},{6,5},{7,6},{8,7},{9,8},{10,9},{11,1... | collective-permute-start | bytes 1474568 | tf_op jit(solution)/shard_map/ppermute | solution.py:345
  29.6 18.3 %collective-permute-start.1 = (f32[12,64,128]{2,1,0:T(8,128)S(1)}, f32[12,64,128]{2,1,0:T(8,128)S(1)}, u32[]{:S(2)}, u32[]{:S(2)}) collective-permute-start(f32[12,64,128]{2,1,0:T(8,128)S(1)} %get-tuple-element.24), channel_id=1, source_target_pairs={{0,1},{1,2},{2,3},{3,4},{4,5},{5,6},{6,7},{7,8},{8,9},{9,10},{10,1... | collective-permute-start | bytes 1179656 | tf_op jit(solution)/shard_map/ppermute | solution.py:344
  31.5 16.3 %collective-permute-start.2 = (f32[12,64,128]{2,1,0:T(8,128)S(1)}, f32[12,64,128]{2,1,0:T(8,128)S(1)}, u32[]{:S(2)}, u32[]{:S(2)}) collective-permute-start(f32[12,64,128]{2,1,0:T(8,128)S(1)} %get-tuple-element.25), channel_id=1, source_target_pairs={{1,0},{2,1},{3,2},{4,3},{5,4},{6,5},{7,6},{8,7},{9,8},{10,9},{11,1... | collective-permute-start | bytes 1179656 | tf_op jit(solution)/shard_map/ppermute | solution.py:345
  35.2 33.1 %collective-permute-start = (f32[8,224,128]{2,1,0:T(8,128)S(1)}, f32[8,224,128]{2,1,0:T(8,128)S(1)}, u32[]{:S(2)}, u32[]{:S(2)}) collective-permute-start(f32[8,224,128]{2,1,0:T(8,128)S(1)} %get-tuple-element.21), channel_id=1, source_target_pairs={{0,16},{1,17},{2,18},{3,19},{4,20},{5,21},{6,22},{7,23},{8,24},{9,... | collective-permute-start | bytes 2752520 | tf_op jit(solution)/shard_map/ppermute | solution.py:364
  55.3 12.9 %copy-start.2 = (s32[12]{0:T(128)S(1)}, s32[12]{0:T(128)}, u32[]{:S(2)}) copy-start(s32[12]{0:T(128)} %slots.11) | copy-start | bytes 148
  65.6 29.8 %collective-permute-start.6 = (f32[8,160,128]{2,1,0:T(8,128)S(1)}, f32[8,160,128]{2,1,0:T(8,128)S(1)}, u32[]{:S(2)}, u32[]{:S(2)}) collective-permute-start(f32[8,160,128]{2,1,0:T(8,128)S(1)} %get-tuple-element.33), channel_id=1, source_target_pairs={{0,16},{1,17},{2,18},{3,19},{4,20},{5,21},{6,22},{7,23},{8,24},{9,... | collective-permute-start | bytes 1966088 | tf_op jit(solution)/shard_map/ppermute | solution.py:364
  66.9 27.4 %collective-permute-start.3 = (f32[8,128,128]{2,1,0:T(8,128)S(1)}, f32[8,128,128]{2,1,0:T(8,128)S(1)}, u32[]{:S(2)}, u32[]{:S(2)}) collective-permute-start(f32[8,128,128]{2,1,0:T(8,128)S(1)} %get-tuple-element.27), channel_id=1, source_target_pairs={{0,16},{1,17},{2,18},{3,19},{4,20},{5,21},{6,22},{7,23},{8,24},{9,... | collective-permute-start | bytes 1572872 | tf_op jit(solution)/shard_map/ppermute | solution.py:364

commit v2 on v1

v2 whole, which is shorter than its diff:
```python
import functools

import jax
import jax.numpy as jnp
from jax import lax
from jax.experimental import pallas as pl
from jax.experimental.pallas import tpu as pltpu
from jax.sharding import PartitionSpec as P

WMAX = 8
RIM = WMAX + 1
LANES = 128
SUB = 8
EDGES = (RIM, 4, 0)
VMEM_LIMIT = 16 * 1024 * 1024
PACK = 16
INNER = 2
F32, BF16 = jnp.float32, jnp.bfloat16


def row_groups(row_count):
    middle = row_count // 2 + 2
    groups = [((RIM, middle),), ((middle, row_count - RIM),)]
    for outer, inner in zip(EDGES[:-1], EDGES[1:]):
        groups.append(((inner, outer), (row_count - outer, row_count - inner)))
    return groups


def rows_in(group):
    return sum(stop - start for start, stop in group)


def split(value):
    high = value.astype(BF16)
    rest = value - high.astype(F32)
    middle = rest.astype(BF16)
    return high, middle, (rest - middle.astype(F32)).astype(BF16)


def band(half_width, band_ref):
    source = lax.broadcasted_iota(jnp.int32, (2 * LANES, LANES), 0)
    target = lax.broadcasted_iota(jnp.int32, (2 * LANES, LANES), 1)
    offset = jnp.where(source >= LANES + LANES // 2, source - 2 * LANES, source) - target
    distance = jnp.abs(offset)
    rim = (distance == half_width + 1).astype(F32)
    edge = (distance == half_width).astype(F32)
    inside = (distance <= half_width).astype(F32)
    both = rim + edge
    fields = (inside, rim - edge, jnp.where(offset > 0, both, -both))
    for field, value in enumerate(fields):
        value = value.astype(BF16)
        for part in range(3):
            band_ref[part * 2 * LANES:(part + 1) * 2 * LANES, field * LANES:(field + 1) * LANES] = value


def clear_ends(blocks, height, left_ref):
    zero = jnp.zeros((height, LANES // 2), BF16)
    for part in range(3):
        at = part * 2 * LANES + LANES
        left_ref[(blocks - 1) * height:blocks * height, at:at + LANES // 2] = zero
        left_ref[0:height, at + LANES // 2:at + LANES] = zero


def column_stage(half_width, blocks, height, load, left_ref, band_ref):
    half = LANES // 2
    band(half_width, band_ref)
    for block in range(blocks):
        here = slice(block * height, (block + 1) * height)
        for part, value in enumerate(split(load(block))):
            at = part * 2 * LANES
            left_ref[here, at:at + LANES] = value
            if block > 0:
                left_ref[(block - 1) * height:block * height, at + LANES:at + LANES + half] = value[:, :half]
            if block < blocks - 1:
                left_ref[(block + 1) * height:(block + 2) * height, at + LANES + half:at + 2 * LANES] = value[:, half:]
    return jnp.dot(left_ref[...], band_ref[...], preferred_element_type=F32)


def own_columns(k, half_width, rows, blocks, x_ref, field_ref, left_ref, band_ref):
    tiles = rows // SUB

    def load(block):
        return jnp.concatenate(
            [x_ref[k, pl.ds((tile * blocks + block) * SUB, SUB), :] for tile in range(tiles)], axis=0)

    result = column_stage(half_width, blocks, rows, load, left_ref, band_ref)
    for block in range(blocks):
        for tile in range(tiles):
            from_row = block * rows + tile * SUB
            start = (tile * SUB + RIM) * blocks + block
            for field in range(3):
                field_ref[k, field, pl.ds(start, SUB, stride=blocks), :] = result[
                    from_row:from_row + SUB, field * LANES:(field + 1) * LANES]


def halo_height(count):
    return -(-2 * count // PACK) * PACK


def halo_columns(k, half_width, blocks, sides, tile_ref, stage_ref, field_ref, left_ref, band_ref):
    places = []
    height = halo_height(sides[0][2])
    for ref, first, count in sides:
        for i in range(count):
            slot = len(places)
            places.append(first + i)
            for half in range(blocks // SUB):
                tile_ref[pl.ds(half * SUB * height + slot, SUB, stride=height), :] = ref[
                    k, pl.ds(i * blocks + half * SUB, SUB), :]

    def load(block):
        return tile_ref[pl.ds(block * height, height), :]

    result = column_stage(half_width, blocks, height, load, left_ref, band_ref)
    for block in range(blocks):
        for first in range(0, len(places), SUB):
            from_row = block * height + first
            for field in range(3):
                stage_ref[field, pl.ds(first * blocks + block, SUB, stride=blocks), :] = result[
                    from_row:from_row + SUB, field * LANES:(field + 1) * LANES]
    for slot, row in enumerate(places):
        for field in range(3):
            field_ref[k, field, pl.ds((row + RIM) * blocks, blocks), :] = stage_ref[
                field, pl.ds(slot * blocks, blocks), :]


def row_stage(k, half_width, near, scale, group, blocks, field_ref, entry_ref):
    def row(field, index):
        return field_ref[k, field, pl.ds(pl.multiple_of(index * blocks, blocks), blocks), :]

    place = 0
    for start, stop in group:
        first = start + RIM
        along = row(1, first)
        for step in range(1, WMAX + 1):
            pair = row(1, first - step) + row(1, first + step)
            along = along + jnp.where(step <= half_width, pair, 0.0)
        for at in range(first, stop + RIM):
            high, low = at + half_width, at - half_width
            across = (row(0, high + 1) - row(0, high)) - (row(0, low) - row(0, low - 1))
            mixed = (row(2, high + 1) + row(2, high)) - (row(2, low) + row(2, low - 1))
            where = pl.ds(place * blocks, blocks)
            entry_ref[k, 0, where, :] = near - scale * along
            entry_ref[k, 1, where, :] = near - scale * across
            entry_ref[k, 2, where, :] = (-0.25 * scale) * mixed
            if at + 1 < stop + RIM:
                along = along + (row(1, high + 1) - row(1, low))
            place += 1


def sweep(planes, length, near_of, entry_ref, conv_ref, start, finish):
    step = next(count * SUB for count in (4, 3, 2, 1) if length % (count * SUB) == 0)

    def part(index, carry):
        where = pl.ds(pl.multiple_of(index * step, step), step)
        state = start(where, (step, LANES))
        now, then = state[:4], state[4:]
        for k in range(planes):
            xx, yy, xy = [entry_ref[k, i, where, :] for i in range(3)]
            kept = 1.0 - near_of(k)
            new = [
                xx * now[0] + xy * now[2] + kept * then[0],
                xx * now[1] + xy * now[3] + kept * then[1],
                xy * now[0] + yy * now[2] + kept * then[2],
                xy * now[1] + yy * now[3] + kept * then[3],
            ]
            now, then = new, now
            conv_ref[k, where, :] = 1.0 - 0.5 * (new[0] + new[3])
        finish(where, now + then)
        return carry

    lax.fori_loop(0, length // step, part, 0)


def identity_state(where, shape):
    one, zero = jnp.ones(shape, F32), jnp.zeros(shape, F32)
    return [one, zero, zero, one] * 2


def writer(state_ref):
    def finish(where, state):
        for i, value in enumerate(state):
            state_ref[i, where, :] = value

    return finish


def scalars_of(k, widths, slots, near, lens):
    half_width = widths[k]
    count = (2 * half_width + 1).astype(F32)
    return half_width, near[slots[k]], lens[slots[k]] / (count * count)


def first_kernel(sizes, widths_hbm, slots_hbm, near_hbm, lens_hbm, x_hbm, field_ref, *rest):
    planes, rows, blocks, groups = sizes
    parts, rest = [rest[3 * part:3 * part + 3] for part in range(INNER)], rest[3 * INNER:]
    sends, (x_ref, widths, slots, near, lens, left_ref, band_ref, plane_sems, table_sems) = rest[:-9], rest[-9:]
    tables = ((widths_hbm, widths), (slots_hbm, slots), (near_hbm, near), (lens_hbm, lens))
    copies = [pltpu.make_async_copy(*pair, table_sems.at[i]) for i, pair in enumerate(tables)]
    for copy in copies:
        copy.start()

    def plane_copy(k):
        return pltpu.make_async_copy(x_hbm.at[k], x_ref.at[k], plane_sems.at[k])

    for k in range(planes):
        plane_copy(k).start()
    clear_ends(blocks, rows, left_ref)
    for copy in copies:
        copy.wait()

    def plane(k, carry):
        plane_copy(k).wait()
        half_width, near_k, scale = scalars_of(k, widths, slots, near, lens)
        own_columns(k, half_width, rows, blocks, x_ref, field_ref, left_ref, band_ref)
        for group, (entry_ref, _, _) in zip(groups, parts):
            row_stage(k, half_width, near_k, scale, group, blocks, field_ref, entry_ref)
        for part, (outer, inner) in enumerate(zip(EDGES[:-1], EDGES[1:])):
            begin, count = RIM - outer, outer - inner
            for ref, first in ((sends[2 * part], rows - begin - count), (sends[2 * part + 1], begin)):
                for i in range(count):
                    row = first + i
                    for half in range(blocks // SUB):
                        start = (row // SUB) * SUB * blocks + half * SUB * SUB + row % SUB
                        ref[k, pl.ds(i * blocks + half * SUB, SUB), :] = x_ref[k, pl.ds(start, SUB, stride=SUB), :]
        return carry

    lax.fori_loop(0, planes, plane, 0)

    @pl.when(lax.axis_index("depth") == 0)
    def _():
        for group, (entry_ref, conv_ref, state_ref) in zip(groups, parts):
            sweep(planes, rows_in(group) * blocks, lambda k: near[slots[k]], entry_ref, conv_ref, identity_state,
                  writer(state_ref))


def later_kernel(sizes, part, widths, slots, near, lens, field_in, before, after, behind, field_ref, entry_ref, conv_ref,
                 state_ref, tile_ref, stage_ref, left_ref, band_ref):
    planes, rows, blocks, groups = sizes
    group = groups[INNER + part]
    outer, inner = EDGES[part], EDGES[part + 1]
    begin, count = RIM - outer, outer - inner
    height = halo_height(count)
    clear_ends(blocks, height, left_ref)
    tile_ref[...] = jnp.zeros(tile_ref.shape, F32)

    def plane(k, carry):
        half_width, near_k, scale = scalars_of(k, widths, slots, near, lens)
        sides = ((before, -begin - count, count), (after, rows + begin, count))
        halo_columns(k, half_width, blocks, sides, tile_ref, stage_ref, field_ref, left_ref, band_ref)
        row_stage(k, half_width, near_k, scale, group, blocks, field_ref, entry_ref)
        return carry

    lax.fori_loop(0, planes, plane, 0)

    @pl.when(lax.axis_index("depth") == 0)
    def _():
        sweep(planes, rows_in(group) * blocks, lambda k: near[slots[k]], entry_ref, conv_ref, identity_state,
              writer(state_ref))


def resume(sizes, part, turn, slots, near, entry_ref, incoming, conv_ref, finish):
    planes, rows, blocks, groups = sizes

    @pl.when(lax.axis_index("depth") == turn)
    def _():
        sweep(planes, rows_in(groups[part]) * blocks, lambda k: near[slots[k]], entry_ref, conv_ref,
              lambda where, shape: [incoming[i, where, :] for i in range(8)], finish)


def resume_kernel(sizes, part, turn, slots, near, entry_ref, incoming, conv_in, conv_ref, *state_ref):
    finish = writer(state_ref[0]) if state_ref else lambda where, state: None
    resume(sizes, part, turn, slots, near, entry_ref, incoming, conv_ref, finish)


def last_kernel(sizes, turn, slots, near, entry_ref, incoming, conv_in, *refs):
    planes, rows, blocks, groups = sizes
    others, (conv_ref, out_hbm, tiles_ref, sems) = refs[:-4], refs[-4:]
    part = len(groups) - 1
    resume(sizes, part, turn, slots, near, entry_ref, incoming, conv_ref, lambda where, state: None)

    def plane_copy(k):
        return pltpu.make_async_copy(tiles_ref.at[k], out_hbm.at[k], sems.at[k])

    def plane(k, carry):
        for group, ref in zip(groups, (*others, conv_ref)):
            place = 0
            for start, stop in group:
                for row in range(start, stop):
                    for half in range(blocks // SUB):
                        to = (row // SUB) * SUB * blocks + half * SUB * SUB + row % SUB
                        tiles_ref[k, pl.ds(to, SUB, stride=SUB), :] = ref[k, pl.ds(place * blocks + half * SUB, SUB), :]
                    place += 1
        plane_copy(k).start()
        return carry

    lax.fori_loop(0, planes, plane, 0)
    for k in range(planes):
        plane_copy(k).wait()


def per_device(potential, widths, plane_slot, ratio_near, ratio_lens):
    planes, rows, cols = potential.shape
    blocks = cols // LANES
    groups = row_groups(rows)
    sizes = (planes, rows, blocks, groups)
    depth_count, sky_count = lax.axis_size("depth"), lax.axis_size("sky")
    up = [(i, i + 1) for i in range(sky_count - 1)]
    down = [(j, i) for i, j in up]
    ahead = [(i, i + 1) for i in range(depth_count - 1)]
    tiled = potential.reshape(planes, rows // SUB, SUB, blocks, LANES).transpose(0, 1, 3, 2, 4)
    tiled = tiled.reshape(planes, rows * blocks, LANES)
    smem = pl.BlockSpec(memory_space=pltpu.SMEM)
    vmem = pl.BlockSpec(memory_space=pltpu.VMEM)
    anywhere = pl.BlockSpec(memory_space=pl.ANY)
    params = pltpu.CompilerParams(vmem_limit_bytes=VMEM_LIMIT)
    scalars = (widths, plane_slot, ratio_near, ratio_lens)
    dma = pltpu.SemaphoreType.DMA
    cost = pl.CostEstimate(flops=1, transcendentals=0, bytes_accessed=1)

    def held(*shape, dtype=F32):
        return pltpu.VMEM(shape, dtype)

    def moved(*shape):
        return jax.ShapeDtypeStruct(shape, F32)

    def in_vmem(array):
        return pltpu.with_memory_space_constraint(array, pltpu.VMEM)

    def in_hbm(array):
        return pltpu.with_memory_space_constraint(array, pltpu.HBM)

    field_shape = held(planes, 3, (rows + 2 * RIM) * blocks, LANES)

    def group_shapes(part):
        length = rows_in(groups[part]) * blocks
        return [held(planes, 3, length, LANES), held(planes, length, LANES), moved(8, length, LANES)]

    def matrix_scratch(height):
        return [held(blocks * height, 6 * LANES, dtype=BF16), held(6 * LANES, 3 * LANES, dtype=BF16)]

    sends = []
    for outer, inner in zip(EDGES[:-1], EDGES[1:]):
        sends += [held(planes, (outer - inner) * blocks, LANES)] * 2
    field, *made = pl.pallas_call(
        functools.partial(first_kernel, sizes),
        out_shape=[field_shape, *sum((group_shapes(part) for part in range(INNER)), []), *sends],
        in_specs=[anywhere] * 5,
        out_specs=[vmem] * (1 + 3 * INNER + len(sends)),
        scratch_shapes=[
            held(planes, rows * blocks, LANES), *[pltpu.SMEM(array.shape, array.dtype) for array in scalars],
            *matrix_scratch(rows), dma((planes,)), dma((len(scalars),))],
        compiler_params=params,
        cost_estimate=cost,
        name="interior",
    )(*[in_hbm(array) for array in (*scalars, tiled)])
    entries, convs, states = [made[i:3 * INNER:3] for i in range(3)]
    packed = made[3 * INNER:]
    arriving = [lax.ppermute(state, "depth", ahead) for state in states]
    for part, (outer, inner) in enumerate(zip(EDGES[:-1], EDGES[1:])):
        before = lax.ppermute(packed[2 * part], "sky", up)
        after = lax.ppermute(packed[2 * part + 1], "sky", down)
        height = halo_height(outer - inner)
        field, entry, conv, state = pl.pallas_call(
            functools.partial(later_kernel, sizes, part),
            out_shape=[field_shape, *group_shapes(INNER + part)],
            in_specs=[smem] * 4 + [vmem] * 3 + [anywhere],
            out_specs=[vmem] * 4,
            scratch_shapes=[held(height * blocks, LANES), held(3, height * blocks, LANES), *matrix_scratch(height)],
            input_output_aliases={4: 0},
            compiler_params=params,
            cost_estimate=cost,
            name="border",
        )(*scalars, in_vmem(field), before, after, arriving[part])
        entries.append(entry)
        convs.append(conv)
        arriving.append(lax.ppermute(state, "depth", ahead))

    for turn in range(1, depth_count):
        last = turn == depth_count - 1
        for part in range(len(groups) - last):
            convs[part], *state = pl.pallas_call(
                functools.partial(resume_kernel, sizes, part, turn),
                out_shape=group_shapes(part)[1:2] + ([] if last else group_shapes(part)[2:3]),
                in_specs=[smem] * 2 + [vmem] * 3,
                out_specs=[vmem] * (1 if last else 2),
                input_output_aliases={4: 0},
                compiler_params=params,
                cost_estimate=cost,
                name="resume",
            )(plane_slot, ratio_near, in_vmem(entries[part]), arriving[part], in_vmem(convs[part]))
            if state:
                arriving[part] = lax.ppermute(state[0], "depth", ahead)

    conv, out = pl.pallas_call(
        functools.partial(last_kernel, sizes, depth_count - 1),
        out_shape=[group_shapes(len(groups) - 1)[1], moved(planes, rows * blocks, LANES)],
        in_specs=[smem] * 2 + [vmem] * (3 + len(groups) - 1),
        out_specs=[vmem, anywhere],
        scratch_shapes=[held(planes, rows * blocks, LANES), dma((planes,))],
        input_output_aliases={4: 0},
        compiler_params=params,
        cost_estimate=cost,
        name="last",
    )(plane_slot, ratio_near, in_vmem(entries[-1]), arriving[-1], in_vmem(convs[-1]),
      *[in_vmem(conv) for conv in convs[:-1]])
    out = out.reshape(planes, rows // SUB, blocks, SUB, LANES).transpose(0, 1, 3, 2, 4)
    return out.reshape(planes, rows, cols)


def solution(mesh):
    return jax.shard_map(
        per_device,
        mesh=mesh,
        in_specs=(P("depth", "sky", None), P("depth"), P("depth"), P(), P()),
        out_specs=P("depth", "sky", None),
        check_vma=False,
    )
```

time: 101 us -> 74.8 us (0.74)
  waiting for transfers between devices: 35.8 us -> 22.7 us
  Pallas kernels: 45.9 us -> 35.1 us
  local copies, waits for them, and re-layouts: 4.51 us -> 0.02 us
  starting transfers between devices: 15 us -> 16.3 us
    ppermute x2, waiting for transfers between devices: 11.4 us -> 0.01 us  [per_device(): before = lax.ppermute(packed[2 * part], 'sky', up)]
    pallas_call x1, Pallas kernels: 19.5 us -> 13.7 us  [per_device(): pl.pallas_call(functools.partial(first_kernel, sizes), out_shape=[field_s...]
    unnamed x12 -> x8, local copies, waits for them, and re-layouts: 4.51 us -> 0.02 us
    pallas_call x2, Pallas kernels: 17.7 us -> 14.9 us  [per_device(): pl.pallas_call(functools.partial(later_kernel, sizes, part), out_shape=[f...]
    ppermute x3 -> x4, waiting for transfers between devices: 24.4 us -> 22.7 us  [the longest x2 17.1 us: per_device(): arriving.append(lax.ppermute(state, 'depth', ahead))]
    pallas_call x1, Pallas kernels: 4.58 us -> 2.95 us  [per_device(): pl.pallas_call(functools.partial(last_kernel, sizes, depth_count - 1), ou...]
    ppermute x3 -> x4, starting transfers between devices: 3.88 us -> 5.17 us  [the longest x2 2.58 us: per_device(): arriving = [lax.ppermute(state, 'depth', ahead) for state in states]]
  transfers between devices with their start and end apart: 7 -> 8, of which waited for: 2 -> 3; matrix products, arithmetic and copies ran while one was open for 0% -> 0% of each run, Pallas kernels for 20% -> 25%
where the time goes in v2:
time: 74.8 us; the launch traced here: 74.3 us
  Pallas kernels  35.1 us (47%)
  waiting for transfers between devices  22.7 us (30%)
  starting transfers between devices  16.3 us (22%)
    ppermute x2, waiting for transfers between devices, per_device(): arriving.append(lax.ppermute(state, 'depth', ahead))  17.1 us
    pallas_call x2, Pallas kernels, per_device(): pl.pallas_call(functools.partial(later_kernel, sizes, part), out_shape=[f...  14.9 us
    pallas_call x1, Pallas kernels, per_device(): pl.pallas_call(functools.partial(first_kernel, sizes), out_shape=[field_s...  13.7 us
    ppermute x2, starting transfers between devices, per_device(): after = lax.ppermute(packed[2 * part + 1], 'sky', down)  7.28 us
    ppermute x2, waiting for transfers between devices, per_device(): arriving = [lax.ppermute(state, 'depth', ahead) for state in states]  5.65 us
    ppermute x2, starting transfers between devices, per_device(): before = lax.ppermute(packed[2 * part], 'sky', up)  3.84 us
    pallas_call x3, Pallas kernels, per_device(): pl.pallas_call(functools.partial(resume_kernel, sizes, part, turn), out_s...  3.55 us
    pallas_call x1, Pallas kernels, per_device(): pl.pallas_call(functools.partial(last_kernel, sizes, depth_count - 1), ou...  2.95 us
  transfers between devices with their start and end apart: 8, of which 3 were waited for; matrix products, arithmetic and copies ran while one was open for 0% of the time, Pallas kernels for 25%

profile of v2, /device:TPU:6, one launch (start us, length us, event | category | flops | bytes accessed | tf_op | source)
XLA Modules:
  0.0 74.3 jit_solution(17397189729602679080)
XLA Ops:
  0.0 0.0 copy-start.1
  0.0 0.0 copy-start
  0.0 0.0 copy-start.3
  0.0 0.0 copy-start.2
  0.0 13.7 %interior.1 = (f32[12,3,800,128]{3,2,1,0:T(8,128)S(1)}, f32[12,3,144,128]{3,2,1,0:T(8,128)S(1)}, f32[12,144,128]{2,1,0:T(8,128)S(1)}, f32[8,144,128]{2,1,0:T(8,1...) custom-call(s32[12]{0:T(128)} %widths.3, ...), custom_call_target="tpu_custom_call" | custom-call | flops 1 | bytes 1 | tf_op jit(solution)/shard_map/interior/pallas_call | solution.py:345
  13.7 1.9 %collective-permute-start = (f32[12,80,128]{2,1,0:T(8,128)S(1)}, f32[12,80,128]{2,1,0:T(8,128)S(1)}, u32[]{:S(2)}, u32[]{:S(2)}) collective-permute-start(f32[12,80,128]{2,1,0:T(8,128)S(1)} %get-tuple-element.25), channel_id=1, source_target_pairs={{0,1},{1,2},{2,3},{3,4},{4,5},{5,6},{6,7},{7,8},{8,9},{9,10},{10,1... | collective-permute-start | bytes 1474568 | tf_op jit(solution)/shard_map/ppermute | solution.py:361
  15.6 1.3 %collective-permute-start.2 = (f32[8,144,128]{2,1,0:T(8,128)S(1)}, f32[8,144,128]{2,1,0:T(8,128)S(1)}, u32[]{:S(2)}, u32[]{:S(2)}) collective-permute-start(f32[8,144,128]{2,1,0:T(8,128)S(1)} %get-tuple-element.27), channel_id=1, source_target_pairs={{0,16},{1,17},{2,18},{3,19},{4,20},{5,21},{6,22},{7,23},{8,24},{9,... | collective-permute-start | bytes 1769480 | tf_op jit(solution)/shard_map/ppermute | solution.py:359
  16.9 3.6 %collective-permute-start.1 = (f32[12,80,128]{2,1,0:T(8,128)S(1)}, f32[12,80,128]{2,1,0:T(8,128)S(1)}, u32[]{:S(2)}, u32[]{:S(2)}) collective-permute-start(f32[12,80,128]{2,1,0:T(8,128)S(1)} %get-tuple-element.26), channel_id=1, source_target_pairs={{1,0},{2,1},{3,2},{4,3},{5,4},{6,5},{7,6},{8,7},{9,8},{10,9},{11,1... | collective-permute-start | bytes 1474568 | tf_op jit(solution)/shard_map/ppermute | solution.py:362
  20.6 1.9 %collective-permute-start.3 = (f32[12,64,128]{2,1,0:T(8,128)S(1)}, f32[12,64,128]{2,1,0:T(8,128)S(1)}, u32[]{:S(2)}, u32[]{:S(2)}) collective-permute-start(f32[12,64,128]{2,1,0:T(8,128)S(1)} %get-tuple-element.29), channel_id=1, source_target_pairs={{0,1},{1,2},{2,3},{3,4},{4,5},{5,6},{6,7},{7,8},{8,9},{9,10},{10,1... | collective-permute-start | bytes 1179656 | tf_op jit(solution)/shard_map/ppermute | solution.py:361
  22.5 3.6 %collective-permute-start.4 = (f32[12,64,128]{2,1,0:T(8,128)S(1)}, f32[12,64,128]{2,1,0:T(8,128)S(1)}, u32[]{:S(2)}, u32[]{:S(2)}) collective-permute-start(f32[12,64,128]{2,1,0:T(8,128)S(1)} %get-tuple-element.30), channel_id=1, source_target_pairs={{1,0},{2,1},{3,2},{4,3},{5,4},{6,5},{7,6},{8,7},{9,8},{10,9},{11,1... | collective-permute-start | bytes 1179656 | tf_op jit(solution)/shard_map/ppermute | solution.py:362
  26.2 0.0 collective-permute-done.before
  26.2 1.3 %collective-permute-start.5 = (f32[8,80,128]{2,1,0:T(8,128)S(1)}, f32[8,80,128]{2,1,0:T(8,128)S(1)}, u32[]{:S(2)}, u32[]{:S(2)}) collective-permute-start(f32[8,80,128]{2,1,0:T(8,128)S(1)} %get-tuple-element.31), channel_id=1, source_target_pairs={{0,16},{1,17},{2,18},{3,19},{4,20},{5,21},{6,22},{7,23},{8,24},{9,... | collective-permute-start | bytes 983048 | tf_op jit(solution)/shard_map/ppermute | solution.py:359
  27.5 0.0 collective-permute-done.1.after
  27.5 5.6 %collective-permute-done.2.behind.incoming = f32[8,144,128]{2,1,0:T(8,128)S(1)} collective-permute-done((f32[8,144,128]{2,1,0:T(8,128)S(1)}, f32[8,144,128]{2,1,0:T(8,128)S(1)}, u32[]{:S(2)}, u32[]{:S(2)}) %collective-permute-start.2) | collective-permute-done | bytes 589856 | tf_op jit(solution)/shard_map/ppermute | solution.py:359
  33.1 0.0 copy-done.1
  33.1 0.0 copy-done
  33.1 0.0 copy-done.3
  33.1 0.0 copy-done.2
  33.2 7.7 %border.2 = (f32[12,3,800,128]{3,2,1,0:T(8,128)S(1)}, f32[12,3,160,128]{3,2,1,0:T(8,128)S(1)}, f32[12,160,128]{2,1,0:T(8,128)S(1)}, f32[8,160,128]{2,1,0:T(8,128)S(1)}) custom-call(s32[12]{0:T(128)S(1)} %copy-done.2, s32[12]{0:T(128)S(1)} %copy-done, f32[16]{0:T(128)S(1)} %copy-done.1, f32[16]{0:T(128)S(1)} %copy-done.3, ...), custom_call_target="tpu_custom_call", output_to_operand_aliasing={{0}: (4, {})} | custom-call | flops 1 | bytes 1 | tf_op jit(solution)/shard_map/border/pallas_call | solution.py:364
  40.9 1.3 %collective-permute-start.7 = (f32[8,160,128]{2,1,0:T(8,128)S(1)}, f32[8,160,128]{2,1,0:T(8,128)S(1)}, u32[]{:S(2)}, u32[]{:S(2)}) collective-permute-start(f32[8,160,128]{2,1,0:T(8,128)S(1)} %get-tuple-element.40), channel_id=1, source_target_pairs={{0,16},{1,17},{2,18},{3,19},{4,20},{5,21},{6,22},{7,23},{8,24},{9,... | collective-permute-start | bytes 1966088 | tf_op jit(solution)/shard_map/ppermute | solution.py:377
  42.2 0.0 collective-permute-done.5.behind.incoming
  42.2 0.0 collective-permute-done.3.before
  42.2 0.0 collective-permute-done.4.after
  42.2 7.2 %border.3 = (f32[12,3,800,128]{3,2,1,0:T(8,128)S(1)}, f32[12,3,128,128]{3,2,1,0:T(8,128)S(1)}, f32[12,128,128]{2,1,0:T(8,128)S(1)}, f32[8,128,128]{2,1,0:T(8,128)S(1)}) custom-call(s32[12]{0:T(128)S(1)} %copy-done.2, s32[12]{0:T(128)S(1)} %copy-done, f32[16]{0:T(128)S(1)} %copy-done.1, f32[16]{0:T(128)S(1)} %copy-done.3, ...), custom_call_target="tpu_custom_call", output_to_operand_aliasing={{0}: (4, {})} | custom-call | flops 1 | bytes 1 | tf_op jit(solution)/shard_map/border/pallas_call | solution.py:364
  49.4 1.3 %collective-permute-start.6 = (f32[8,128,128]{2,1,0:T(8,128)S(1)}, f32[8,128,128]{2,1,0:T(8,128)S(1)}, u32[]{:S(2)}, u32[]{:S(2)}) collective-permute-start(f32[8,128,128]{2,1,0:T(8,128)S(1)} %get-tuple-element.33), channel_id=1, source_target_pairs={{0,16},{1,17},{2,18},{3,19},{4,20},{5,21},{6,22},{7,23},{8,24},{9,... | collective-permute-start | bytes 1572872 | tf_op jit(solution)/shard_map/ppermute | solution.py:377
  50.7 1.0 %resume.4.refs_1_ = f32[12,80,128]{2,1,0:T(8,128)S(1)} custom-call(s32[12]{0:T(128)S(1)} %copy-done, f32[16]{0:T(128)S(1)} %copy-done.1, f32[12,3,80,128]{3,2,1,0:T(8,128)S(1)} %get-tuple-element.37.entry_ref, f32[8,80,128]{2,1,0:T(8,128)S(1)} %collective-permute-done.5.behind.incoming, ...), custom_call_target="tpu_custom_call", output_to_operand_aliasing={{}: (4, {})} | custom-call | flops 1 | bytes 1 | tf_op jit(solution)/shard_map/resume/pallas_call | solution.py:382
  51.7 1.3 %resume.3.refs_0_ = f32[12,144,128]{2,1,0:T(8,128)S(1)} custom-call(s32[12]{0:T(128)S(1)} %copy-done, f32[16]{0:T(128)S(1)} %copy-done.1, f32[12,3,144,128]{3,2,1,0:T(8,128)S(1)} %get-tuple-element.35.entry_ref, f32[8,144,128]{2,1,0:T(8,128)S(1)} %collective-permute-done.2.behind.incoming, ...), custom_call_target="tpu_custom_call", output_to_operand_aliasing={{}: (4, {})} | custom-call | flops 1 | bytes 1 | tf_op jit(solution)/shard_map/resume/pallas_call | solution.py:382
  52.9 7.2 %collective-permute-done.7.incoming = f32[8,160,128]{2,1,0:T(8,128)S(1)} collective-permute-done((f32[8,160,128]{2,1,0:T(8,128)S(1)}, f32[8,160,128]{2,1,0:T(8,128)S(1)}, u32[]{:S(2)}, u32[]{:S(2)}) %collective-permute-start.7) | collective-permute-done | bytes 655392 | tf_op jit(solution)/shard_map/ppermute | solution.py:377
  60.1 1.3 %resume.5.refs_2_ = f32[12,160,128]{2,1,0:T(8,128)S(1)} custom-call(s32[12]{0:T(128)S(1)} %copy-done, f32[16]{0:T(128)S(1)} %copy-done.1, f32[12,3,160,128]{3,2,1,0:T(8,128)S(1)} %get-tuple-element.39.entry_ref, f32[8,160,128]{2,1,0:T(8,128)S(1)} %collective-permute-done.7.incoming, ...), custom_call_target="tpu_custom_call", output_to_operand_aliasing={{}: (4, {})} | custom-call | flops 1 | bytes 1 | tf_op jit(solution)/shard_map/resume/pallas_call | solution.py:382
  61.4 9.9 %collective-permute-done.6.incoming = f32[8,128,128]{2,1,0:T(8,128)S(1)} collective-permute-done((f32[8,128,128]{2,1,0:T(8,128)S(1)}, f32[8,128,128]{2,1,0:T(8,128)S(1)}, u32[]{:S(2)}, u32[]{:S(2)}) %collective-permute-start.6) | collective-permute-done | bytes 524320 | tf_op jit(solution)/shard_map/ppermute | solution.py:377
  71.3 3.0 %last.1 = (f32[12,128,128]{2,1,0:T(8,128)S(1)}, f32[12,512,128]{2,1,0:T(8,128)}) custom-call(s32[12]{0:T(128)S(1)} %copy-done, f32[16]{0:T(128)S(1)} %copy-done.1, f32[12,3,128,128]{3,2,1,0:T(8,128)S(1)} %get-tuple-element.32.entry_ref, f32[8,128,128]{2,1,0:T(8,128)S(1)} %collective-permute-done.6.incoming, ...), custom_call_target="tpu_custom_call", output_to_operand_aliasing={{0}: (4, {})} | custom-call | flops 1 | bytes 1 | tf_op jit(solution)/shard_map/last/pallas_call | solution.py:395
Async XLA Ops:
  0.0 33.1 %copy-start.1 = (f32[16]{0:T(128)S(1)}, f32[16]{0:T(128)}, u32[]{:S(2)}) copy-start(f32[16]{0:T(128)} %near.11) | copy-start | bytes 196
  0.0 33.1 %copy-start = (s32[12]{0:T(128)S(1)}, s32[12]{0:T(128)}, u32[]{:S(2)}) copy-start(s32[12]{0:T(128)} %slots.11) | copy-start | bytes 148
  0.0 33.1 %copy-start.3 = (f32[16]{0:T(128)S(1)}, f32[16]{0:T(128)}, u32[]{:S(2)}) copy-start(f32[16]{0:T(128)} %lens.3) | copy-start | bytes 196
  0.0 33.1 %copy-start.2 = (s32[12]{0:T(128)S(1)}, s32[12]{0:T(128)}, u32[]{:S(2)}) copy-start(s32[12]{0:T(128)} %widths.3) | copy-start | bytes 148
  13.7 12.5 %collective-permute-start = (f32[12,80,128]{2,1,0:T(8,128)S(1)}, f32[12,80,128]{2,1,0:T(8,128)S(1)}, u32[]{:S(2)}, u32[]{:S(2)}) collective-permute-start(f32[12,80,128]{2,1,0:T(8,128)S(1)} %get-tuple-element.25), channel_id=1, source_target_pairs={{0,1},{1,2},{2,3},{3,4},{4,5},{5,6},{6,7},{7,8},{8,9},{9,10},{10,1... | collective-permute-start | bytes 1474568 | tf_op jit(solution)/shard_map/ppermute | solution.py:361
  15.6 17.5 %collective-permute-start.2 = (f32[8,144,128]{2,1,0:T(8,128)S(1)}, f32[8,144,128]{2,1,0:T(8,128)S(1)}, u32[]{:S(2)}, u32[]{:S(2)}) collective-permute-start(f32[8,144,128]{2,1,0:T(8,128)S(1)} %get-tuple-element.27), channel_id=1, source_target_pairs={{0,16},{1,17},{2,18},{3,19},{4,20},{5,21},{6,22},{7,23},{8,24},{9,... | collective-permute-start | bytes 1769480 | tf_op jit(solution)/shard_map/ppermute | solution.py:359
  16.9 10.5 %collective-permute-start.1 = (f32[12,80,128]{2,1,0:T(8,128)S(1)}, f32[12,80,128]{2,1,0:T(8,128)S(1)}, u32[]{:S(2)}, u32[]{:S(2)}) collective-permute-start(f32[12,80,128]{2,1,0:T(8,128)S(1)} %get-tuple-element.26), channel_id=1, source_target_pairs={{1,0},{2,1},{3,2},{4,3},{5,4},{6,5},{7,6},{8,7},{9,8},{10,9},{11,1... | collective-permute-start | bytes 1474568 | tf_op jit(solution)/shard_map/ppermute | solution.py:362
  20.6 21.6 %collective-permute-start.3 = (f32[12,64,128]{2,1,0:T(8,128)S(1)}, f32[12,64,128]{2,1,0:T(8,128)S(1)}, u32[]{:S(2)}, u32[]{:S(2)}) collective-permute-start(f32[12,64,128]{2,1,0:T(8,128)S(1)} %get-tuple-element.29), channel_id=1, source_target_pairs={{0,1},{1,2},{2,3},{3,4},{4,5},{5,6},{6,7},{7,8},{8,9},{9,10},{10,1... | collective-permute-start | bytes 1179656 | tf_op jit(solution)/shard_map/ppermute | solution.py:361
  22.5 19.7 %collective-permute-start.4 = (f32[12,64,128]{2,1,0:T(8,128)S(1)}, f32[12,64,128]{2,1,0:T(8,128)S(1)}, u32[]{:S(2)}, u32[]{:S(2)}) collective-permute-start(f32[12,64,128]{2,1,0:T(8,128)S(1)} %get-tuple-element.30), channel_id=1, source_target_pairs={{1,0},{2,1},{3,2},{4,3},{5,4},{6,5},{7,6},{8,7},{9,8},{10,9},{11,1... | collective-permute-start | bytes 1179656 | tf_op jit(solution)/shard_map/ppermute | solution.py:362
  26.2 16.0 %collective-permute-start.5 = (f32[8,80,128]{2,1,0:T(8,128)S(1)}, f32[8,80,128]{2,1,0:T(8,128)S(1)}, u32[]{:S(2)}, u32[]{:S(2)}) collective-permute-start(f32[8,80,128]{2,1,0:T(8,128)S(1)} %get-tuple-element.31), channel_id=1, source_target_pairs={{0,16},{1,17},{2,18},{3,19},{4,20},{5,21},{6,22},{7,23},{8,24},{9,... | collective-permute-start | bytes 983048 | tf_op jit(solution)/shard_map/ppermute | solution.py:359
  40.9 19.2 %collective-permute-start.7 = (f32[8,160,128]{2,1,0:T(8,128)S(1)}, f32[8,160,128]{2,1,0:T(8,128)S(1)}, u32[]{:S(2)}, u32[]{:S(2)}) collective-permute-start(f32[8,160,128]{2,1,0:T(8,128)S(1)} %get-tuple-element.40), channel_id=1, source_target_pairs={{0,16},{1,17},{2,18},{3,19},{4,20},{5,21},{6,22},{7,23},{8,24},{9,... | collective-permute-start | bytes 1966088 | tf_op jit(solution)/shard_map/ppermute | solution.py:377
  49.4 21.9 %collective-permute-start.6 = (f32[8,128,128]{2,1,0:T(8,128)S(1)}, f32[8,128,128]{2,1,0:T(8,128)S(1)}, u32[]{:S(2)}, u32[]{:S(2)}) collective-permute-start(f32[8,128,128]{2,1,0:T(8,128)S(1)} %get-tuple-element.33), channel_id=1, source_target_pairs={{0,16},{1,17},{2,18},{3,19},{4,20},{5,21},{6,22},{7,23},{8,24},{9,... | collective-permute-start | bytes 1572872 | tf_op jit(solution)/shard_map/ppermute | solution.py:377

commit v3 on v2

v3 whole, which is shorter than its diff:
```python
import functools

import jax
import jax.numpy as jnp
from jax import lax
from jax.experimental import pallas as pl
from jax.experimental.pallas import tpu as pltpu
from jax.sharding import PartitionSpec as P

WMAX = 8
RIM = WMAX + 1
LANES = 128
SUB = 8
EDGES = (RIM, 4, 0)
INNER_ROWS = 4
PARTS = (3, 2, 2)
VMEM_LIMIT = 16 * 1024 * 1024
INNER = 2
F32, BF16 = jnp.float32, jnp.bfloat16


def row_groups(row_count):
    first = (row_count - INNER_ROWS) // 2
    groups = [((first, first + INNER_ROWS),), ((RIM, first), (first + INNER_ROWS, row_count - RIM))]
    for outer, inner in zip(EDGES[:-1], EDGES[1:]):
        groups.append(((inner, outer), (row_count - outer, row_count - inner)))
    return groups


def rows_in(group):
    return sum(stop - start for start, stop in group)


def split(value, parts):
    found = []
    for part in range(parts):
        found.append(value.astype(BF16))
        if part + 1 < parts:
            value = value - found[-1].astype(F32)
    return found


def make_bands(planes, widths, band_ref):
    source = lax.broadcasted_iota(jnp.int32, (LANES, 2 * LANES), 0)
    target = lax.broadcasted_iota(jnp.int32, (LANES, 2 * LANES), 1)
    across = jnp.where(target >= LANES + LANES // 2, source + 2 * LANES, source)
    offset = across - target
    distance = jnp.abs(offset)

    def plane(k, carry):
        half_width = widths[k]
        rim = (distance == half_width + 1).astype(F32)
        edge = (distance == half_width).astype(F32)
        inside = (distance <= half_width).astype(F32)
        both = rim + edge
        for field, value in enumerate((rim - edge, jnp.where(offset > 0, both, -both), inside)):
            band_ref[k, field] = value.astype(BF16)
        return carry

    lax.fori_loop(0, planes, plane, 0)


def entries_of(k, half_width, near, scale, group, blocks, x_ref, band_ref, left_ref, beside_ref, entry_ref):
    def row(index):
        return x_ref[k, pl.ds(pl.multiple_of(index * blocks, blocks), blocks), :]

    place = 0
    for start, stop in group:
        first = start + RIM
        total = row(first)
        for step in range(1, WMAX + 1):
            total = total + jnp.where(step <= half_width, row(first - step) + row(first + step), 0.0)
        for at in range(first, stop + RIM):
            high, low = at + half_width, at - half_width
            rim_high, edge_high, edge_low, rim_low = row(high + 1), row(high), row(low), row(low - 1)
            values = (total, (rim_high + edge_high) - (edge_low + rim_low),
                      (rim_high - edge_high) - (edge_low - rim_low))
            total = total + (rim_high - edge_low)
            here = slice(place * blocks, (place + 1) * blocks)
            for field, value in enumerate(values):
                for part, piece in enumerate(split(value, PARTS[field])):
                    left_ref[field, here, part * LANES:(part + 1) * LANES] = piece
            place += 1
    length = place * blocks
    pitch = blocks + SUB
    left_lane = lax.broadcasted_iota(jnp.int32, (blocks, LANES), 1) < LANES // 2
    factors = (-scale, -0.25 * scale, -scale)
    added = (near, 0.0, near)
    for field in range(3):
        weight = jnp.concatenate([band_ref[k, field]] * PARTS[field], axis=0)
        product = jnp.dot(left_ref[field, :length, :PARTS[field] * LANES], weight, preferred_element_type=F32)
        for at in range(place):
            beside_ref[field, pl.ds(at * pitch + SUB, blocks), :] = product[at * blocks:(at + 1) * blocks, LANES:]
        for at in range(place):
            beside = jnp.where(left_lane, beside_ref[field, pl.ds(at * pitch + SUB - 1, blocks), :],
                               beside_ref[field, pl.ds(at * pitch + SUB + 1, blocks), :])
            value = factors[field] * (product[at * blocks:(at + 1) * blocks, :LANES] + beside)
            entry_ref[k, field, pl.ds(at * blocks, blocks), :] = value + added[field] if field != 1 else value


def sweep(planes, length, near_of, entry_ref, conv_ref, start, finish):
    step = next(count * SUB for count in (4, 3, 2, 1) if length % (count * SUB) == 0)

    def part(index, carry):
        where = pl.ds(pl.multiple_of(index * step, step), step)
        state = start(where, (step, LANES))
        now, then = state[:4], state[4:]
        for k in range(planes):
            xx, xy, yy = [entry_ref[k, i, where, :] for i in range(3)]
            kept = 1.0 - near_of(k)
            new = [
                xx * now[0] + xy * now[2] + kept * then[0],
                xx * now[1] + xy * now[3] + kept * then[1],
                xy * now[0] + yy * now[2] + kept * then[2],
                xy * now[1] + yy * now[3] + kept * then[3],
            ]
            now, then = new, now
            conv_ref[k, where, :] = 1.0 - 0.5 * (new[0] + new[3])
        finish(where, now + then)
        return carry

    lax.fori_loop(0, length // step, part, 0)


def identity_state(where, shape):
    one, zero = jnp.ones(shape, F32), jnp.zeros(shape, F32)
    return [one, zero, zero, one] * 2


def writer(state_ref):
    def finish(where, state):
        for i, value in enumerate(state):
            state_ref[i, where, :] = value

    return finish


def group_stage(sizes, part, scalars, x_ref, band_ref, left_ref, beside_ref, entry_ref, conv_ref, state_ref,
                before_plane=lambda k: None):
    planes, rows, blocks, groups = sizes
    widths, slots, near, lens = scalars
    beside_ref[...] = jnp.zeros(beside_ref.shape, F32)

    def plane(k, carry):
        before_plane(k)
        half_width = widths[k]
        count = (2 * half_width + 1).astype(F32)
        entries_of(k, half_width, near[slots[k]], lens[slots[k]] / (count * count), groups[part], blocks, x_ref,
                   band_ref, left_ref, beside_ref, entry_ref)
        return carry

    lax.fori_loop(0, planes, plane, 0)

    @pl.when(lax.axis_index("depth") == 0)
    def _():
        sweep(planes, rows_in(groups[part]) * blocks, lambda k: near[slots[k]], entry_ref, conv_ref, identity_state,
              writer(state_ref))


def first_kernel(sizes, widths_hbm, slots_hbm, near_hbm, lens_hbm, potential_hbm, x_ref, band_ref, entry_ref, conv_ref,
                 state_ref, left_ref, beside_ref, tiles_ref, widths, slots, near, lens, plane_sems, table_sems):
    planes, rows, blocks, groups = sizes
    tables = ((widths_hbm, widths), (slots_hbm, slots), (near_hbm, near), (lens_hbm, lens))
    copies = [pltpu.make_async_copy(*pair, table_sems.at[i]) for i, pair in enumerate(tables)]
    for copy in copies:
        copy.start()

    def plane_copy(k):
        return pltpu.make_async_copy(potential_hbm.at[k], tiles_ref.at[k], plane_sems.at[k])

    for k in range(planes):
        plane_copy(k).start()
    for copy in copies:
        copy.wait()
    make_bands(planes, widths, band_ref)

    def arrive(k):
        plane_copy(k).wait()
        for row in range(rows):
            for half in range(blocks // SUB):
                start = (row // SUB) * SUB * blocks + half * SUB * SUB + row % SUB
                x_ref[k, pl.ds((row + RIM) * blocks + half * SUB, SUB), :] = tiles_ref[
                    k, pl.ds(start, SUB, stride=SUB), :]

    group_stage(sizes, 0, (widths, slots, near, lens), x_ref, band_ref, left_ref, beside_ref, entry_ref, conv_ref,
                state_ref, arrive)


def second_kernel(sizes, widths, slots, near, lens, x_ref, band_ref, entry_ref, conv_ref, state_ref, *rest):
    planes, rows, blocks, groups = sizes
    sends, (left_ref, beside_ref) = rest[:-2], rest[-2:]

    def leave(k):
        for part, (outer, inner) in enumerate(zip(EDGES[:-1], EDGES[1:])):
            begin, count = RIM - outer, outer - inner
            for ref, first in ((sends[2 * part], rows - begin - count), (sends[2 * part + 1], begin)):
                ref[k] = x_ref[k, pl.ds((first + RIM) * blocks, count * blocks), :]

    group_stage(sizes, 1, (widths, slots, near, lens), x_ref, band_ref, left_ref, beside_ref, entry_ref, conv_ref,
                state_ref, leave)


def border_kernel(sizes, part, widths, slots, near, lens, x_in, band_ref, before, after, behind, x_ref, entry_ref,
                  conv_ref, state_ref, left_ref, beside_ref):
    planes, rows, blocks, groups = sizes
    outer, inner = EDGES[part], EDGES[part + 1]
    begin, count = RIM - outer, outer - inner

    def arrive(k):
        x_ref[k, pl.ds((RIM - begin - count) * blocks, count * blocks), :] = before[k]
        x_ref[k, pl.ds((RIM + rows + begin) * blocks, count * blocks), :] = after[k]

    group_stage(sizes, INNER + part, (widths, slots, near, lens), x_ref, band_ref, left_ref, beside_ref, entry_ref,
                conv_ref, state_ref, arrive)


def resume(sizes, part, turn, slots, near, entry_ref, incoming, conv_ref, finish):
    planes, rows, blocks, groups = sizes

    @pl.when(lax.axis_index("depth") == turn)
    def _():
        sweep(planes, rows_in(groups[part]) * blocks, lambda k: near[slots[k]], entry_ref, conv_ref,
              lambda where, shape: [incoming[i, where, :] for i in range(8)], finish)


def resume_kernel(sizes, part, turn, slots, near, entry_ref, incoming, conv_in, conv_ref, *state_ref):
    finish = writer(state_ref[0]) if state_ref else lambda where, state: None
    resume(sizes, part, turn, slots, near, entry_ref, incoming, conv_ref, finish)


def last_kernel(sizes, turn, slots, near, entry_ref, incoming, conv_in, *refs):
    planes, rows, blocks, groups = sizes
    others, (conv_ref, out_hbm, tiles_ref, sems) = refs[:-4], refs[-4:]
    part = len(groups) - 1
    resume(sizes, part, turn, slots, near, entry_ref, incoming, conv_ref, lambda where, state: None)

    def plane_copy(k):
        return pltpu.make_async_copy(tiles_ref.at[k], out_hbm.at[k], sems.at[k])

    def plane(k, carry):
        for group, ref in zip(groups, (*others, conv_ref)):
            place = 0
            for start, stop in group:
                for row in range(start, stop):
                    for half in range(blocks // SUB):
                        to = (row // SUB) * SUB * blocks + half * SUB * SUB + row % SUB
                        tiles_ref[k, pl.ds(to, SUB, stride=SUB), :] = ref[k, pl.ds(place * blocks + half * SUB, SUB), :]
                    place += 1
        plane_copy(k).start()
        return carry

    lax.fori_loop(0, planes, plane, 0)
    for k in range(planes):
        plane_copy(k).wait()


def per_device(potential, widths, plane_slot, ratio_near, ratio_lens):
    planes, rows, cols = potential.shape
    blocks = cols // LANES
    groups = row_groups(rows)
    sizes = (planes, rows, blocks, groups)
    depth_count, sky_count = lax.axis_size("depth"), lax.axis_size("sky")
    up = [(i, i + 1) for i in range(sky_count - 1)]
    down = [(j, i) for i, j in up]
    ahead = [(i, i + 1) for i in range(depth_count - 1)]
    tiled = potential.reshape(planes, rows // SUB, SUB, blocks, LANES).transpose(0, 1, 3, 2, 4)
    tiled = tiled.reshape(planes, rows * blocks, LANES)
    smem = pl.BlockSpec(memory_space=pltpu.SMEM)
    vmem = pl.BlockSpec(memory_space=pltpu.VMEM)
    anywhere = pl.BlockSpec(memory_space=pl.ANY)
    params = pltpu.CompilerParams(vmem_limit_bytes=VMEM_LIMIT)
    scalars = (widths, plane_slot, ratio_near, ratio_lens)
    dma = pltpu.SemaphoreType.DMA
    cost = pl.CostEstimate(flops=1, transcendentals=0, bytes_accessed=1)

    def held(*shape, dtype=F32):
        return pltpu.VMEM(shape, dtype)

    def moved(*shape):
        return jax.ShapeDtypeStruct(shape, F32)

    def in_vmem(array):
        return pltpu.with_memory_space_constraint(array, pltpu.VMEM)

    def in_hbm(array):
        return pltpu.with_memory_space_constraint(array, pltpu.HBM)

    x_shape = held(planes, (rows + 2 * RIM) * blocks, LANES)
    band_shape = held(planes, 3, LANES, 2 * LANES, dtype=BF16)

    def group_shapes(part):
        length = rows_in(groups[part]) * blocks
        return [held(planes, 3, length, LANES), held(planes, length, LANES), moved(8, length, LANES)]

    def group_scratch(part):
        count = rows_in(groups[part])
        return [held(3, count * blocks, max(PARTS) * LANES, dtype=BF16),
                held(3, (count + 1) * (blocks + SUB), LANES)]

    sends = []
    for outer, inner in zip(EDGES[:-1], EDGES[1:]):
        sends += [moved(planes, (outer - inner) * blocks, LANES)] * 2
    x, bands, *group = pl.pallas_call(
        functools.partial(first_kernel, sizes),
        out_shape=[x_shape, band_shape, *group_shapes(0)],
        in_specs=[anywhere] * 5,
        out_specs=[vmem] * 5,
        scratch_shapes=[
            *group_scratch(0), held(planes, rows * blocks, LANES),
            *[pltpu.SMEM(array.shape, array.dtype) for array in scalars], dma((planes,)), dma((len(scalars),))],
        compiler_params=params,
        cost_estimate=cost,
        name="first",
    )(*[in_hbm(array) for array in (*scalars, tiled)])
    made = [group]
    arriving = [lax.ppermute(group[2], "depth", ahead)]
    *group, = pl.pallas_call(
        functools.partial(second_kernel, sizes),
        out_shape=[*group_shapes(1), *sends],
        in_specs=[smem] * 4 + [vmem] * 2,
        out_specs=[vmem] * (3 + len(sends)),
        scratch_shapes=group_scratch(1),
        compiler_params=params,
        cost_estimate=cost,
        name="second",
    )(*scalars, in_vmem(x), in_vmem(bands))
    group, packed = group[:3], group[3:]
    made.append(group)
    arriving.append(lax.ppermute(group[2], "depth", ahead))
    for part, (outer, inner) in enumerate(zip(EDGES[:-1], EDGES[1:])):
        before = lax.ppermute(packed[2 * part], "sky", up)
        after = lax.ppermute(packed[2 * part + 1], "sky", down)
        x, *group = pl.pallas_call(
            functools.partial(border_kernel, sizes, part),
            out_shape=[x_shape, *group_shapes(INNER + part)],
            in_specs=[smem] * 4 + [vmem] * 4 + [anywhere],
            out_specs=[vmem] * 4,
            scratch_shapes=group_scratch(INNER + part),
            input_output_aliases={4: 0},
            compiler_params=params,
            cost_estimate=cost,
            name="border",
        )(*scalars, in_vmem(x), in_vmem(bands), before, after, arriving[part])
        made.append(group)
        arriving.append(lax.ppermute(group[2], "depth", ahead))
    entries, convs = [group[0] for group in made], [group[1] for group in made]

    for turn in range(1, depth_count):
        last = turn == depth_count - 1
        for part in range(len(groups) - last):
            convs[part], *state = pl.pallas_call(
                functools.partial(resume_kernel, sizes, part, turn),
                out_shape=group_shapes(part)[1:2] + ([] if last else group_shapes(part)[2:3]),
                in_specs=[smem] * 2 + [vmem] * 3,
                out_specs=[vmem] * (1 if last else 2),
                input_output_aliases={4: 0},
                compiler_params=params,
                cost_estimate=cost,
                name="resume",
            )(plane_slot, ratio_near, in_vmem(entries[part]), arriving[part], in_vmem(convs[part]))
            if state:
                arriving[part] = lax.ppermute(state[0], "depth", ahead)

    conv, out = pl.pallas_call(
        functools.partial(last_kernel, sizes, depth_count - 1),
        out_shape=[group_shapes(len(groups) - 1)[1], moved(planes, rows * blocks, LANES)],
        in_specs=[smem] * 2 + [vmem] * (3 + len(groups) - 1),
        out_specs=[vmem, anywhere],
        scratch_shapes=[held(planes, rows * blocks, LANES), dma((planes,))],
        input_output_aliases={4: 0},
        compiler_params=params,
        cost_estimate=cost,
        name="last",
    )(plane_slot, ratio_near, in_vmem(entries[-1]), arriving[-1], in_vmem(convs[-1]),
      *[in_vmem(conv) for conv in convs[:-1]])
    out = out.reshape(planes, rows // SUB, blocks, SUB, LANES).transpose(0, 1, 3, 2, 4)
    return out.reshape(planes, rows, cols)


def solution(mesh):
    return jax.shard_map(
        per_device,
        mesh=mesh,
        in_specs=(P("depth", "sky", None), P("depth"), P("depth"), P(), P()),
        out_specs=P("depth", "sky", None),
        check_vma=False,
    )
```

time: 74.8 us -> 65.9 us (0.88)
  Pallas kernels: 35.1 us -> 24.1 us
  waiting for transfers between devices: 22.7 us -> 25.1 us
    pallas_call x3 -> x4, Pallas kernels: 28.6 us -> 17.6 us  [the longest x2 8.23 us: per_device(): pl.pallas_call(functools.partial(border_kernel, sizes, part), out_shape=[...]
    ppermute x2, waiting for transfers between devices: 0.01 us -> 7.05 us  [per_device(): before = lax.ppermute(packed[2 * part], 'sky', up)]
    ppermute x4, waiting for transfers between devices: 22.7 us -> 18 us  [the longest x3 18 us: per_device(): arriving.append(lax.ppermute(group[2], 'depth', ahead))]
  transfers between devices with their start and end apart: 8 -> 8, of which waited for: 3 -> 4; matrix products, arithmetic and copies ran while one was open for 0% -> 0% of each run, Pallas kernels for 25% -> 24%
where the time goes in v3:
time: 65.9 us; the launch traced here: 65.7 us
  waiting for transfers between devices  25.1 us (38%)
  Pallas kernels  24.1 us (37%)
  starting transfers between devices  16.3 us (25%)
    ppermute x3, waiting for transfers between devices, per_device(): arriving.append(lax.ppermute(group[2], 'depth', ahead))  18 us
    pallas_call x2, Pallas kernels, per_device(): pl.pallas_call(functools.partial(border_kernel, sizes, part), out_shape=[...  8.23 us
    ppermute x2, starting transfers between devices, per_device(): after = lax.ppermute(packed[2 * part + 1], 'sky', down)  7.28 us
    ppermute x2, waiting for transfers between devices, per_device(): before = lax.ppermute(packed[2 * part], 'sky', up)  7.05 us
    pallas_call x1, Pallas kernels, per_device(): pl.pallas_call(functools.partial(first_kernel, sizes), out_shape=[x_shape...  5.06 us
    pallas_call x1, Pallas kernels, per_device(): pl.pallas_call(functools.partial(second_kernel, sizes), out_shape=[*group...  4.36 us
    ppermute x3, starting transfers between devices, per_device(): arriving.append(lax.ppermute(group[2], 'depth', ahead))  3.88 us
    ppermute x2, starting transfers between devices, per_device(): before = lax.ppermute(packed[2 * part], 'sky', up)  3.84 us
  transfers between devices with their start and end apart: 8, of which 4 were waited for; matrix products, arithmetic and copies ran while one was open for 0% of the time, Pallas kernels for 24%

profile of v3, /device:TPU:6, one launch (start us, length us, event | category | flops | bytes accessed | tf_op | source)
XLA Modules:
  0.0 65.7 jit_solution(1359960410571798003)
XLA Ops:
  0.0 0.0 copy-start.1
  0.0 0.0 copy-start
  0.0 0.0 copy-start.3
  0.0 0.0 copy-start.2
  0.0 5.1 %first.1 = (f32[12,800,128]{2,1,0:T(8,128)S(1)}, bf16[12,3,128,256]{3,2,1,0:T(8,128)(2,1)S(1)}, f32[12,3,64,128]{3,2,1,0:T(8,128)S(1)}, f32[12,64,128]{2,1,0:T(8,128)S(1)}, f32[8,64,128]{2,1,0:T(8,128)S(1)}) custom-call(s32[12]{0:T(128)} %widths.5, s32[12]{0:T(128)} %slots.13, f32[16]{0:T(128)} %near.13, f32[16]{0:T(128)} %lens.5, f32[12,512,128]{2,1,0:T(8,128)} %bitcast.10), custom_call_target="tpu_custom_call" | custom-call | flops 1 | bytes 1 | tf_op jit(solution)/shard_map/first/pallas_call | solution.py:303
  5.1 1.3 %collective-permute-start.2 = (f32[8,64,128]{2,1,0:T(8,128)S(1)}, f32[8,64,128]{2,1,0:T(8,128)S(1)}, u32[]{:S(2)}, u32[]{:S(2)}) collective-permute-start(f32[8,64,128]{2,1,0:T(8,128)S(1)} %get-tuple-element.29), channel_id=1, source_target_pairs={{0,16},{1,17},{2,18},{3,19},{4,20},{5,21},{6,22},{7,23},{8,24},{9,... | collective-permute-start | bytes 786440 | tf_op jit(solution)/shard_map/ppermute | solution.py:316
  6.4 0.0 copy-done.1
  6.4 0.0 copy-done
  6.4 0.0 copy-done.3
  6.4 0.0 copy-done.2
  6.4 4.4 %second.1 = (f32[12,3,160,128]{3,2,1,0:T(8,128)S(1)}, f32[12,160,128]{2,1,0:T(8,128)S(1)}, f32[8,160,128]{2,1,0:T(8,128)S(1)}, f32[12,80,128]{2,1,0:T(8,128)S(1)...) custom-call(s32[12]{0:T(128)S(1)} %copy-done.2, s32[12]{0:T(128)S(1)} %copy-done, ...), custom_call_target="tpu_custom_call" | custom-call | flops 1 | bytes 1 | tf_op jit(solution)/shard_map/second/pallas_call | solution.py:317
  10.8 1.3 %collective-permute-start.5 = (f32[8,160,128]{2,1,0:T(8,128)S(1)}, f32[8,160,128]{2,1,0:T(8,128)S(1)}, u32[]{:S(2)}, u32[]{:S(2)}) collective-permute-start(f32[8,160,128]{2,1,0:T(8,128)S(1)} %get-tuple-element.33), channel_id=1, source_target_pairs={{0,16},{1,17},{2,18},{3,19},{4,20},{5,21},{6,22},{7,23},{8,24},{9,... | collective-permute-start | bytes 1966088 | tf_op jit(solution)/shard_map/ppermute | solution.py:329
  12.1 1.9 %collective-permute-start = (f32[12,80,128]{2,1,0:T(8,128)S(1)}, f32[12,80,128]{2,1,0:T(8,128)S(1)}, u32[]{:S(2)}, u32[]{:S(2)}) collective-permute-start(f32[12,80,128]{2,1,0:T(8,128)S(1)} %get-tuple-element.27), channel_id=1, source_target_pairs={{0,1},{1,2},{2,3},{3,4},{4,5},{5,6},{6,7},{7,8},{8,9},{9,10},{10,1... | collective-permute-start | bytes 1474568 | tf_op jit(solution)/shard_map/ppermute | solution.py:331
  14.0 3.6 %collective-permute-start.1 = (f32[12,80,128]{2,1,0:T(8,128)S(1)}, f32[12,80,128]{2,1,0:T(8,128)S(1)}, u32[]{:S(2)}, u32[]{:S(2)}) collective-permute-start(f32[12,80,128]{2,1,0:T(8,128)S(1)} %get-tuple-element.28), channel_id=1, source_target_pairs={{1,0},{2,1},{3,2},{4,3},{5,4},{6,5},{7,6},{8,7},{9,8},{10,9},{11,1... | collective-permute-start | bytes 1474568 | tf_op jit(solution)/shard_map/ppermute | solution.py:332
  17.7 1.9 %collective-permute-start.3 = (f32[12,64,128]{2,1,0:T(8,128)S(1)}, f32[12,64,128]{2,1,0:T(8,128)S(1)}, u32[]{:S(2)}, u32[]{:S(2)}) collective-permute-start(f32[12,64,128]{2,1,0:T(8,128)S(1)} %get-tuple-element.31), channel_id=1, source_target_pairs={{0,1},{1,2},{2,3},{3,4},{4,5},{5,6},{6,7},{7,8},{8,9},{9,10},{10,1... | collective-permute-start | bytes 1179656 | tf_op jit(solution)/shard_map/ppermute | solution.py:331
  19.6 0.0 collective-permute-done.2.behind.incoming
  19.6 3.6 %collective-permute-start.4 = (f32[12,64,128]{2,1,0:T(8,128)S(1)}, f32[12,64,128]{2,1,0:T(8,128)S(1)}, u32[]{:S(2)}, u32[]{:S(2)}) collective-permute-start(f32[12,64,128]{2,1,0:T(8,128)S(1)} %get-tuple-element.32), channel_id=1, source_target_pairs={{1,0},{2,1},{3,2},{4,3},{5,4},{6,5},{7,6},{8,7},{9,8},{10,9},{11,1... | collective-permute-start | bytes 1179656 | tf_op jit(solution)/shard_map/ppermute | solution.py:332
  23.3 4.2 %collective-permute-done.before = f32[12,80,128]{2,1,0:T(8,128)S(1)} collective-permute-done((f32[12,80,128]{2,1,0:T(8,128)S(1)}, f32[12,80,128]{2,1,0:T(8,128)S(1)}, u32[]{:S(2)}, u32[]{:S(2)}) %collective-permute-start) | collective-permute-done | bytes 491552 | tf_op jit(solution)/shard_map/ppermute | solution.py:331
  27.5 0.0 collective-permute-done.1.after
  27.5 4.3 %border.2 = (f32[12,800,128]{2,1,0:T(8,128)S(1)}, f32[12,3,160,128]{3,2,1,0:T(8,128)S(1)}, f32[12,160,128]{2,1,0:T(8,128)S(1)}, f32[8,160,128]{2,1,0:T(8,128)S(1)}) custom-call(s32[12]{0:T(128)S(1)} %copy-done.2, s32[12]{0:T(128)S(1)} %copy-done, f32[16]{0:T(128)S(1)} %copy-done.1, f32[16]{0:T(128)S(1)} %copy-done.3, ...), custom_call_target="tpu_custom_call", output_to_operand_aliasing={{0}: (4, {})} | custom-call | flops 1 | bytes 1 | tf_op jit(solution)/shard_map/border/pallas_call | solution.py:333
  31.8 1.3 %collective-permute-start.7 = (f32[8,160,128]{2,1,0:T(8,128)S(1)}, f32[8,160,128]{2,1,0:T(8,128)S(1)}, u32[]{:S(2)}, u32[]{:S(2)}) collective-permute-start(f32[8,160,128]{2,1,0:T(8,128)S(1)} %get-tuple-element.42), channel_id=1, source_target_pairs={{0,16},{1,17},{2,18},{3,19},{4,20},{5,21},{6,22},{7,23},{8,24},{9,... | collective-permute-start | bytes 1966088 | tf_op jit(solution)/shard_map/ppermute | solution.py:345
  33.1 2.8 %collective-permute-done.3.before = f32[12,64,128]{2,1,0:T(8,128)S(1)} collective-permute-done((f32[12,64,128]{2,1,0:T(8,128)S(1)}, f32[12,64,128]{2,1,0:T(8,128)S(1)}, u32[]{:S(2)}, u32[]{:S(2)}) %collective-permute-start.3) | collective-permute-done | bytes 393248 | tf_op jit(solution)/shard_map/ppermute | solution.py:331
  35.9 0.0 collective-permute-done.4.after
  35.9 0.0 collective-permute-done.5.behind.incoming
  35.9 3.9 %border.3 = (f32[12,800,128]{2,1,0:T(8,128)S(1)}, f32[12,3,128,128]{3,2,1,0:T(8,128)S(1)}, f32[12,128,128]{2,1,0:T(8,128)S(1)}, f32[8,128,128]{2,1,0:T(8,128)S(1)}) custom-call(s32[12]{0:T(128)S(1)} %copy-done.2, s32[12]{0:T(128)S(1)} %copy-done, f32[16]{0:T(128)S(1)} %copy-done.1, f32[16]{0:T(128)S(1)} %copy-done.3, ...), custom_call_target="tpu_custom_call", output_to_operand_aliasing={{0}: (4, {})} | custom-call | flops 1 | bytes 1 | tf_op jit(solution)/shard_map/border/pallas_call | solution.py:333
  39.9 1.3 %collective-permute-start.6 = (f32[8,128,128]{2,1,0:T(8,128)S(1)}, f32[8,128,128]{2,1,0:T(8,128)S(1)}, u32[]{:S(2)}, u32[]{:S(2)}) collective-permute-start(f32[8,128,128]{2,1,0:T(8,128)S(1)} %get-tuple-element.35), channel_id=1, source_target_pairs={{0,16},{1,17},{2,18},{3,19},{4,20},{5,21},{6,22},{7,23},{8,24},{9,... | collective-permute-start | bytes 1572872 | tf_op jit(solution)/shard_map/ppermute | solution.py:345
  41.2 0.9 %resume.3.refs_0_ = f32[12,64,128]{2,1,0:T(8,128)S(1)} custom-call(s32[12]{0:T(128)S(1)} %copy-done, f32[16]{0:T(128)S(1)} %copy-done.1, f32[12,3,64,128]{3,2,1,0:T(8,128)S(1)} %get-tuple-element.37.entry_ref, f32[8,64,128]{2,1,0:T(8,128)S(1)} %collective-permute-done.2.behind.incoming, ...), custom_call_target="tpu_custom_call", output_to_operand_aliasing={{}: (4, {})} | custom-call | flops 1 | bytes 1 | tf_op jit(solution)/shard_map/resume/pallas_call | solution.py:351
  42.0 1.3 %resume.4.refs_1_ = f32[12,160,128]{2,1,0:T(8,128)S(1)} custom-call(s32[12]{0:T(128)S(1)} %copy-done, f32[16]{0:T(128)S(1)} %copy-done.1, f32[12,3,160,128]{3,2,1,0:T(8,128)S(1)} %get-tuple-element.39.entry_ref, f32[8,160,128]{2,1,0:T(8,128)S(1)} %collective-permute-done.5.behind.incoming, ...), custom_call_target="tpu_custom_call", output_to_operand_aliasing={{}: (4, {})} | custom-call | flops 1 | bytes 1 | tf_op jit(solution)/shard_map/resume/pallas_call | solution.py:351
  43.4 9.6 %collective-permute-done.7.incoming = f32[8,160,128]{2,1,0:T(8,128)S(1)} collective-permute-done((f32[8,160,128]{2,1,0:T(8,128)S(1)}, f32[8,160,128]{2,1,0:T(8,128)S(1)}, u32[]{:S(2)}, u32[]{:S(2)}) %collective-permute-start.7) | collective-permute-done | bytes 655392 | tf_op jit(solution)/shard_map/ppermute | solution.py:345
  52.9 1.3 %resume.5.refs_2_ = f32[12,160,128]{2,1,0:T(8,128)S(1)} custom-call(s32[12]{0:T(128)S(1)} %copy-done, f32[16]{0:T(128)S(1)} %copy-done.1, f32[12,3,160,128]{3,2,1,0:T(8,128)S(1)} %get-tuple-element.41.entry_ref, f32[8,160,128]{2,1,0:T(8,128)S(1)} %collective-permute-done.7.incoming, ...), custom_call_target="tpu_custom_call", output_to_operand_aliasing={{}: (4, {})} | custom-call | flops 1 | bytes 1 | tf_op jit(solution)/shard_map/resume/pallas_call | solution.py:351
  54.3 8.4 %collective-permute-done.6.incoming = f32[8,128,128]{2,1,0:T(8,128)S(1)} collective-permute-done((f32[8,128,128]{2,1,0:T(8,128)S(1)}, f32[8,128,128]{2,1,0:T(8,128)S(1)}, u32[]{:S(2)}, u32[]{:S(2)}) %collective-permute-start.6) | collective-permute-done | bytes 524320 | tf_op jit(solution)/shard_map/ppermute | solution.py:345
  62.7 3.0 %last.1 = (f32[12,128,128]{2,1,0:T(8,128)S(1)}, f32[12,512,128]{2,1,0:T(8,128)}) custom-call(s32[12]{0:T(128)S(1)} %copy-done, f32[16]{0:T(128)S(1)} %copy-done.1, f32[12,3,128,128]{3,2,1,0:T(8,128)S(1)} %get-tuple-element.34.entry_ref, f32[8,128,128]{2,1,0:T(8,128)S(1)} %collective-permute-done.6.incoming, ...), custom_call_target="tpu_custom_call", output_to_operand_aliasing={{0}: (4, {})} | custom-call | flops 1 | bytes 1 | tf_op jit(solution)/shard_map/last/pallas_call | solution.py:364
Async XLA Ops:
  0.0 6.4 %copy-start.1 = (f32[16]{0:T(128)S(1)}, f32[16]{0:T(128)}, u32[]{:S(2)}) copy-start(f32[16]{0:T(128)} %near.13) | copy-start | bytes 196
  0.0 6.4 %copy-start = (s32[12]{0:T(128)S(1)}, s32[12]{0:T(128)}, u32[]{:S(2)}) copy-start(s32[12]{0:T(128)} %slots.13) | copy-start | bytes 148
  0.0 6.4 %copy-start.3 = (f32[16]{0:T(128)S(1)}, f32[16]{0:T(128)}, u32[]{:S(2)}) copy-start(f32[16]{0:T(128)} %lens.5) | copy-start | bytes 196
  0.0 6.4 %copy-start.2 = (s32[12]{0:T(128)S(1)}, s32[12]{0:T(128)}, u32[]{:S(2)}) copy-start(s32[12]{0:T(128)} %widths.5) | copy-start | bytes 148
  5.1 14.5 %collective-permute-start.2 = (f32[8,64,128]{2,1,0:T(8,128)S(1)}, f32[8,64,128]{2,1,0:T(8,128)S(1)}, u32[]{:S(2)}, u32[]{:S(2)}) collective-permute-start(f32[8,64,128]{2,1,0:T(8,128)S(1)} %get-tuple-element.29), channel_id=1, source_target_pairs={{0,16},{1,17},{2,18},{3,19},{4,20},{5,21},{6,22},{7,23},{8,24},{9,... | collective-permute-start | bytes 786440 | tf_op jit(solution)/shard_map/ppermute | solution.py:316
  10.8 25.1 %collective-permute-start.5 = (f32[8,160,128]{2,1,0:T(8,128)S(1)}, f32[8,160,128]{2,1,0:T(8,128)S(1)}, u32[]{:S(2)}, u32[]{:S(2)}) collective-permute-start(f32[8,160,128]{2,1,0:T(8,128)S(1)} %get-tuple-element.33), channel_id=1, source_target_pairs={{0,16},{1,17},{2,18},{3,19},{4,20},{5,21},{6,22},{7,23},{8,24},{9,... | collective-permute-start | bytes 1966088 | tf_op jit(solution)/shard_map/ppermute | solution.py:329
  12.1 15.4 %collective-permute-start = (f32[12,80,128]{2,1,0:T(8,128)S(1)}, f32[12,80,128]{2,1,0:T(8,128)S(1)}, u32[]{:S(2)}, u32[]{:S(2)}) collective-permute-start(f32[12,80,128]{2,1,0:T(8,128)S(1)} %get-tuple-element.27), channel_id=1, source_target_pairs={{0,1},{1,2},{2,3},{3,4},{4,5},{5,6},{6,7},{7,8},{8,9},{9,10},{10,1... | collective-permute-start | bytes 1474568 | tf_op jit(solution)/shard_map/ppermute | solution.py:331
  14.0 13.5 %collective-permute-start.1 = (f32[12,80,128]{2,1,0:T(8,128)S(1)}, f32[12,80,128]{2,1,0:T(8,128)S(1)}, u32[]{:S(2)}, u32[]{:S(2)}) collective-permute-start(f32[12,80,128]{2,1,0:T(8,128)S(1)} %get-tuple-element.28), channel_id=1, source_target_pairs={{1,0},{2,1},{3,2},{4,3},{5,4},{6,5},{7,6},{8,7},{9,8},{10,9},{11,1... | collective-permute-start | bytes 1474568 | tf_op jit(solution)/shard_map/ppermute | solution.py:332
  17.7 18.3 %collective-permute-start.3 = (f32[12,64,128]{2,1,0:T(8,128)S(1)}, f32[12,64,128]{2,1,0:T(8,128)S(1)}, u32[]{:S(2)}, u32[]{:S(2)}) collective-permute-start(f32[12,64,128]{2,1,0:T(8,128)S(1)} %get-tuple-element.31), channel_id=1, source_target_pairs={{0,1},{1,2},{2,3},{3,4},{4,5},{5,6},{6,7},{7,8},{8,9},{9,10},{10,1... | collective-permute-start | bytes 1179656 | tf_op jit(solution)/shard_map/ppermute | solution.py:331
  19.6 16.3 %collective-permute-start.4 = (f32[12,64,128]{2,1,0:T(8,128)S(1)}, f32[12,64,128]{2,1,0:T(8,128)S(1)}, u32[]{:S(2)}, u32[]{:S(2)}) collective-permute-start(f32[12,64,128]{2,1,0:T(8,128)S(1)} %get-tuple-element.32), channel_id=1, source_target_pairs={{1,0},{2,1},{3,2},{4,3},{5,4},{6,5},{7,6},{8,7},{9,8},{10,9},{11,1... | collective-permute-start | bytes 1179656 | tf_op jit(solution)/shard_map/ppermute | solution.py:332
  31.8 21.1 %collective-permute-start.7 = (f32[8,160,128]{2,1,0:T(8,128)S(1)}, f32[8,160,128]{2,1,0:T(8,128)S(1)}, u32[]{:S(2)}, u32[]{:S(2)}) collective-permute-start(f32[8,160,128]{2,1,0:T(8,128)S(1)} %get-tuple-element.42), channel_id=1, source_target_pairs={{0,16},{1,17},{2,18},{3,19},{4,20},{5,21},{6,22},{7,23},{8,24},{9,... | collective-permute-start | bytes 1966088 | tf_op jit(solution)/shard_map/ppermute | solution.py:345
  39.9 22.8 %collective-permute-start.6 = (f32[8,128,128]{2,1,0:T(8,128)S(1)}, f32[8,128,128]{2,1,0:T(8,128)S(1)}, u32[]{:S(2)}, u32[]{:S(2)}) collective-permute-start(f32[8,128,128]{2,1,0:T(8,128)S(1)} %get-tuple-element.35), channel_id=1, source_target_pairs={{0,16},{1,17},{2,18},{3,19},{4,20},{5,21},{6,22},{7,23},{8,24},{9,... | collective-permute-start | bytes 1572872 | tf_op jit(solution)/shard_map/ppermute | solution.py:345

commit v4 on v3

v4 whole, which is shorter than its diff:
```python
import functools

import jax
import jax.numpy as jnp
from jax import lax
from jax.experimental import pallas as pl
from jax.experimental.pallas import tpu as pltpu
from jax.sharding import PartitionSpec as P

WMAX = 8
RIM = WMAX + 1
LANES = 128
SUB = 8
WEIGHT = 100000000
TOGETHER = 4
PARTS = (3, 2, 2)
VMEM_LIMIT = 16 * 1024 * 1024
F32, BF16 = jnp.float32, jnp.bfloat16


def group_sizes(row_count):
    return (row_count - 2 * RIM, RIM, RIM)


def side_starts(row_count):
    low, high = (0, -RIM), (row_count - RIM, row_count)
    even = lax.rem(lax.axis_index("sky"), 2) == 0
    paired = [jnp.where(even, b, a) for a, b in zip(low, high)]
    other = [jnp.where(even, a, b) for a, b in zip(low, high)]
    return paired, other


def first_row(row_count, part):
    return RIM if part == 0 else side_starts(row_count)[part - 1][0]


def split(value, parts):
    found = []
    for part in range(parts):
        found.append(value.astype(BF16))
        if part + 1 < parts:
            value = value - found[-1].astype(F32)
    return found


def make_bands(planes, widths, band_ref):
    source = lax.broadcasted_iota(jnp.int32, (LANES, 2 * LANES), 0)
    target = lax.broadcasted_iota(jnp.int32, (LANES, 2 * LANES), 1)
    across = jnp.where(target >= LANES + LANES // 2, source + 2 * LANES, source)
    offset = across - target
    distance = jnp.abs(offset)

    def plane(k, carry):
        half_width = widths[k]
        rim = (distance == half_width + 1).astype(F32)
        edge = (distance == half_width).astype(F32)
        inside = (distance <= half_width).astype(F32)
        both = rim + edge
        for field, value in enumerate((rim - edge, jnp.where(offset > 0, both, -both), inside)):
            band_ref[k, field] = value.astype(BF16)
        return carry

    lax.fori_loop(0, planes, plane, 0)


def build(k, half_width, first, count, blocks, x_ref, left_ref):
    def row(index):
        return x_ref[k, pl.ds(pl.multiple_of(index * blocks, blocks), blocks), :]

    total = row(first)
    for step in range(1, WMAX + 1):
        total = total + jnp.where(step <= half_width, row(first - step) + row(first + step), 0.0)
    for i in range(count):
        high, low = first + i + half_width, first + i - half_width
        rim_high, edge_high, edge_low, rim_low = row(high + 1), row(high), row(low), row(low - 1)
        values = (total, (rim_high + edge_high) - (edge_low + rim_low),
                  (rim_high - edge_high) - (edge_low - rim_low))
        total = total + (rim_high - edge_low)
        here = slice(i * blocks, (i + 1) * blocks)
        for field, value in enumerate(values):
            for part, piece in enumerate(split(value, PARTS[field])):
                left_ref[field, here, part * LANES:(part + 1) * LANES] = piece


def multiply(k, field, band_ref, left_ref):
    weight = jnp.concatenate([band_ref[k, field]] * PARTS[field], axis=0)
    return jnp.dot(left_ref[field, :, :PARTS[field] * LANES], weight, preferred_element_type=F32)


def combine(k, field, near, scale, blocks, product, beside_ref, entry_ref):
    pitch = blocks + SUB
    count = product.shape[0] // blocks
    left_lane = lax.broadcasted_iota(jnp.int32, (blocks, LANES), 1) < LANES // 2
    factor = -0.25 * scale if field == 1 else -scale
    for at in range(count):
        beside_ref[field, pl.ds(at * pitch + SUB, blocks), :] = product[at * blocks:(at + 1) * blocks, LANES:]
    for at in range(count):
        beside = jnp.where(left_lane, beside_ref[field, pl.ds(at * pitch + SUB - 1, blocks), :],
                           beside_ref[field, pl.ds(at * pitch + SUB + 1, blocks), :])
        value = factor * (product[at * blocks:(at + 1) * blocks, :LANES] + beside)
        entry_ref[k, field, pl.ds(at * blocks, blocks), :] = value if field == 1 else value + near


def sweep(planes, length, near_of, entry_ref, conv_ref, start, finish):
    step = next(count * SUB for count in (4, 3, 2, 1) if length % (count * SUB) == 0)

    def part(index, carry):
        where = pl.ds(pl.multiple_of(index * step, step), step)
        state = start(where, (step, LANES))
        now, then = state[:4], state[4:]
        for k in range(planes):
            xx, xy, yy = [entry_ref[k, i, where, :] for i in range(3)]
            kept = 1.0 - near_of(k)
            new = [
                xx * now[0] + xy * now[2] + kept * then[0],
                xx * now[1] + xy * now[3] + kept * then[1],
                xy * now[0] + yy * now[2] + kept * then[2],
                xy * now[1] + yy * now[3] + kept * then[3],
            ]
            now, then = new, now
            conv_ref[k, where, :] = 1.0 - 0.5 * (new[0] + new[3])
        finish(where, now + then)
        return carry

    lax.fori_loop(0, length // step, part, 0)


def identity_state(where, shape):
    one, zero = jnp.ones(shape, F32), jnp.zeros(shape, F32)
    return [one, zero, zero, one] * 2


def writer(state_ref):
    def finish(where, state):
        for i, value in enumerate(state):
            state_ref[i, where, :] = value

    return finish


def group_stage(sizes, part, scalars, x_ref, band_ref, left_refs, beside_refs, entry_ref, conv_ref, state_ref,
                before_plane=lambda k: None):
    planes, rows, blocks = sizes
    widths, slots, near, lens = scalars
    first, count = first_row(rows, part) + RIM, group_sizes(rows)[part]
    together = len(left_refs)
    for beside_ref in beside_refs:
        beside_ref[...] = jnp.zeros(beside_ref.shape, F32)

    def step(index, carry):
        ks = [index * together + i for i in range(together)]
        for k in ks:
            before_plane(k)
        for k, left_ref in zip(ks, left_refs):
            build(k, widths[k], first, count, blocks, x_ref, left_ref)
        for field in range(3):
            for k, left_ref, beside_ref in zip(ks, left_refs, beside_refs):
                width = (2 * widths[k] + 1).astype(F32)
                combine(k, field, near[slots[k]], lens[slots[k]] / (width * width), blocks,
                        multiply(k, field, band_ref, left_ref), beside_ref, entry_ref)
        return carry

    lax.fori_loop(0, planes // together, step, 0)

    @pl.when(lax.axis_index("depth") == 0)
    def _():
        sweep(planes, group_sizes(rows)[part] * blocks, lambda k: near[slots[k]], entry_ref, conv_ref, identity_state,
              writer(state_ref))


def first_kernel(sizes, widths_hbm, slots_hbm, near_hbm, lens_hbm, potential_hbm, x_ref, band_ref, entry_ref, conv_ref,
                 state_ref, paired_ref, other_ref, *scratch):
    planes, rows, blocks = sizes
    scratch, (tiles_ref, widths, slots, near, lens, plane_sems, table_sems) = scratch[:-7], scratch[-7:]
    tables = ((widths_hbm, widths), (slots_hbm, slots), (near_hbm, near), (lens_hbm, lens))
    copies = [pltpu.make_async_copy(*pair, table_sems.at[i]) for i, pair in enumerate(tables)]
    for copy in copies:
        copy.start()

    def plane_copy(k):
        return pltpu.make_async_copy(potential_hbm.at[k], tiles_ref.at[k], plane_sems.at[k])

    for k in range(planes):
        plane_copy(k).start()
    for copy in copies:
        copy.wait()
    make_bands(planes, widths, band_ref)
    sides = [(start + RIM) * blocks for start, _ in side_starts(rows)]

    def arrive(k):
        plane_copy(k).wait()
        for row in range(rows):
            for half in range(blocks // SUB):
                start = (row // SUB) * SUB * blocks + half * SUB * SUB + row % SUB
                x_ref[k, pl.ds((row + RIM) * blocks + half * SUB, SUB), :] = tiles_ref[
                    k, pl.ds(start, SUB, stride=SUB), :]
        for ref, side in zip((paired_ref, other_ref), sides):
            ref[k] = x_ref[k, pl.ds(pl.multiple_of(side, blocks), RIM * blocks), :]

    group_stage(sizes, 0, (widths, slots, near, lens), x_ref, band_ref, scratch[::2], scratch[1::2], entry_ref, conv_ref,
                state_ref, arrive)


def border_kernel(sizes, part, widths, slots, near, lens, x_in, band_ref, rows_in, *refs):
    planes, rows, blocks = sizes
    x_ref, entry_ref, conv_ref, state_ref, *scratch = refs[part - 1:]
    start = side_starts(rows)[part - 1][1] + RIM

    def arrive(k):
        x_ref[k, pl.ds(pl.multiple_of(start * blocks, blocks), RIM * blocks), :] = rows_in[k]

    group_stage(sizes, part, (widths, slots, near, lens), x_ref, band_ref, scratch[::2], scratch[1::2], entry_ref,
                conv_ref, state_ref, arrive)


def resume(sizes, part, turn, slots, near, entry_ref, incoming, conv_ref, finish):
    planes, rows, blocks = sizes

    @pl.when(lax.axis_index("depth") == turn)
    def _():
        sweep(planes, group_sizes(rows)[part] * blocks, lambda k: near[slots[k]], entry_ref, conv_ref,
              lambda where, shape: [incoming[i, where, :] for i in range(8)], finish)


def resume_kernel(sizes, part, turn, slots, near, entry_ref, incoming, conv_in, conv_ref, *state_ref):
    finish = writer(state_ref[0]) if state_ref else lambda where, state: None
    resume(sizes, part, turn, slots, near, entry_ref, incoming, conv_ref, finish)


def last_kernel(sizes, turn, slots, near, entry_ref, incoming, conv_in, *refs):
    planes, rows, blocks = sizes
    others, (conv_ref, out_hbm, tiles_ref, sems) = refs[:-4], refs[-4:]
    part = len(others)
    resume(sizes, part, turn, slots, near, entry_ref, incoming, conv_ref, lambda where, state: None)

    def plane_copy(k):
        return pltpu.make_async_copy(tiles_ref.at[k], out_hbm.at[k], sems.at[k])

    def plane(k, carry):
        for part, ref in enumerate((*others, conv_ref)):
            start = first_row(rows, part)
            for i in range(group_sizes(rows)[part]):
                row = start + i
                for half in range(blocks // SUB):
                    to = (row // SUB) * SUB * blocks + half * SUB * SUB + row % SUB
                    tiles_ref[k, pl.ds(to, SUB, stride=SUB), :] = ref[k, pl.ds(i * blocks + half * SUB, SUB), :]
        plane_copy(k).start()
        return carry

    lax.fori_loop(0, planes, plane, 0)
    for k in range(planes):
        plane_copy(k).wait()


def per_device(potential, widths, plane_slot, ratio_near, ratio_lens):
    planes, rows, cols = potential.shape
    blocks = cols // LANES
    sizes = (planes, rows, blocks)
    parts = len(group_sizes(rows))
    together = next(count for count in range(TOGETHER, 0, -1) if planes % count == 0)
    depth_count, sky_count = lax.axis_size("depth"), lax.axis_size("sky")
    swaps = [[pair for i in range(first, sky_count - 1, 2) for pair in ((i, i + 1), (i + 1, i))] for first in (0, 1)]
    ahead = [(i, i + 1) for i in range(depth_count - 1)]
    tiled = potential.reshape(planes, rows // SUB, SUB, blocks, LANES).transpose(0, 1, 3, 2, 4)
    tiled = tiled.reshape(planes, rows * blocks, LANES)
    smem = pl.BlockSpec(memory_space=pltpu.SMEM)
    vmem = pl.BlockSpec(memory_space=pltpu.VMEM)
    anywhere = pl.BlockSpec(memory_space=pl.ANY)
    params = pltpu.CompilerParams(vmem_limit_bytes=VMEM_LIMIT)
    scalars = (widths, plane_slot, ratio_near, ratio_lens)
    dma = pltpu.SemaphoreType.DMA
    cost = pl.CostEstimate(flops=1, transcendentals=0, bytes_accessed=1)

    def held(*shape, dtype=F32):
        return pltpu.VMEM(shape, dtype)

    def moved(*shape):
        return jax.ShapeDtypeStruct(shape, F32)

    def in_vmem(array):
        return pltpu.with_memory_space_constraint(array, pltpu.VMEM)

    def in_hbm(array):
        return pltpu.with_memory_space_constraint(array, pltpu.HBM)

    x_shape = held(planes, (rows + 2 * RIM) * blocks, LANES)
    band_shape = held(planes, 3, LANES, 2 * LANES, dtype=BF16)

    def group_shapes(part):
        length = group_sizes(rows)[part] * blocks
        return [held(planes, 3, length, LANES), held(planes, length, LANES), moved(8, length, LANES)]

    def group_scratch(part):
        count = group_sizes(rows)[part]
        return [held(3, count * blocks, max(PARTS) * LANES, dtype=BF16),
                held(3, (count + 1) * (blocks + SUB), LANES)] * together

    side = moved(planes, RIM * blocks, LANES)
    x, bands, *group, paired, other = pl.pallas_call(
        functools.partial(first_kernel, sizes),
        out_shape=[x_shape, band_shape, *group_shapes(0), side, side],
        in_specs=[anywhere] * 5,
        out_specs=[vmem] * 7,
        scratch_shapes=[
            *group_scratch(0), held(planes, rows * blocks, LANES),
            *[pltpu.SMEM(array.shape, array.dtype) for array in scalars], dma((planes,)), dma((len(scalars),))],
        compiler_params=params,
        cost_estimate=cost,
        name="first",
    )(*[in_hbm(array) for array in (*scalars, tiled)])
    made = [group]
    arriving = [lax.ppermute(group[2], "depth", ahead)]
    swapped = [lax.ppermute(paired, "sky", swaps[0]), lax.ppermute(other, "sky", swaps[1])]
    entries, convs = [group[0] for group in made], [group[1] for group in made]

    def resumed(part, turn):
        last = turn == depth_count - 1
        convs[part], *state = pl.pallas_call(
            functools.partial(resume_kernel, sizes, part, turn),
            out_shape=group_shapes(part)[1:2] + ([] if last else group_shapes(part)[2:3]),
            in_specs=[smem] * 2 + [vmem] * 3,
            out_specs=[vmem] * (1 if last else 2),
            input_output_aliases={4: 0},
            compiler_params=params,
            cost_estimate=cost,
            name="resume",
        )(plane_slot, ratio_near, in_vmem(entries[part]), arriving[part], in_vmem(convs[part]))
        if state:
            arriving[part] = lax.ppermute(state[0], "depth", ahead)

    for part in range(1, parts):
        x, *group = pl.pallas_call(
            functools.partial(border_kernel, sizes, part),
            out_shape=[x_shape, *group_shapes(part)],
            in_specs=[smem] * 4 + [vmem] * 3 + [anywhere] * (part - 1),
            out_specs=[vmem] * 4,
            scratch_shapes=group_scratch(part),
            input_output_aliases={4: 0},
            compiler_params=params,
            cost_estimate=cost,
            name="border",
        )(*scalars, in_vmem(x), in_vmem(bands), swapped[part - 1], *arriving[:part - 1])
        entries.append(group[0])
        convs.append(group[1])
        arriving.append(lax.ppermute(group[2], "depth", ahead))
    for turn in range(1, depth_count):
        for part in range(parts - (turn == depth_count - 1)):
            resumed(part, turn)

    conv, out = pl.pallas_call(
        functools.partial(last_kernel, sizes, depth_count - 1),
        out_shape=[group_shapes(parts - 1)[1], moved(planes, rows * blocks, LANES)],
        in_specs=[smem] * 2 + [vmem] * (3 + parts - 1),
        out_specs=[vmem, anywhere],
        scratch_shapes=[held(planes, rows * blocks, LANES), dma((planes,))],
        input_output_aliases={4: 0},
        compiler_params=params,
        cost_estimate=cost,
        name="last",
    )(plane_slot, ratio_near, in_vmem(entries[-1]), arriving[-1], in_vmem(convs[-1]),
      *[in_vmem(conv) for conv in convs[:-1]])
    out = out.reshape(planes, rows // SUB, blocks, SUB, LANES).transpose(0, 1, 3, 2, 4)
    return out.reshape(planes, rows, cols)


def solution(mesh):
    return jax.shard_map(
        per_device,
        mesh=mesh,
        in_specs=(P("depth", "sky", None), P("depth"), P("depth"), P(), P()),
        out_specs=P("depth", "sky", None),
        check_vma=False,
    )
```

time: 65.9 us -> 58.2 us (0.88)
  starting transfers between devices: 16.3 us -> 6.45 us
  waiting for transfers between devices: 25.1 us -> 34.1 us
  Pallas kernels: 24.1 us -> 17.2 us
    ppermute x4 -> x2, waiting for transfers between devices: 7.05 us -> 17.1 us  [the longest x1 17.1 us: per_device(): lax.ppermute(other, 'sky', swaps[1])]
    ppermute x4 -> x2, starting transfers between devices: 11.1 us -> 2.57 us  [the longest x1 2.5 us: per_device(): lax.ppermute(other, 'sky', swaps[1])]
    pallas_call x4 -> x2, Pallas kernels: 7.86 us -> 2.88 us  [resumed(): pl.pallas_call(functools.partial(resume_kernel, sizes, part, turn), out_s...]
    pallas_call x2, Pallas kernels: 8.23 us -> 5.68 us  [per_device(): pl.pallas_call(functools.partial(border_kernel, sizes, part), out_shape=[...]
    ppermute x3 -> x2, starting transfers between devices: 3.88 us -> 2.58 us  [per_device(): arriving.append(lax.ppermute(group[2], 'depth', ahead))]
    ppermute x3 -> x2, waiting for transfers between devices: 18 us -> 17 us  [per_device(): arriving.append(lax.ppermute(group[2], 'depth', ahead))]
  transfers between devices with their start and end apart: 8 -> 5, of which waited for: 4 -> 3; matrix products, arithmetic and copies ran while one was open for 0% -> 0% of each run, Pallas kernels for 24% -> 15%
where the time goes in v4:
time: 58.2 us; the launch traced here: 58 us
  waiting for transfers between devices  34.1 us (59%)
  Pallas kernels  17.2 us (30%)
  starting transfers between devices  6.45 us (11%)
    ppermute x1, waiting for transfers between devices, per_device(): lax.ppermute(other, 'sky', swaps[1])  17.1 us
    ppermute x2, waiting for transfers between devices, per_device(): arriving.append(lax.ppermute(group[2], 'depth', ahead))  17 us
    pallas_call x2, Pallas kernels, per_device(): pl.pallas_call(functools.partial(border_kernel, sizes, part), out_shape=[...  5.68 us
    pallas_call x1, Pallas kernels, per_device(): pl.pallas_call(functools.partial(first_kernel, sizes), out_shape=[x_shape...  5.61 us
    pallas_call x1, Pallas kernels, per_device(): pl.pallas_call(functools.partial(last_kernel, sizes, depth_count - 1), ou...  3.08 us
    pallas_call x2, Pallas kernels, resumed(): pl.pallas_call(functools.partial(resume_kernel, sizes, part, turn), out_s...  2.88 us
    ppermute x2, starting transfers between devices, per_device(): arriving.append(lax.ppermute(group[2], 'depth', ahead))  2.58 us
    ppermute x1, starting transfers between devices, per_device(): lax.ppermute(other, 'sky', swaps[1])  2.5 us
  transfers between devices with their start and end apart: 5, of which 3 were waited for; matrix products, arithmetic and copies ran while one was open for 0% of the time, Pallas kernels for 15%

profile of v4, /device:TPU:6, one launch (start us, length us, event | category | flops | bytes accessed | tf_op | source)
XLA Modules:
  0.0 58.0 jit_solution(1485730121479709152)
XLA Ops:
  0.0 0.0 copy-start.1
  0.0 0.0 copy-start
  0.0 0.0 copy-start.3
  0.0 0.0 copy-start.2
  0.0 5.6 %first.1 = (f32[12,800,128]{2,1,0:T(8,128)S(1)}, bf16[12,3,128,256]{3,2,1,0:T(8,128)(2,1)S(1)}, f32[12,3,224,128]{3,2,1,0:T(8,128)S(1)}, f32[12,224,128]{2,1,0:T...) custom-call(s32[12]{0:T(128)} %widths.3, s32[12]{0:T(128)} %slots.9, ...), custom_call_target="tpu_custom_call" | custom-call | flops 1 | bytes 1 | tf_op jit(solution)/shard_map/first/pallas_call | solution.py:299
  5.6 1.3 %collective-permute-start.2 = (f32[8,224,128]{2,1,0:T(8,128)S(1)}, f32[8,224,128]{2,1,0:T(8,128)S(1)}, u32[]{:S(2)}, u32[]{:S(2)}) collective-permute-start(f32[8,224,128]{2,1,0:T(8,128)S(1)} %get-tuple-element.25), channel_id=1, source_target_pairs={{0,16},{1,17},{2,18},{3,19},{4,20},{5,21},{6,22},{7,23},{8,24},{9,... | collective-permute-start | bytes 2752520 | tf_op jit(solution)/shard_map/ppermute | solution.py:312
  6.9 0.1 collective-permute-start
  7.0 2.5 %collective-permute-start.1 = (f32[12,144,128]{2,1,0:T(8,128)S(1)}, f32[12,144,128]{2,1,0:T(8,128)S(1)}, u32[]{:S(2)}, u32[]{:S(2)}) collective-permute-start(f32[12,144,128]{2,1,0:T(8,128)S(1)} %get-tuple-element.24), channel_id=1, source_target_pairs={{1,2},{2,1},{3,4},{4,3},{5,6},{6,5},{7,8},{8,7},{9,10},{10,9},{11,... | collective-permute-start | bytes 2654216 | tf_op jit(solution)/shard_map/ppermute | solution.py:313
  9.5 0.0 collective-permute-done.rows_in
  9.5 0.0 copy-done.1
  9.5 0.0 copy-done
  9.6 0.0 copy-done.3
  9.6 0.0 copy-done.2
  9.6 2.8 %border.2 = (f32[12,800,128]{2,1,0:T(8,128)S(1)}, f32[12,3,144,128]{3,2,1,0:T(8,128)S(1)}, f32[12,144,128]{2,1,0:T(8,128)S(1)}, f32[8,144,128]{2,1,0:T(8,128)S(1)}) custom-call(s32[12]{0:T(128)S(1)} %copy-done.2, s32[12]{0:T(128)S(1)} %copy-done, f32[16]{0:T(128)S(1)} %copy-done.1, f32[16]{0:T(128)S(1)} %copy-done.3, ...), custom_call_target="tpu_custom_call", output_to_operand_aliasing={{0}: (4, {})} | custom-call | flops 1 | bytes 1 | tf_op jit(solution)/shard_map/border/pallas_call | solution.py:332
  12.4 1.3 %collective-permute-start.4 = (f32[8,144,128]{2,1,0:T(8,128)S(1)}, f32[8,144,128]{2,1,0:T(8,128)S(1)}, u32[]{:S(2)}, u32[]{:S(2)}) collective-permute-start(f32[8,144,128]{2,1,0:T(8,128)S(1)} %get-tuple-element.32), channel_id=1, source_target_pairs={{0,16},{1,17},{2,18},{3,19},{4,20},{5,21},{6,22},{7,23},{8,24},{9,... | collective-permute-start | bytes 1769480 | tf_op jit(solution)/shard_map/ppermute | solution.py:345
  13.7 17.1 %collective-permute-done.1.rows_in = f32[12,144,128]{2,1,0:T(8,128)S(1)} collective-permute-done((f32[12,144,128]{2,1,0:T(8,128)S(1)}, f32[12,144,128]{2,1,0:T(8,128)S(1)}, u32[]{:S(2)}, u32[]{:S(2)}) %collective-permute-start.1) | collective-permute-done | bytes 884768 | tf_op jit(solution)/shard_map/ppermute | solution.py:313
  30.9 0.0 collective-permute-done.2.refs_0_.incoming
  30.9 2.8 %border.3 = (f32[12,800,128]{2,1,0:T(8,128)S(1)}, f32[12,3,144,128]{3,2,1,0:T(8,128)S(1)}, f32[12,144,128]{2,1,0:T(8,128)S(1)}, f32[8,144,128]{2,1,0:T(8,128)S(1)}) custom-call(s32[12]{0:T(128)S(1)} %copy-done.2, s32[12]{0:T(128)S(1)} %copy-done, f32[16]{0:T(128)S(1)} %copy-done.1, f32[16]{0:T(128)S(1)} %copy-done.3, ...), custom_call_target="tpu_custom_call", output_to_operand_aliasing={{0}: (4, {})} | custom-call | flops 1 | bytes 1 | tf_op jit(solution)/shard_map/border/pallas_call | solution.py:332
  33.7 1.3 %collective-permute-start.3 = (f32[8,144,128]{2,1,0:T(8,128)S(1)}, f32[8,144,128]{2,1,0:T(8,128)S(1)}, u32[]{:S(2)}, u32[]{:S(2)}) collective-permute-start(f32[8,144,128]{2,1,0:T(8,128)S(1)} %get-tuple-element.27), channel_id=1, source_target_pairs={{0,16},{1,17},{2,18},{3,19},{4,20},{5,21},{6,22},{7,23},{8,24},{9,... | collective-permute-start | bytes 1769480 | tf_op jit(solution)/shard_map/ppermute | solution.py:345
  35.0 1.6 %resume.2.refs_0_ = f32[12,224,128]{2,1,0:T(8,128)S(1)} custom-call(s32[12]{0:T(128)S(1)} %copy-done, f32[16]{0:T(128)S(1)} %copy-done.1, f32[12,3,224,128]{3,2,1,0:T(8,128)S(1)} %get-tuple-element.29.entry_ref, f32[8,224,128]{2,1,0:T(8,128)S(1)} %collective-permute-done.2.refs_0_.incoming, ...), custom_call_target="tpu_custom_call", output_to_operand_aliasing={{}: (4, {})} | custom-call | flops 1 | bytes 1 | tf_op jit(solution)/shard_map/resume/pallas_call | solution.py:318
  36.6 6.8 %collective-permute-done.4.incoming = f32[8,144,128]{2,1,0:T(8,128)S(1)} collective-permute-done((f32[8,144,128]{2,1,0:T(8,128)S(1)}, f32[8,144,128]{2,1,0:T(8,128)S(1)}, u32[]{:S(2)}, u32[]{:S(2)}) %collective-permute-start.4) | collective-permute-done | bytes 589856 | tf_op jit(solution)/shard_map/ppermute | solution.py:345
  43.4 1.3 %resume.3.refs_1_ = f32[12,144,128]{2,1,0:T(8,128)S(1)} custom-call(s32[12]{0:T(128)S(1)} %copy-done, f32[16]{0:T(128)S(1)} %copy-done.1, f32[12,3,144,128]{3,2,1,0:T(8,128)S(1)} %get-tuple-element.31.entry_ref, f32[8,144,128]{2,1,0:T(8,128)S(1)} %collective-permute-done.4.incoming, ...), custom_call_target="tpu_custom_call", output_to_operand_aliasing={{}: (4, {})} | custom-call | flops 1 | bytes 1 | tf_op jit(solution)/shard_map/resume/pallas_call | solution.py:318
  44.7 10.2 %collective-permute-done.3.incoming = f32[8,144,128]{2,1,0:T(8,128)S(1)} collective-permute-done((f32[8,144,128]{2,1,0:T(8,128)S(1)}, f32[8,144,128]{2,1,0:T(8,128)S(1)}, u32[]{:S(2)}, u32[]{:S(2)}) %collective-permute-start.3) | collective-permute-done | bytes 589856 | tf_op jit(solution)/shard_map/ppermute | solution.py:345
  54.9 3.1 %last.1 = (f32[12,144,128]{2,1,0:T(8,128)S(1)}, f32[12,512,128]{2,1,0:T(8,128)}) custom-call(s32[12]{0:T(128)S(1)} %copy-done, f32[16]{0:T(128)S(1)} %copy-done.1, f32[12,3,144,128]{3,2,1,0:T(8,128)S(1)} %get-tuple-element.26.entry_ref, f32[8,144,128]{2,1,0:T(8,128)S(1)} %collective-permute-done.3.incoming, ...), custom_call_target="tpu_custom_call", output_to_operand_aliasing={{0}: (4, {})} | custom-call | flops 1 | bytes 1 | tf_op jit(solution)/shard_map/last/pallas_call | solution.py:350
Async XLA Ops:
  0.0 9.5 %copy-start.1 = (f32[16]{0:T(128)S(1)}, f32[16]{0:T(128)}, u32[]{:S(2)}) copy-start(f32[16]{0:T(128)} %near.9) | copy-start | bytes 196
  0.0 9.5 %copy-start = (s32[12]{0:T(128)S(1)}, s32[12]{0:T(128)}, u32[]{:S(2)}) copy-start(s32[12]{0:T(128)} %slots.9) | copy-start | bytes 148
  0.0 9.6 %copy-start.3 = (f32[16]{0:T(128)S(1)}, f32[16]{0:T(128)}, u32[]{:S(2)}) copy-start(f32[16]{0:T(128)} %lens.3) | copy-start | bytes 196
  0.0 9.6 %copy-start.2 = (s32[12]{0:T(128)S(1)}, s32[12]{0:T(128)}, u32[]{:S(2)}) copy-start(s32[12]{0:T(128)} %widths.3) | copy-start | bytes 148
  5.6 25.2 %collective-permute-start.2 = (f32[8,224,128]{2,1,0:T(8,128)S(1)}, f32[8,224,128]{2,1,0:T(8,128)S(1)}, u32[]{:S(2)}, u32[]{:S(2)}) collective-permute-start(f32[8,224,128]{2,1,0:T(8,128)S(1)} %get-tuple-element.25), channel_id=1, source_target_pairs={{0,16},{1,17},{2,18},{3,19},{4,20},{5,21},{6,22},{7,23},{8,24},{9,... | collective-permute-start | bytes 2752520 | tf_op jit(solution)/shard_map/ppermute | solution.py:312
  6.9 2.6 %collective-permute-start = (f32[12,144,128]{2,1,0:T(8,128)S(1)}, f32[12,144,128]{2,1,0:T(8,128)S(1)}, u32[]{:S(2)}, u32[]{:S(2)}) collective-permute-start(f32[12,144,128]{2,1,0:T(8,128)S(1)} %get-tuple-element.22), channel_id=1, source_target_pairs={{0,1},{1,0},{2,3},{3,2},{4,5},{5,4},{6,7},{7,6},{8,9},{9,8},{10,11... | collective-permute-start | bytes 2654216 | tf_op jit(solution)/shard_map/ppermute | solution.py:313
  7.0 23.8 %collective-permute-start.1 = (f32[12,144,128]{2,1,0:T(8,128)S(1)}, f32[12,144,128]{2,1,0:T(8,128)S(1)}, u32[]{:S(2)}, u32[]{:S(2)}) collective-permute-start(f32[12,144,128]{2,1,0:T(8,128)S(1)} %get-tuple-element.24), channel_id=1, source_target_pairs={{1,2},{2,1},{3,4},{4,3},{5,6},{6,5},{7,8},{8,7},{9,10},{10,9},{11,... | collective-permute-start | bytes 2654216 | tf_op jit(solution)/shard_map/ppermute | solution.py:313
  12.4 31.0 %collective-permute-start.4 = (f32[8,144,128]{2,1,0:T(8,128)S(1)}, f32[8,144,128]{2,1,0:T(8,128)S(1)}, u32[]{:S(2)}, u32[]{:S(2)}) collective-permute-start(f32[8,144,128]{2,1,0:T(8,128)S(1)} %get-tuple-element.32), channel_id=1, source_target_pairs={{0,16},{1,17},{2,18},{3,19},{4,20},{5,21},{6,22},{7,23},{8,24},{9,... | collective-permute-start | bytes 1769480 | tf_op jit(solution)/shard_map/ppermute | solution.py:345
  33.7 21.2 %collective-permute-start.3 = (f32[8,144,128]{2,1,0:T(8,128)S(1)}, f32[8,144,128]{2,1,0:T(8,128)S(1)}, u32[]{:S(2)}, u32[]{:S(2)}) collective-permute-start(f32[8,144,128]{2,1,0:T(8,128)S(1)} %get-tuple-element.27), channel_id=1, source_target_pairs={{0,16},{1,17},{2,18},{3,19},{4,20},{5,21},{6,22},{7,23},{8,24},{9,... | collective-permute-start | bytes 1769480 | tf_op jit(solution)/shard_map/ppermute | solution.py:345

commit v5 on v4

--- a/solution.py
+++ b/solution.py
@@ -11,9 +11,11 @@
 RIM = WMAX + 1
 LANES = 128
 SUB = 8
-WEIGHT = 100000000
 TOGETHER = 4
 PARTS = (3, 2, 2)
+SHARES = 2
+SENT = 7
+TINY, POLE, FAR = 1e-30, 1e-20, 1e10
 VMEM_LIMIT = 16 * 1024 * 1024
 F32, BF16 = jnp.float32, jnp.bfloat16
 
@@ -125,6 +127,37 @@
     lax.fori_loop(0, length // step, part, 0)
 
 
+def packed_state(state):
+    a00, a01, a10, a11, b00, b01, b10, b11 = state
+    p = [a00 + b01, a10 + b11, a01 - b00, a11 - b10]
+    q = [a00 - b01, a10 - b11, a01 + b00, a11 + b10]
+    most = jnp.maximum(jnp.maximum(jnp.abs(q[0]), jnp.abs(q[1])), jnp.maximum(jnp.abs(q[2]), jnp.abs(q[3])))
+    scale = 1.0 / jnp.maximum(most, TINY)
+    q = [value * scale for value in q]
+    side = q[0] * q[0] + q[1] * q[1] + q[2] * q[2]
+    reach = jnp.sqrt(side + q[3] * q[3]) + jnp.abs(q[3])
+    ahead = q[3] >= 0.0
+    factor = jnp.where(ahead, 1.0, reach) / jnp.where(ahead, jnp.maximum(reach, TINY), jnp.maximum(side, POLE))
+    at_pole = jnp.logical_and(jnp.logical_not(ahead), side < POLE)
+    u = [value * factor for value in q[:3]]
+    return p + [jnp.where(at_pole, FAR, u[0]), u[1], u[2]]
+
+
+def unpacked_state(values):
+    p, u = values[:4], values[4:]
+    most = jnp.maximum(jnp.maximum(jnp.abs(p[0]), jnp.abs(p[1])), jnp.maximum(jnp.abs(p[2]), jnp.abs(p[3])))
+    bound = jnp.maximum(most, TINY)
+    scale = 1.0 / bound
+    unit = [value * scale for value in p]
+    norm = bound * jnp.sqrt((unit[0] * unit[0] + unit[1] * unit[1]) + (unit[2] * unit[2] + unit[3] * unit[3]))
+    square = u[0] * u[0] + u[1] * u[1] + u[2] * u[2]
+    share = 1.0 / (1.0 + square)
+    q = [norm * (2.0 * share * value) for value in u] + [norm * ((1.0 - square) * share)]
+    half = lambda a, b: 0.5 * (a + b)
+    return [half(p[0], q[0]), half(p[2], q[2]), half(p[1], q[1]), half(p[3], q[3]),
+            half(q[2], -p[2]), half(p[0], -q[0]), half(q[3], -p[3]), half(p[1], -q[1])]
+
+
 def identity_state(where, shape):
     one, zero = jnp.ones(shape, F32), jnp.zeros(shape, F32)
     return [one, zero, zero, one] * 2
@@ -132,7 +165,7 @@
 
 def writer(state_ref):
     def finish(where, state):
-        for i, value in enumerate(state):
+        for i, value in enumerate(packed_state(state)):
             state_ref[i, where, :] = value
 
     return finish
@@ -169,9 +202,11 @@
 
 
 def first_kernel(sizes, widths_hbm, slots_hbm, near_hbm, lens_hbm, potential_hbm, x_ref, band_ref, entry_ref, conv_ref,
-                 state_ref, paired_ref, other_ref, *scratch):
+                 state_ref, *refs):
     planes, rows, blocks = sizes
+    sends, scratch = refs[:2 * SHARES], refs[2 * SHARES:]
     scratch, (tiles_ref, widths, slots, near, lens, plane_sems, table_sems) = scratch[:-7], scratch[-7:]
+    share = planes // SHARES
     tables = ((widths_hbm, widths), (slots_hbm, slots), (near_hbm, near), (lens_hbm, lens))
     copies = [pltpu.make_async_copy(*pair, table_sems.at[i]) for i, pair in enumerate(tables)]
     for copy in copies:
@@ -194,20 +229,31 @@
                 start = (row // SUB) * SUB * blocks + half * SUB * SUB + row % SUB
                 x_ref[k, pl.ds((row + RIM) * blocks + half * SUB, SUB), :] = tiles_ref[
                     k, pl.ds(start, SUB, stride=SUB), :]
-        for ref, side in zip((paired_ref, other_ref), sides):
-            ref[k] = x_ref[k, pl.ds(pl.multiple_of(side, blocks), RIM * blocks), :]
+        for i, side in enumerate(sides):
+            rows_out = x_ref[k, pl.ds(pl.multiple_of(side, blocks), RIM * blocks), :]
+            for piece in range(SHARES):
+
+                @pl.when(lax.div(k, share) == piece)
+                def _(ref=sends[i * SHARES + piece]):
+                    ref[lax.rem(k, share)] = rows_out
 
     group_stage(sizes, 0, (widths, slots, near, lens), x_ref, band_ref, scratch[::2], scratch[1::2], entry_ref, conv_ref,
                 state_ref, arrive)
 
 
-def border_kernel(sizes, part, widths, slots, near, lens, x_in, band_ref, rows_in, *refs):
+def border_kernel(sizes, part, widths, slots, near, lens, x_in, band_ref, *refs):
     planes, rows, blocks = sizes
+    arrived, refs = refs[:SHARES], refs[SHARES:]
+    share = planes // SHARES
     x_ref, entry_ref, conv_ref, state_ref, *scratch = refs[part - 1:]
     start = side_starts(rows)[part - 1][1] + RIM
 
     def arrive(k):
-        x_ref[k, pl.ds(pl.multiple_of(start * blocks, blocks), RIM * blocks), :] = rows_in[k]
+        for piece, ref in enumerate(arrived):
+
+            @pl.when(lax.div(k, share) == piece)
+            def _(ref=ref):
+                x_ref[k, pl.ds(pl.multiple_of(start * blocks, blocks), RIM * blocks), :] = ref[lax.rem(k, share)]
 
     group_stage(sizes, part, (widths, slots, near, lens), x_ref, band_ref, scratch[::2], scratch[1::2], entry_ref,
                 conv_ref, state_ref, arrive)
@@ -219,7 +265,7 @@
     @pl.when(lax.axis_index("depth") == turn)
     def _():
         sweep(planes, group_sizes(rows)[part] * blocks, lambda k: near[slots[k]], entry_ref, conv_ref,
-              lambda where, shape: [incoming[i, where, :] for i in range(8)], finish)
+              lambda where, shape: unpacked_state([incoming[i, where, :] for i in range(SENT)]), finish)
 
 
 def resume_kernel(sizes, part, turn, slots, near, entry_ref, incoming, conv_in, conv_ref, *state_ref):
@@ -288,19 +334,19 @@
 
     def group_shapes(part):
         length = group_sizes(rows)[part] * blocks
-        return [held(planes, 3, length, LANES), held(planes, length, LANES), moved(8, length, LANES)]
+        return [held(planes, 3, length, LANES), held(planes, length, LANES), moved(SENT, length, LANES)]
 
     def group_scratch(part):
         count = group_sizes(rows)[part]
         return [held(3, count * blocks, max(PARTS) * LANES, dtype=BF16),
                 held(3, (count + 1) * (blocks + SUB), LANES)] * together
 
-    side = moved(planes, RIM * blocks, LANES)
-    x, bands, *group, paired, other = pl.pallas_call(
+    side = moved(planes // SHARES, RIM * blocks, LANES)
+    x, bands, *rest = pl.pallas_call(
         functools.partial(first_kernel, sizes),
-        out_shape=[x_shape, band_shape, *group_shapes(0), side, side],
+        out_shape=[x_shape, band_shape, *group_shapes(0), *[side] * (2 * SHARES)],
         in_specs=[anywhere] * 5,
-        out_specs=[vmem] * 7,
+        out_specs=[vmem] * (5 + 2 * SHARES),
         scratch_shapes=[
             *group_scratch(0), held(planes, rows * blocks, LANES),
             *[pltpu.SMEM(array.shape, array.dtype) for array in scalars], dma((planes,)), dma((len(scalars),))],
@@ -308,9 +354,11 @@
         cost_estimate=cost,
         name="first",
     )(*[in_hbm(array) for array in (*scalars, tiled)])
+    group, sends = rest[:3], rest[3:]
     made = [group]
     arriving = [lax.ppermute(group[2], "depth", ahead)]
-    swapped = [lax.ppermute(paired, "sky", swaps[0]), lax.ppermute(other, "sky", swaps[1])]
+    swapped = [[lax.ppermute(piece, "sky", swap) for piece in sends[i * SHARES:(i + 1) * SHARES]]
+               for i, swap in enumerate(swaps)]
     entries, convs = [group[0] for group in made], [group[1] for group in made]
 
     def resumed(part, turn):
@@ -332,14 +380,14 @@
         x, *group = pl.pallas_call(
             functools.partial(border_kernel, sizes, part),
             out_shape=[x_shape, *group_shapes(part)],
-            in_specs=[smem] * 4 + [vmem] * 3 + [anywhere] * (part - 1),
+            in_specs=[smem] * 4 + [vmem] * (2 + SHARES) + [anywhere] * (part - 1),
             out_specs=[vmem] * 4,
             scratch_shapes=group_scratch(part),
             input_output_aliases={4: 0},
             compiler_params=params,
             cost_estimate=cost,
             name="border",
-        )(*scalars, in_vmem(x), in_vmem(bands), swapped[part - 1], *arriving[:part - 1])
+        )(*scalars, in_vmem(x), in_vmem(bands), *swapped[part - 1], *arriving[:part - 1])
         entries.append(group[0])
         convs.append(group[1])
         arriving.append(lax.ppermute(group[2], "depth", ahead))

time: 58.2 us -> 53 us (0.911)
  waiting for transfers between devices: 34.1 us -> 23.9 us
  starting transfers between devices: 6.45 us -> 9.99 us
  Pallas kernels: 17.2 us -> 18.7 us
    ppermute x2, waiting for transfers between devices: 17 us -> 10.2 us  [per_device(): arriving.append(lax.ppermute(group[2], 'depth', ahead))]
    ppermute x2 -> x4, starting transfers between devices: 2.57 us -> 6.12 us  [per_device(): lax.ppermute(piece, 'sky', swap)]
    ppermute x2 -> x4, waiting for transfers between devices: 17.1 us -> 13.7 us  [per_device(): lax.ppermute(piece, 'sky', swap)]
  transfers between devices with their start and end apart: 5 -> 7, of which waited for: 3 -> 4; matrix products, arithmetic and copies ran while one was open for 0% -> 0% of each run, Pallas kernels for 15% -> 18%
where the time goes in v5:
time: 53 us; the launch traced here: 52.8 us
  waiting for transfers between devices  23.9 us (45%)
  Pallas kernels  18.7 us (35%)
  starting transfers between devices  9.99 us (19%)
    ppermute x4, waiting for transfers between devices, per_device(): lax.ppermute(piece, 'sky', swap)  13.7 us
    ppermute x2, waiting for transfers between devices, per_device(): arriving.append(lax.ppermute(group[2], 'depth', ahead))  10.2 us
    pallas_call x2, Pallas kernels, per_device(): pl.pallas_call(functools.partial(border_kernel, sizes, part), out_shape=[...  6.24 us
    ppermute x4, starting transfers between devices, per_device(): lax.ppermute(piece, 'sky', swap)  6.12 us
    pallas_call x1, Pallas kernels, per_device(): pl.pallas_call(functools.partial(first_kernel, sizes), out_shape=[x_shape...  5.84 us
    pallas_call x2, Pallas kernels, resumed(): pl.pallas_call(functools.partial(resume_kernel, sizes, part, turn), out_s...  3.34 us
    pallas_call x1, Pallas kernels, per_device(): pl.pallas_call(functools.partial(last_kernel, sizes, depth_count - 1), ou...  3.27 us
    ppermute x2, starting transfers between devices, per_device(): arriving.append(lax.ppermute(group[2], 'depth', ahead))  2.58 us
  transfers between devices with their start and end apart: 7, of which 4 were waited for; matrix products, arithmetic and copies ran while one was open for 0% of the time, Pallas kernels for 18%

profile of v5, /device:TPU:6, one launch (start us, length us, event | category | flops | bytes accessed | tf_op | source)
XLA Modules:
  0.0 52.8 jit_solution(6973311905144973934)
XLA Ops:
  0.0 0.0 copy-start.1
  0.0 0.0 copy-start
  0.0 0.0 copy-start.3
  0.0 0.0 copy-start.2
  0.0 5.8 %first.1 = (f32[12,800,128]{2,1,0:T(8,128)S(1)}, bf16[12,3,128,256]{3,2,1,0:T(8,128)(2,1)S(1)}, f32[12,3,224,128]{3,2,1,0:T(8,128)S(1)}, f32[12,224,128]{2,1,0:T...) custom-call(s32[12]{0:T(128)} %widths.3, ...), custom_call_target="tpu_custom_call" | custom-call | flops 1 | bytes 1 | tf_op jit(solution)/shard_map/first/pallas_call | solution.py:345
  5.9 1.3 %collective-permute-start.4 = (f32[7,224,128]{2,1,0:T(8,128)S(1)}, f32[7,224,128]{2,1,0:T(8,128)S(1)}, u32[]{:S(2)}, u32[]{:S(2)}) collective-permute-start(f32[7,224,128]{2,1,0:T(8,128)S(1)} %get-tuple-element.29), channel_id=1, source_target_pairs={{0,16},{1,17},{2,18},{3,19},{4,20},{5,21},{6,22},{7,23},{8,24},{9,... | collective-permute-start | bytes 2408456 | tf_op jit(solution)/shard_map/ppermute | solution.py:359
  7.2 0.1 collective-permute-start
  7.2 0.5 collective-permute-start.1
  7.7 2.1 %collective-permute-start.2 = (f32[6,144,128]{2,1,0:T(8,128)S(1)}, f32[6,144,128]{2,1,0:T(8,128)S(1)}, u32[]{:S(2)}, u32[]{:S(2)}) collective-permute-start(f32[6,144,128]{2,1,0:T(8,128)S(1)} %get-tuple-element.27), channel_id=1, source_target_pairs={{1,2},{2,1},{3,4},{4,3},{5,6},{6,5},{7,8},{8,7},{9,10},{10,9},{11,... | collective-permute-start | bytes 1327112 | tf_op jit(solution)/shard_map/ppermute | solution.py:360
  9.8 3.5 %collective-permute-start.3 = (f32[6,144,128]{2,1,0:T(8,128)S(1)}, f32[6,144,128]{2,1,0:T(8,128)S(1)}, u32[]{:S(2)}, u32[]{:S(2)}) collective-permute-start(f32[6,144,128]{2,1,0:T(8,128)S(1)} %get-tuple-element.28), channel_id=1, source_target_pairs={{1,2},{2,1},{3,4},{4,3},{5,6},{6,5},{7,8},{8,7},{9,10},{10,9},{11,... | collective-permute-start | bytes 1327112 | tf_op jit(solution)/shard_map/ppermute | solution.py:360
  13.3 0.0 collective-permute-done.refs_0_
  13.3 0.0 collective-permute-done.1.refs_1_
  13.3 0.0 copy-done.1
  13.3 0.0 copy-done
  13.3 0.0 copy-done.3
  13.4 0.0 copy-done.2
  13.4 3.2 %border.2 = (f32[12,800,128]{2,1,0:T(8,128)S(1)}, f32[12,3,144,128]{3,2,1,0:T(8,128)S(1)}, f32[12,144,128]{2,1,0:T(8,128)S(1)}, f32[7,144,128]{2,1,0:T(8,128)S(1)}) custom-call(s32[12]{0:T(128)S(1)} %copy-done.2, s32[12]{0:T(128)S(1)} %copy-done, f32[16]{0:T(128)S(1)} %copy-done.1, f32[16]{0:T(128)S(1)} %copy-done.3, ...), custom_call_target="tpu_custom_call", output_to_operand_aliasing={{0}: (4, {})} | custom-call | flops 1 | bytes 1 | tf_op jit(solution)/shard_map/border/pallas_call | solution.py:380
  16.5 1.3 %collective-permute-start.6 = (f32[7,144,128]{2,1,0:T(8,128)S(1)}, f32[7,144,128]{2,1,0:T(8,128)S(1)}, u32[]{:S(2)}, u32[]{:S(2)}) collective-permute-start(f32[7,144,128]{2,1,0:T(8,128)S(1)} %get-tuple-element.36), channel_id=1, source_target_pairs={{0,16},{1,17},{2,18},{3,19},{4,20},{5,21},{6,22},{7,23},{8,24},{9,... | collective-permute-start | bytes 1548296 | tf_op jit(solution)/shard_map/ppermute | solution.py:393
  17.8 9.0 %collective-permute-done.2.refs_0_ = f32[6,144,128]{2,1,0:T(8,128)S(1)} collective-permute-done((f32[6,144,128]{2,1,0:T(8,128)S(1)}, f32[6,144,128]{2,1,0:T(8,128)S(1)}, u32[]{:S(2)}, u32[]{:S(2)}) %collective-permute-start.2) | collective-permute-done | bytes 442400 | tf_op jit(solution)/shard_map/ppermute | solution.py:360
  26.8 4.7 %collective-permute-done.3.refs_1_ = f32[6,144,128]{2,1,0:T(8,128)S(1)} collective-permute-done((f32[6,144,128]{2,1,0:T(8,128)S(1)}, f32[6,144,128]{2,1,0:T(8,128)S(1)}, u32[]{:S(2)}, u32[]{:S(2)}) %collective-permute-start.3) | collective-permute-done | bytes 442400 | tf_op jit(solution)/shard_map/ppermute | solution.py:360
  31.6 0.0 collective-permute-done.4.refs_2_.incoming
  31.6 3.1 %border.3 = (f32[12,800,128]{2,1,0:T(8,128)S(1)}, f32[12,3,144,128]{3,2,1,0:T(8,128)S(1)}, f32[12,144,128]{2,1,0:T(8,128)S(1)}, f32[7,144,128]{2,1,0:T(8,128)S(1)}) custom-call(s32[12]{0:T(128)S(1)} %copy-done.2, s32[12]{0:T(128)S(1)} %copy-done, f32[16]{0:T(128)S(1)} %copy-done.1, f32[16]{0:T(128)S(1)} %copy-done.3, ...), custom_call_target="tpu_custom_call", output_to_operand_aliasing={{0}: (4, {})} | custom-call | flops 1 | bytes 1 | tf_op jit(solution)/shard_map/border/pallas_call | solution.py:380
  34.7 1.3 %collective-permute-start.5 = (f32[7,144,128]{2,1,0:T(8,128)S(1)}, f32[7,144,128]{2,1,0:T(8,128)S(1)}, u32[]{:S(2)}, u32[]{:S(2)}) collective-permute-start(f32[7,144,128]{2,1,0:T(8,128)S(1)} %get-tuple-element.31), channel_id=1, source_target_pairs={{0,16},{1,17},{2,18},{3,19},{4,20},{5,21},{6,22},{7,23},{8,24},{9,... | collective-permute-start | bytes 1548296 | tf_op jit(solution)/shard_map/ppermute | solution.py:393
  36.0 1.9 %resume.2.refs_0_ = f32[12,224,128]{2,1,0:T(8,128)S(1)} custom-call(s32[12]{0:T(128)S(1)} %copy-done, f32[16]{0:T(128)S(1)} %copy-done.1, f32[12,3,224,128]{3,2,1,0:T(8,128)S(1)} %get-tuple-element.33.entry_ref, f32[7,224,128]{2,1,0:T(8,128)S(1)} %collective-permute-done.4.refs_2_.incoming, ...), custom_call_target="tpu_custom_call", output_to_operand_aliasing={{}: (4, {})} | custom-call | flops 1 | bytes 1 | tf_op jit(solution)/shard_map/resume/pallas_call | solution.py:366
  37.9 1.7 %collective-permute-done.6.incoming = f32[7,144,128]{2,1,0:T(8,128)S(1)} collective-permute-done((f32[7,144,128]{2,1,0:T(8,128)S(1)}, f32[7,144,128]{2,1,0:T(8,128)S(1)}, u32[]{:S(2)}, u32[]{:S(2)}) %collective-permute-start.6) | collective-permute-done | bytes 516128 | tf_op jit(solution)/shard_map/ppermute | solution.py:393
  39.6 1.4 %resume.3.refs_1_ = f32[12,144,128]{2,1,0:T(8,128)S(1)} custom-call(s32[12]{0:T(128)S(1)} %copy-done, f32[16]{0:T(128)S(1)} %copy-done.1, f32[12,3,144,128]{3,2,1,0:T(8,128)S(1)} %get-tuple-element.35.entry_ref, f32[7,144,128]{2,1,0:T(8,128)S(1)} %collective-permute-done.6.incoming, ...), custom_call_target="tpu_custom_call", output_to_operand_aliasing={{}: (4, {})} | custom-call | flops 1 | bytes 1 | tf_op jit(solution)/shard_map/resume/pallas_call | solution.py:366
  41.0 8.5 %collective-permute-done.5.incoming = f32[7,144,128]{2,1,0:T(8,128)S(1)} collective-permute-done((f32[7,144,128]{2,1,0:T(8,128)S(1)}, f32[7,144,128]{2,1,0:T(8,128)S(1)}, u32[]{:S(2)}, u32[]{:S(2)}) %collective-permute-start.5) | collective-permute-done | bytes 516128 | tf_op jit(solution)/shard_map/ppermute | solution.py:393
  49.5 3.3 %last.1 = (f32[12,144,128]{2,1,0:T(8,128)S(1)}, f32[12,512,128]{2,1,0:T(8,128)}) custom-call(s32[12]{0:T(128)S(1)} %copy-done, f32[16]{0:T(128)S(1)} %copy-done.1, f32[12,3,144,128]{3,2,1,0:T(8,128)S(1)} %get-tuple-element.30.entry_ref, f32[7,144,128]{2,1,0:T(8,128)S(1)} %collective-permute-done.5.incoming, ...), custom_call_target="tpu_custom_call", output_to_operand_aliasing={{0}: (4, {})} | custom-call | flops 1 | bytes 1 | tf_op jit(solution)/shard_map/last/pallas_call | solution.py:398
Async XLA Ops:
  0.0 13.3 %copy-start.1 = (f32[16]{0:T(128)S(1)}, f32[16]{0:T(128)}, u32[]{:S(2)}) copy-start(f32[16]{0:T(128)} %near.9) | copy-start | bytes 196
  0.0 13.3 %copy-start = (s32[12]{0:T(128)S(1)}, s32[12]{0:T(128)}, u32[]{:S(2)}) copy-start(s32[12]{0:T(128)} %slots.9) | copy-start | bytes 148
  0.0 13.3 %copy-start.3 = (f32[16]{0:T(128)S(1)}, f32[16]{0:T(128)}, u32[]{:S(2)}) copy-start(f32[16]{0:T(128)} %lens.3) | copy-start | bytes 196
  0.0 13.3 %copy-start.2 = (s32[12]{0:T(128)S(1)}, s32[12]{0:T(128)}, u32[]{:S(2)}) copy-start(s32[12]{0:T(128)} %widths.3) | copy-start | bytes 148
  5.9 25.7 %collective-permute-start.4 = (f32[7,224,128]{2,1,0:T(8,128)S(1)}, f32[7,224,128]{2,1,0:T(8,128)S(1)}, u32[]{:S(2)}, u32[]{:S(2)}) collective-permute-start(f32[7,224,128]{2,1,0:T(8,128)S(1)} %get-tuple-element.29), channel_id=1, source_target_pairs={{0,16},{1,17},{2,18},{3,19},{4,20},{5,21},{6,22},{7,23},{8,24},{9,... | collective-permute-start | bytes 2408456 | tf_op jit(solution)/shard_map/ppermute | solution.py:359
  7.2 6.1 %collective-permute-start = (f32[6,144,128]{2,1,0:T(8,128)S(1)}, f32[6,144,128]{2,1,0:T(8,128)S(1)}, u32[]{:S(2)}, u32[]{:S(2)}) collective-permute-start(f32[6,144,128]{2,1,0:T(8,128)S(1)} %get-tuple-element.24), channel_id=1, source_target_pairs={{0,1},{1,0},{2,3},{3,2},{4,5},{5,4},{6,7},{7,6},{8,9},{9,8},{10,11... | collective-permute-start | bytes 1327112 | tf_op jit(solution)/shard_map/ppermute | solution.py:360
  7.2 6.1 %collective-permute-start.1 = (f32[6,144,128]{2,1,0:T(8,128)S(1)}, f32[6,144,128]{2,1,0:T(8,128)S(1)}, u32[]{:S(2)}, u32[]{:S(2)}) collective-permute-start(f32[6,144,128]{2,1,0:T(8,128)S(1)} %get-tuple-element.25), channel_id=1, source_target_pairs={{0,1},{1,0},{2,3},{3,2},{4,5},{5,4},{6,7},{7,6},{8,9},{9,8},{10,11... | collective-permute-start | bytes 1327112 | tf_op jit(solution)/shard_map/ppermute | solution.py:360
  7.7 19.1 %collective-permute-start.2 = (f32[6,144,128]{2,1,0:T(8,128)S(1)}, f32[6,144,128]{2,1,0:T(8,128)S(1)}, u32[]{:S(2)}, u32[]{:S(2)}) collective-permute-start(f32[6,144,128]{2,1,0:T(8,128)S(1)} %get-tuple-element.27), channel_id=1, source_target_pairs={{1,2},{2,1},{3,4},{4,3},{5,6},{6,5},{7,8},{8,7},{9,10},{10,9},{11,... | collective-permute-start | bytes 1327112 | tf_op jit(solution)/shard_map/ppermute | solution.py:360
  9.8 21.7 %collective-permute-start.3 = (f32[6,144,128]{2,1,0:T(8,128)S(1)}, f32[6,144,128]{2,1,0:T(8,128)S(1)}, u32[]{:S(2)}, u32[]{:S(2)}) collective-permute-start(f32[6,144,128]{2,1,0:T(8,128)S(1)} %get-tuple-element.28), channel_id=1, source_target_pairs={{1,2},{2,1},{3,4},{4,3},{5,6},{6,5},{7,8},{8,7},{9,10},{10,9},{11,... | collective-permute-start | bytes 1327112 | tf_op jit(solution)/shard_map/ppermute | solution.py:360
  16.5 23.1 %collective-permute-start.6 = (f32[7,144,128]{2,1,0:T(8,128)S(1)}, f32[7,144,128]{2,1,0:T(8,128)S(1)}, u32[]{:S(2)}, u32[]{:S(2)}) collective-permute-start(f32[7,144,128]{2,1,0:T(8,128)S(1)} %get-tuple-element.36), channel_id=1, source_target_pairs={{0,16},{1,17},{2,18},{3,19},{4,20},{5,21},{6,22},{7,23},{8,24},{9,... | collective-permute-start | bytes 1548296 | tf_op jit(solution)/shard_map/ppermute | solution.py:393
  34.7 14.8 %collective-permute-start.5 = (f32[7,144,128]{2,1,0:T(8,128)S(1)}, f32[7,144,128]{2,1,0:T(8,128)S(1)}, u32[]{:S(2)}, u32[]{:S(2)}) collective-permute-start(f32[7,144,128]{2,1,0:T(8,128)S(1)} %get-tuple-element.31), channel_id=1, source_target_pairs={{0,16},{1,17},{2,18},{3,19},{4,20},{5,21},{6,22},{7,23},{8,24},{9,... | collective-permute-start | bytes 1548296 | tf_op jit(solution)/shard_map/ppermute | solution.py:393

commit v6 on v5

--- a/solution.py
+++ b/solution.py
@@ -13,6 +13,7 @@
 SUB = 8
 TOGETHER = 4
 PARTS = (3, 2, 2)
+BORDER_SHARES = (((0, 1),), ((0,), (1,)))
 SHARES = 2
 SENT = 7
 TINY, POLE, FAR = 1e-30, 1e-20, 1e10
@@ -45,24 +46,24 @@
     return found
 
 
-def make_bands(planes, widths, band_ref):
+def make_bands(band_ref):
     source = lax.broadcasted_iota(jnp.int32, (LANES, 2 * LANES), 0)
     target = lax.broadcasted_iota(jnp.int32, (LANES, 2 * LANES), 1)
     across = jnp.where(target >= LANES + LANES // 2, source + 2 * LANES, source)
     offset = across - target
     distance = jnp.abs(offset)
 
-    def plane(k, carry):
-        half_width = widths[k]
+    def width(index, carry):
+        half_width = index + 1
         rim = (distance == half_width + 1).astype(F32)
         edge = (distance == half_width).astype(F32)
         inside = (distance <= half_width).astype(F32)
         both = rim + edge
         for field, value in enumerate((rim - edge, jnp.where(offset > 0, both, -both), inside)):
-            band_ref[k, field] = value.astype(BF16)
+            band_ref[index, field] = value.astype(BF16)
         return carry
 
-    lax.fori_loop(0, planes, plane, 0)
+    lax.fori_loop(0, WMAX, width, 0)
 
 
 def build(k, half_width, first, count, blocks, x_ref, left_ref):
@@ -84,8 +85,8 @@
                 left_ref[field, here, part * LANES:(part + 1) * LANES] = piece
 
 
-def multiply(k, field, band_ref, left_ref):
-    weight = jnp.concatenate([band_ref[k, field]] * PARTS[field], axis=0)
+def multiply(half_width, field, band_ref, left_ref):
+    weight = jnp.concatenate([band_ref[half_width - 1, field]] * PARTS[field], axis=0)
     return jnp.dot(left_ref[field, :, :PARTS[field] * LANES], weight, preferred_element_type=F32)
 
 
@@ -108,20 +109,29 @@
 
     def part(index, carry):
         where = pl.ds(pl.multiple_of(index * step, step), step)
-        state = start(where, (step, LANES))
-        now, then = state[:4], state[4:]
+        now, then = (None, None) if start is None else start(where)
         for k in range(planes):
             xx, xy, yy = [entry_ref[k, i, where, :] for i in range(3)]
             kept = 1.0 - near_of(k)
-            new = [
-                xx * now[0] + xy * now[2] + kept * then[0],
-                xx * now[1] + xy * now[3] + kept * then[1],
-                xy * now[0] + yy * now[2] + kept * then[2],
-                xy * now[1] + yy * now[3] + kept * then[3],
-            ]
-            now, then = new, now
+            if now is None:
+                one, zero = jnp.ones((step, LANES), F32), jnp.zeros((step, LANES), F32)
+                now, new = [one, zero, zero, one], [xx + kept, xy, xy, yy + kept]
+            else:
+                new = [
+                    xx * now[0] + xy * now[2],
+                    xx * now[1] + xy * now[3],
+                    xy * now[0] + yy * now[2],
+                    xy * now[1] + yy * now[3],
+                ]
+                if then is None:
+                    new = [new[0] + kept, new[1], new[2], new[3] + kept]
+                else:
+                    new = [value + kept * old for value, old in zip(new, then)]
+            then = now if k or start is not None else None
+            now = new
             conv_ref[k, where, :] = 1.0 - 0.5 * (new[0] + new[3])
-        finish(where, now + then)
+        if finish is not None:
+            finish(where, now + then)
         return carry
 
     lax.fori_loop(0, length // step, part, 0)
@@ -154,13 +164,9 @@
     share = 1.0 / (1.0 + square)
     q = [norm * (2.0 * share * value) for value in u] + [norm * ((1.0 - square) * share)]
     half = lambda a, b: 0.5 * (a + b)
-    return [half(p[0], q[0]), half(p[2], q[2]), half(p[1], q[1]), half(p[3], q[3]),
-            half(q[2], -p[2]), half(p[0], -q[0]), half(q[3], -p[3]), half(p[1], -q[1])]
-
-
-def identity_state(where, shape):
-    one, zero = jnp.ones(shape, F32), jnp.zeros(shape, F32)
-    return [one, zero, zero, one] * 2
+    now = [half(p[0], q[0]), half(p[2], q[2]), half(p[1], q[1]), half(p[3], q[3])]
+    then = [half(q[2], -p[2]), half(p[0], -q[0]), half(q[3], -p[3]), half(p[1], -q[1])]
+    return now, then
 
 
 def writer(state_ref):
@@ -171,34 +177,45 @@
     return finish
 
 
-def group_stage(sizes, part, scalars, x_ref, band_ref, left_refs, beside_refs, entry_ref, conv_ref, state_ref,
-                before_plane=lambda k: None):
+def steps_of(planes, shares):
+    count = planes // SHARES
+    per = next(n for n in range(max(1, TOGETHER // len(shares)), 0, -1) if count % n == 0)
+    return count // per, per
+
+
+def group_stage(sizes, part, scalars, x_ref, band_ref, scratch, entry_ref, conv_ref, state_ref, before_plane,
+                shares=tuple(range(SHARES))):
     planes, rows, blocks = sizes
     widths, slots, near, lens = scalars
+    left_refs, beside_refs = scratch[::2], scratch[1::2]
     first, count = first_row(rows, part) + RIM, group_sizes(rows)[part]
-    together = len(left_refs)
+    steps, per = steps_of(planes, shares)
     for beside_ref in beside_refs:
         beside_ref[...] = jnp.zeros(beside_ref.shape, F32)
 
     def step(index, carry):
-        ks = [index * together + i for i in range(together)]
-        for k in ks:
-            before_plane(k)
+        ks = []
+        for i in range(per):
+            for share in shares:
+                place = index * per + i
+                ks.append(place * SHARES + share)
+                before_plane(share, place, ks[-1])
         for k, left_ref in zip(ks, left_refs):
             build(k, widths[k], first, count, blocks, x_ref, left_ref)
         for field in range(3):
             for k, left_ref, beside_ref in zip(ks, left_refs, beside_refs):
                 width = (2 * widths[k] + 1).astype(F32)
                 combine(k, field, near[slots[k]], lens[slots[k]] / (width * width), blocks,
-                        multiply(k, field, band_ref, left_ref), beside_ref, entry_ref)
+                        multiply(widths[k], field, band_ref, left_ref), beside_ref, entry_ref)
         return carry
 
-    lax.fori_loop(0, planes // together, step, 0)
-
-    @pl.when(lax.axis_index("depth") == 0)
-    def _():
-        sweep(planes, group_sizes(rows)[part] * blocks, lambda k: near[slots[k]], entry_ref, conv_ref, identity_state,
-              writer(state_ref))
+    lax.fori_loop(0, steps, step, 0)
+    if shares[-1] == SHARES - 1:
+
+        @pl.when(lax.axis_index("depth") == 0)
+        def _():
+            sweep(planes, group_sizes(rows)[part] * blocks, lambda k: near[slots[k]], entry_ref, conv_ref, None,
+                  writer(state_ref))
 
 
 def first_kernel(sizes, widths_hbm, slots_hbm, near_hbm, lens_hbm, potential_hbm, x_ref, band_ref, entry_ref, conv_ref,
@@ -206,7 +223,6 @@
     planes, rows, blocks = sizes
     sends, scratch = refs[:2 * SHARES], refs[2 * SHARES:]
     scratch, (tiles_ref, widths, slots, near, lens, plane_sems, table_sems) = scratch[:-7], scratch[-7:]
-    share = planes // SHARES
     tables = ((widths_hbm, widths), (slots_hbm, slots), (near_hbm, near), (lens_hbm, lens))
     copies = [pltpu.make_async_copy(*pair, table_sems.at[i]) for i, pair in enumerate(tables)]
     for copy in copies:
@@ -217,12 +233,12 @@
 
     for k in range(planes):
         plane_copy(k).start()
+    make_bands(band_ref)
     for copy in copies:
         copy.wait()
-    make_bands(planes, widths, band_ref)
     sides = [(start + RIM) * blocks for start, _ in side_starts(rows)]
 
-    def arrive(k):
+    def arrive(share, place, k):
         plane_copy(k).wait()
         for row in range(rows):
             for half in range(blocks // SUB):
@@ -230,33 +246,26 @@
                 x_ref[k, pl.ds((row + RIM) * blocks + half * SUB, SUB), :] = tiles_ref[
                     k, pl.ds(start, SUB, stride=SUB), :]
         for i, side in enumerate(sides):
-            rows_out = x_ref[k, pl.ds(pl.multiple_of(side, blocks), RIM * blocks), :]
-            for piece in range(SHARES):
-
-                @pl.when(lax.div(k, share) == piece)
-                def _(ref=sends[i * SHARES + piece]):
-                    ref[lax.rem(k, share)] = rows_out
-
-    group_stage(sizes, 0, (widths, slots, near, lens), x_ref, band_ref, scratch[::2], scratch[1::2], entry_ref, conv_ref,
-                state_ref, arrive)
-
-
-def border_kernel(sizes, part, widths, slots, near, lens, x_in, band_ref, *refs):
-    planes, rows, blocks = sizes
-    arrived, refs = refs[:SHARES], refs[SHARES:]
-    share = planes // SHARES
-    x_ref, entry_ref, conv_ref, state_ref, *scratch = refs[part - 1:]
+            sends[i * SHARES + share][place] = x_ref[k, pl.ds(pl.multiple_of(side, blocks), RIM * blocks), :]
+
+    group_stage(sizes, 0, (widths, slots, near, lens), x_ref, band_ref, scratch, entry_ref, conv_ref, state_ref, arrive)
+
+
+def border_kernel(sizes, part, shares, widths, slots, near, lens, band_ref, x_in, entry_in, *refs):
+    planes, rows, blocks = sizes
+    arrived, refs = refs[:len(shares)], refs[len(shares):]
+    last = shares[-1] == SHARES - 1
+    outputs = 4 if last else 2
+    scratch_count = 2 * len(shares) * steps_of(planes, shares)[1]
+    refs, scratch = refs[-outputs - scratch_count:-scratch_count], refs[-scratch_count:]
+    x_ref, entry_ref, conv_ref, state_ref = (*refs, None, None)[:4]
     start = side_starts(rows)[part - 1][1] + RIM
 
-    def arrive(k):
-        for piece, ref in enumerate(arrived):
-
-            @pl.when(lax.div(k, share) == piece)
-            def _(ref=ref):
-                x_ref[k, pl.ds(pl.multiple_of(start * blocks, blocks), RIM * blocks), :] = ref[lax.rem(k, share)]
-
-    group_stage(sizes, part, (widths, slots, near, lens), x_ref, band_ref, scratch[::2], scratch[1::2], entry_ref,
-                conv_ref, state_ref, arrive)
+    def arrive(share, place, k):
+        x_ref[k, pl.ds(pl.multiple_of(start * blocks, blocks), RIM * blocks), :] = arrived[shares.index(share)][place]
+
+    group_stage(sizes, part, (widths, slots, near, lens), x_ref, band_ref, scratch, entry_ref, conv_ref, state_ref, arrive,
+                shares)
 
 
 def resume(sizes, part, turn, slots, near, entry_ref, incoming, conv_ref, finish):
@@ -265,37 +274,60 @@
     @pl.when(lax.axis_index("depth") == turn)
     def _():
         sweep(planes, group_sizes(rows)[part] * blocks, lambda k: near[slots[k]], entry_ref, conv_ref,
-              lambda where, shape: unpacked_state([incoming[i, where, :] for i in range(SENT)]), finish)
+              lambda where: unpacked_state([incoming[i, where, :] for i in range(SENT)]), finish)
 
 
 def resume_kernel(sizes, part, turn, slots, near, entry_ref, incoming, conv_in, conv_ref, *state_ref):
-    finish = writer(state_ref[0]) if state_ref else lambda where, state: None
-    resume(sizes, part, turn, slots, near, entry_ref, incoming, conv_ref, finish)
-
-
-def last_kernel(sizes, turn, slots, near, entry_ref, incoming, conv_in, *refs):
-    planes, rows, blocks = sizes
-    others, (conv_ref, out_hbm, tiles_ref, sems) = refs[:-4], refs[-4:]
-    part = len(others)
-    resume(sizes, part, turn, slots, near, entry_ref, incoming, conv_ref, lambda where, state: None)
+    resume(sizes, part, turn, slots, near, entry_ref, incoming, conv_ref, writer(state_ref[0]) if state_ref else None)
+
+
+def place_rows(sizes, part, k, conv_ref, tiles_ref):
+    planes, rows, blocks = sizes
+    start = first_row(rows, part)
+    for i in range(group_sizes(rows)[part]):
+        row = start + i
+        for half in range(blocks // SUB):
+            to = lax.div(row, SUB) * SUB * blocks + half * SUB * SUB + lax.rem(row, SUB)
+            tiles_ref[k, pl.ds(to, SUB, stride=SUB), :] = conv_ref[k, pl.ds(i * blocks + half * SUB, SUB), :]
+
+
+def write_out(sizes, late, tiles_ref, out_hbm, sems, before_plane):
+    planes, rows, blocks = sizes
+    even = lax.rem(lax.axis_index("sky"), 2) == 0
+    tail = -(-RIM // SUB) * SUB
+    if late:
+        start, count = jnp.where(even, 0, rows - tail), tail
+    else:
+        start, count = jnp.where(even, tail, 0), rows - tail
 
     def plane_copy(k):
-        return pltpu.make_async_copy(tiles_ref.at[k], out_hbm.at[k], sems.at[k])
+        where = pl.ds(pl.multiple_of(start * blocks, SUB * blocks), count * blocks)
+        return pltpu.make_async_copy(tiles_ref.at[k, where], out_hbm.at[k, where], sems.at[k])
 
     def plane(k, carry):
-        for part, ref in enumerate((*others, conv_ref)):
-            start = first_row(rows, part)
-            for i in range(group_sizes(rows)[part]):
-                row = start + i
-                for half in range(blocks // SUB):
-                    to = (row // SUB) * SUB * blocks + half * SUB * SUB + row % SUB
-                    tiles_ref[k, pl.ds(to, SUB, stride=SUB), :] = ref[k, pl.ds(i * blocks + half * SUB, SUB), :]
+        before_plane(k)
         plane_copy(k).start()
         return carry
 
     lax.fori_loop(0, planes, plane, 0)
     for k in range(planes):
         plane_copy(k).wait()
+
+
+def early_kernel(sizes, *refs):
+    *conv_refs, tiles_ref, out_hbm, sems = refs
+
+    def place(k):
+        for part, conv_ref in enumerate(conv_refs):
+            place_rows(sizes, part, k, conv_ref, tiles_ref)
+
+    write_out(sizes, False, tiles_ref, out_hbm, sems, place)
+
+
+def last_kernel(sizes, part, turn, slots, near, entry_ref, incoming, conv_in, tiles_in, out_in, conv_ref, tiles_ref,
+                out_hbm, sems):
+    resume(sizes, part, turn, slots, near, entry_ref, incoming, conv_ref, None)
+    write_out(sizes, True, tiles_ref, out_hbm, sems, lambda k: place_rows(sizes, part, k, conv_ref, tiles_ref))
 
 
 def per_device(potential, widths, plane_slot, ratio_near, ratio_lens):
@@ -303,7 +335,6 @@
     blocks = cols // LANES
     sizes = (planes, rows, blocks)
     parts = len(group_sizes(rows))
-    together = next(count for count in range(TOGETHER, 0, -1) if planes % count == 0)
     depth_count, sky_count = lax.axis_size("depth"), lax.axis_size("sky")
     swaps = [[pair for i in range(first, sky_count - 1, 2) for pair in ((i, i + 1), (i + 1, i))] for first in (0, 1)]
     ahead = [(i, i + 1) for i in range(depth_count - 1)]
@@ -330,16 +361,16 @@
         return pltpu.with_memory_space_constraint(array, pltpu.HBM)
 
     x_shape = held(planes, (rows + 2 * RIM) * blocks, LANES)
-    band_shape = held(planes, 3, LANES, 2 * LANES, dtype=BF16)
+    band_shape = held(WMAX, 3, LANES, 2 * LANES, dtype=BF16)
 
     def group_shapes(part):
         length = group_sizes(rows)[part] * blocks
         return [held(planes, 3, length, LANES), held(planes, length, LANES), moved(SENT, length, LANES)]
 
-    def group_scratch(part):
+    def group_scratch(part, shares):
         count = group_sizes(rows)[part]
         return [held(3, count * blocks, max(PARTS) * LANES, dtype=BF16),
-                held(3, (count + 1) * (blocks + SUB), LANES)] * together
+                held(3, (count + 1) * (blocks + SUB), LANES)] * (len(shares) * steps_of(planes, shares)[1])
 
     side = moved(planes // SHARES, RIM * blocks, LANES)
     x, bands, *rest = pl.pallas_call(
@@ -348,7 +379,7 @@
         in_specs=[anywhere] * 5,
         out_specs=[vmem] * (5 + 2 * SHARES),
         scratch_shapes=[
-            *group_scratch(0), held(planes, rows * blocks, LANES),
+            *group_scratch(0, range(SHARES)), held(planes, rows * blocks, LANES),
             *[pltpu.SMEM(array.shape, array.dtype) for array in scalars], dma((planes,)), dma((len(scalars),))],
         compiler_params=params,
         cost_estimate=cost,
@@ -360,6 +391,7 @@
     swapped = [[lax.ppermute(piece, "sky", swap) for piece in sends[i * SHARES:(i + 1) * SHARES]]
                for i, swap in enumerate(swaps)]
     entries, convs = [group[0] for group in made], [group[1] for group in made]
+    out_shape = moved(planes, rows * blocks, LANES)
 
     def resumed(part, turn):
         last = turn == depth_count - 1
@@ -377,36 +409,50 @@
             arriving[part] = lax.ppermute(state[0], "depth", ahead)
 
     for part in range(1, parts):
-        x, *group = pl.pallas_call(
-            functools.partial(border_kernel, sizes, part),
-            out_shape=[x_shape, *group_shapes(part)],
-            in_specs=[smem] * 4 + [vmem] * (2 + SHARES) + [anywhere] * (part - 1),
-            out_specs=[vmem] * 4,
-            scratch_shapes=group_scratch(part),
-            input_output_aliases={4: 0},
-            compiler_params=params,
-            cost_estimate=cost,
-            name="border",
-        )(*scalars, in_vmem(x), in_vmem(bands), *swapped[part - 1], *arriving[:part - 1])
-        entries.append(group[0])
-        convs.append(group[1])
-        arriving.append(lax.ppermute(group[2], "depth", ahead))
+        entry = None
+        for shares in BORDER_SHARES[part - 1]:
+            last = shares[-1] == SHARES - 1
+            behind = arriving[:1] if last and part > 1 else []
+            x, entry, *group = pl.pallas_call(
+                functools.partial(border_kernel, sizes, part, shares),
+                out_shape=[x_shape, *group_shapes(part)[:3 if last else 1]],
+                in_specs=[smem] * 4 + [vmem] * 2 + [anywhere if entry is None else vmem] + [vmem] * len(shares)
+                + [anywhere] * len(behind),
+                out_specs=[vmem] * (4 if last else 2),
+                scratch_shapes=group_scratch(part, shares),
+                input_output_aliases={5: 0} if entry is None else {5: 0, 6: 1},
+                compiler_params=params,
+                cost_estimate=cost,
+                name="border",
+            )(*scalars, in_vmem(bands), in_vmem(x), plane_slot if entry is None else in_vmem(entry),
+              *[swapped[part - 1][share] for share in shares], *behind)
+        entries.append(entry)
+        convs.append(group[0])
+        arriving.append(lax.ppermute(group[1], "depth", ahead))
     for turn in range(1, depth_count):
         for part in range(parts - (turn == depth_count - 1)):
             resumed(part, turn)
-
-    conv, out = pl.pallas_call(
-        functools.partial(last_kernel, sizes, depth_count - 1),
-        out_shape=[group_shapes(parts - 1)[1], moved(planes, rows * blocks, LANES)],
-        in_specs=[smem] * 2 + [vmem] * (3 + parts - 1),
+    tiles, out = pl.pallas_call(
+        functools.partial(early_kernel, sizes),
+        out_shape=[held(planes, rows * blocks, LANES), out_shape],
+        in_specs=[vmem] * (parts - 1),
         out_specs=[vmem, anywhere],
-        scratch_shapes=[held(planes, rows * blocks, LANES), dma((planes,))],
-        input_output_aliases={4: 0},
+        scratch_shapes=[dma((planes,))],
+        compiler_params=params,
+        cost_estimate=cost,
+        name="early",
+    )(*[in_vmem(conv) for conv in convs[:-1]])
+    conv, tiles, out = pl.pallas_call(
+        functools.partial(last_kernel, sizes, parts - 1, depth_count - 1),
+        out_shape=[group_shapes(parts - 1)[1], held(planes, rows * blocks, LANES), out_shape],
+        in_specs=[smem] * 2 + [vmem] * 4 + [anywhere],
+        out_specs=[vmem, vmem, anywhere],
+        scratch_shapes=[dma((planes,))],
+        input_output_aliases={4: 0, 5: 1, 6: 2},
         compiler_params=params,
         cost_estimate=cost,
         name="last",
-    )(plane_slot, ratio_near, in_vmem(entries[-1]), arriving[-1], in_vmem(convs[-1]),
-      *[in_vmem(conv) for conv in convs[:-1]])
+    )(plane_slot, ratio_near, in_vmem(entries[-1]), arriving[-1], in_vmem(convs[-1]), in_vmem(tiles), out)
     out = out.reshape(planes, rows // SUB, blocks, SUB, LANES).transpose(0, 1, 3, 2, 4)
     return out.reshape(planes, rows, cols)
 

time: 53 us -> 51.6 us (0.974)
  waiting for transfers between devices: 23.9 us -> 22.2 us
    ppermute x4, waiting for transfers between devices: 13.7 us -> 12.1 us  [per_device(): lax.ppermute(piece, 'sky', swap)]
    pallas_call x3 -> x5, Pallas kernels: 9.51 us -> 10.6 us  [the longest x3 6.62 us: per_device(): pl.pallas_call(functools.partial(border_kernel, sizes, part, shares), out...]
    pallas_call x1, Pallas kernels: 5.84 us -> 4.93 us  [per_device(): pl.pallas_call(functools.partial(first_kernel, sizes), out_shape=[x_shape...]
  transfers between devices with their start and end apart: 7 -> 7, of which waited for: 4 -> 4; matrix products, arithmetic and copies ran while one was open for 0% -> 0% of each run, Pallas kernels for 18% -> 22%
where the time goes in v6:
time: 51.6 us; the launch traced here: 51.3 us
  waiting for transfers between devices  22.2 us (43%)
  Pallas kernels  18.9 us (37%)
  starting transfers between devices  9.99 us (19%)
    ppermute x4, waiting for transfers between devices, per_device(): lax.ppermute(piece, 'sky', swap)  12.1 us
    ppermute x2, waiting for transfers between devices, per_device(): arriving.append(lax.ppermute(group[1], 'depth', ahead))  10.1 us
    pallas_call x3, Pallas kernels, per_device(): pl.pallas_call(functools.partial(border_kernel, sizes, part, shares), out...  6.62 us
    ppermute x4, starting transfers between devices, per_device(): lax.ppermute(piece, 'sky', swap)  6.12 us
    pallas_call x1, Pallas kernels, per_device(): pl.pallas_call(functools.partial(first_kernel, sizes), out_shape=[x_shape...  4.93 us
    pallas_call x2, Pallas kernels, resumed(): pl.pallas_call(functools.partial(resume_kernel, sizes, part, turn), out_s...  3.34 us
    pallas_call x1, Pallas kernels, per_device(): pl.pallas_call(functools.partial(last_kernel, sizes, parts - 1, depth_cou...  2.71 us
    ppermute x2, starting transfers between devices, per_device(): arriving.append(lax.ppermute(group[1], 'depth', ahead))  2.58 us
  transfers between devices with their start and end apart: 7, of which 4 were waited for; matrix products, arithmetic and copies ran while one was open for 0% of the time, Pallas kernels for 22%

profile of v6, /device:TPU:6, one launch (start us, length us, event | category | flops | bytes accessed | tf_op | source)
XLA Modules:
  0.0 51.3 jit_solution(11732342660852405720)
XLA Ops:
  0.0 0.0 copy-start.1
  0.0 0.0 copy-start
  0.0 0.0 copy-start.3
  0.0 0.0 copy-start.2
  0.0 4.9 %first.1 = (f32[12,800,128]{2,1,0:T(8,128)S(1)}, bf16[8,3,128,256]{3,2,1,0:T(8,128)(2,1)S(1)}, f32[12,3,224,128]{3,2,1,0:T(8,128)S(1)}, f32[12,224,128]{2,1,0:T(...) custom-call(s32[12]{0:T(128)} %widths.5, ...), custom_call_target="tpu_custom_call" | custom-call | flops 1 | bytes 1 | tf_op jit(solution)/shard_map/first/pallas_call | solution.py:376
  5.0 1.3 %collective-permute-start.4 = (f32[7,224,128]{2,1,0:T(8,128)S(1)}, f32[7,224,128]{2,1,0:T(8,128)S(1)}, u32[]{:S(2)}, u32[]{:S(2)}) collective-permute-start(f32[7,224,128]{2,1,0:T(8,128)S(1)} %get-tuple-element.35), channel_id=1, source_target_pairs={{0,16},{1,17},{2,18},{3,19},{4,20},{5,21},{6,22},{7,23},{8,24},{9,... | collective-permute-start | bytes 2408456 | tf_op jit(solution)/shard_map/ppermute | solution.py:390
  6.3 0.1 collective-permute-start
  6.3 0.5 collective-permute-start.1
  6.8 2.1 %collective-permute-start.2 = (f32[6,144,128]{2,1,0:T(8,128)S(1)}, f32[6,144,128]{2,1,0:T(8,128)S(1)}, u32[]{:S(2)}, u32[]{:S(2)}) collective-permute-start(f32[6,144,128]{2,1,0:T(8,128)S(1)} %get-tuple-element.31), channel_id=1, source_target_pairs={{1,2},{2,1},{3,4},{4,3},{5,6},{6,5},{7,8},{8,7},{9,10},{10,9},{11,... | collective-permute-start | bytes 1327112 | tf_op jit(solution)/shard_map/ppermute | solution.py:391
  8.9 3.5 %collective-permute-start.3 = (f32[6,144,128]{2,1,0:T(8,128)S(1)}, f32[6,144,128]{2,1,0:T(8,128)S(1)}, u32[]{:S(2)}, u32[]{:S(2)}) collective-permute-start(f32[6,144,128]{2,1,0:T(8,128)S(1)} %get-tuple-element.34), channel_id=1, source_target_pairs={{1,2},{2,1},{3,4},{4,3},{5,6},{6,5},{7,8},{8,7},{9,10},{10,9},{11,... | collective-permute-start | bytes 1327112 | tf_op jit(solution)/shard_map/ppermute | solution.py:391
  12.4 0.0 collective-permute-done.refs_0_
  12.4 0.0 collective-permute-done.1.refs_1_
  12.4 0.0 copy-done.1
  12.4 0.0 copy-done
  12.4 0.0 copy-done.3
  12.5 0.0 copy-done.2
  12.5 3.0 %border.3 = (f32[12,800,128]{2,1,0:T(8,128)S(1)}, f32[12,3,144,128]{3,2,1,0:T(8,128)S(1)}, f32[12,144,128]{2,1,0:T(8,128)S(1)}, f32[7,144,128]{2,1,0:T(8,128)S(1)}) custom-call(s32[12]{0:T(128)S(1)} %copy-done.2, s32[12]{0:T(128)S(1)} %copy-done, f32[16]{0:T(128)S(1)} %copy-done.1, f32[16]{0:T(128)S(1)} %copy-done.3, ...), custom_call_target="tpu_custom_call", output_to_operand_aliasing={{0}: (5, {})} | custom-call | flops 1 | bytes 1 | tf_op jit(solution)/shard_map/border/pallas_call | solution.py:416
  15.5 1.3 %collective-permute-start.6 = (f32[7,144,128]{2,1,0:T(8,128)S(1)}, f32[7,144,128]{2,1,0:T(8,128)S(1)}, u32[]{:S(2)}, u32[]{:S(2)}) collective-permute-start(f32[7,144,128]{2,1,0:T(8,128)S(1)} %get-tuple-element.42), channel_id=1, source_target_pairs={{0,16},{1,17},{2,18},{3,19},{4,20},{5,21},{6,22},{7,23},{8,24},{9,... | collective-permute-start | bytes 1548296 | tf_op jit(solution)/shard_map/ppermute | solution.py:431
  16.8 9.1 %collective-permute-done.2.refs_0_ = f32[6,144,128]{2,1,0:T(8,128)S(1)} collective-permute-done((f32[6,144,128]{2,1,0:T(8,128)S(1)}, f32[6,144,128]{2,1,0:T(8,128)S(1)}, u32[]{:S(2)}, u32[]{:S(2)}) %collective-permute-start.2) | collective-permute-done | bytes 442400 | tf_op jit(solution)/shard_map/ppermute | solution.py:391
  25.9 1.8 %border.4 = (f32[12,800,128]{2,1,0:T(8,128)S(1)}, f32[12,3,144,128]{3,2,1,0:T(8,128)S(1)}) custom-call(s32[12]{0:T(128)S(1)} %copy-done.2, s32[12]{0:T(128)S(1)} %copy-done, f32[16]{0:T(128)S(1)} %copy-done.1, f32[16]{0:T(128)S(1)} %copy-done.3, bf16[8,3,128,256]{3,2,1,0:T(8,128)(2,1)S(1)} %get-tuple-element.26.band_ref, ...), custom_call_target="tpu_custom_call", output_to_operand_aliasing={{0}: (5, {})} | custom-call | flops 1 | bytes 1 | tf_op jit(solution)/shard_map/border/pallas_call | solution.py:416
  27.7 2.9 %collective-permute-done.3.refs_0_ = f32[6,144,128]{2,1,0:T(8,128)S(1)} collective-permute-done((f32[6,144,128]{2,1,0:T(8,128)S(1)}, f32[6,144,128]{2,1,0:T(8,128)S(1)}, u32[]{:S(2)}, u32[]{:S(2)}) %collective-permute-start.3) | collective-permute-done | bytes 442400 | tf_op jit(solution)/shard_map/ppermute | solution.py:391
  30.7 0.0 collective-permute-done.4.refs_1_.incoming
  30.7 1.8 %border.5 = (f32[12,800,128]{2,1,0:T(8,128)S(1)}, f32[12,3,144,128]{3,2,1,0:T(8,128)S(1)}, f32[12,144,128]{2,1,0:T(8,128)S(1)}, f32[7,144,128]{2,1,0:T(8,128)S(1)}) custom-call(s32[12]{0:T(128)S(1)} %copy-done.2, s32[12]{0:T(128)S(1)} %copy-done, f32[16]{0:T(128)S(1)} %copy-done.1, f32[16]{0:T(128)S(1)} %copy-done.3, ...), custom_call_target="tpu_custom_call", output_to_operand_aliasing={{0}: (5, {}), {1}: (6, {})} | custom-call | flops 1 | bytes 1 | tf_op jit(solution)/shard_map/border/pallas_call | solution.py:416
  32.5 1.3 %collective-permute-start.5 = (f32[7,144,128]{2,1,0:T(8,128)S(1)}, f32[7,144,128]{2,1,0:T(8,128)S(1)}, u32[]{:S(2)}, u32[]{:S(2)}) collective-permute-start(f32[7,144,128]{2,1,0:T(8,128)S(1)} %get-tuple-element.37), channel_id=1, source_target_pairs={{0,16},{1,17},{2,18},{3,19},{4,20},{5,21},{6,22},{7,23},{8,24},{9,... | collective-permute-start | bytes 1548296 | tf_op jit(solution)/shard_map/ppermute | solution.py:431
  33.8 1.9 %resume.2.refs_0_ = f32[12,224,128]{2,1,0:T(8,128)S(1)} custom-call(s32[12]{0:T(128)S(1)} %copy-done, f32[16]{0:T(128)S(1)} %copy-done.1, f32[12,3,224,128]{3,2,1,0:T(8,128)S(1)} %get-tuple-element.39.entry_ref, f32[7,224,128]{2,1,0:T(8,128)S(1)} %collective-permute-done.4.refs_1_.incoming, ...), custom_call_target="tpu_custom_call", output_to_operand_aliasing={{}: (4, {})} | custom-call | flops 1 | bytes 1 | tf_op jit(solution)/shard_map/resume/pallas_call | solution.py:398
  35.7 3.0 %collective-permute-done.6.incoming = f32[7,144,128]{2,1,0:T(8,128)S(1)} collective-permute-done((f32[7,144,128]{2,1,0:T(8,128)S(1)}, f32[7,144,128]{2,1,0:T(8,128)S(1)}, u32[]{:S(2)}, u32[]{:S(2)}) %collective-permute-start.6) | collective-permute-done | bytes 516128 | tf_op jit(solution)/shard_map/ppermute | solution.py:431
  38.7 1.4 %resume.3.refs_1_ = f32[12,144,128]{2,1,0:T(8,128)S(1)} custom-call(s32[12]{0:T(128)S(1)} %copy-done, f32[16]{0:T(128)S(1)} %copy-done.1, f32[12,3,144,128]{3,2,1,0:T(8,128)S(1)} %get-tuple-element.41.entry_ref, f32[7,144,128]{2,1,0:T(8,128)S(1)} %collective-permute-done.6.incoming, ...), custom_call_target="tpu_custom_call", output_to_operand_aliasing={{}: (4, {})} | custom-call | flops 1 | bytes 1 | tf_op jit(solution)/shard_map/resume/pallas_call | solution.py:398
  40.1 1.3 %early.1 = (f32[12,512,128]{2,1,0:T(8,128)S(1)}, f32[12,512,128]{2,1,0:T(8,128)}) custom-call(f32[12,224,128]{2,1,0:T(8,128)S(1)} %resume.2.refs_0_, f32[12,144,128]{2,1,0:T(8,128)S(1)} %resume.3.refs_1_), custom_call_target="tpu_custom_call" | custom-call | flops 1 | bytes 1 | tf_op jit(solution)/shard_map/early/pallas_call | solution.py:435
  41.4 7.2 %collective-permute-done.5.incoming = f32[7,144,128]{2,1,0:T(8,128)S(1)} collective-permute-done((f32[7,144,128]{2,1,0:T(8,128)S(1)}, f32[7,144,128]{2,1,0:T(8,128)S(1)}, u32[]{:S(2)}, u32[]{:S(2)}) %collective-permute-start.5) | collective-permute-done | bytes 516128 | tf_op jit(solution)/shard_map/ppermute | solution.py:431
  48.6 2.7 %last.1 = (f32[12,144,128]{2,1,0:T(8,128)S(1)}, f32[12,512,128]{2,1,0:T(8,128)S(1)}, f32[12,512,128]{2,1,0:T(8,128)}) custom-call(s32[12]{0:T(128)S(1)} %copy-done, f32[16]{0:T(128)S(1)} %copy-done.1, f32[12,3,144,128]{3,2,1,0:T(8,128)S(1)} %get-tuple-element.36.entry_ref, ...), custom_call_target="tpu_custom_call", output_to_operand_aliasing={{0}: (4, {}), {1}: (5, {}), {2}: (6, {})} | custom-call | flops 1 | bytes 1 | tf_op jit(solution)/shard_map/last/pallas_call | solution.py:445
Async XLA Ops:
  0.0 12.4 %copy-start.1 = (f32[16]{0:T(128)S(1)}, f32[16]{0:T(128)}, u32[]{:S(2)}) copy-start(f32[16]{0:T(128)} %near.11) | copy-start | bytes 196
  0.0 12.4 %copy-start = (s32[12]{0:T(128)S(1)}, s32[12]{0:T(128)}, u32[]{:S(2)}) copy-start(s32[12]{0:T(128)} %slots.11) | copy-start | bytes 148
  0.0 12.4 %copy-start.3 = (f32[16]{0:T(128)S(1)}, f32[16]{0:T(128)}, u32[]{:S(2)}) copy-start(f32[16]{0:T(128)} %lens.5) | copy-start | bytes 196
  0.0 12.4 %copy-start.2 = (s32[12]{0:T(128)S(1)}, s32[12]{0:T(128)}, u32[]{:S(2)}) copy-start(s32[12]{0:T(128)} %widths.5) | copy-start | bytes 148
  5.0 25.7 %collective-permute-start.4 = (f32[7,224,128]{2,1,0:T(8,128)S(1)}, f32[7,224,128]{2,1,0:T(8,128)S(1)}, u32[]{:S(2)}, u32[]{:S(2)}) collective-permute-start(f32[7,224,128]{2,1,0:T(8,128)S(1)} %get-tuple-element.35), channel_id=1, source_target_pairs={{0,16},{1,17},{2,18},{3,19},{4,20},{5,21},{6,22},{7,23},{8,24},{9,... | collective-permute-start | bytes 2408456 | tf_op jit(solution)/shard_map/ppermute | solution.py:390
  6.3 6.1 %collective-permute-start = (f32[6,144,128]{2,1,0:T(8,128)S(1)}, f32[6,144,128]{2,1,0:T(8,128)S(1)}, u32[]{:S(2)}, u32[]{:S(2)}) collective-permute-start(f32[6,144,128]{2,1,0:T(8,128)S(1)} %get-tuple-element.28), channel_id=1, source_target_pairs={{0,1},{1,0},{2,3},{3,2},{4,5},{5,4},{6,7},{7,6},{8,9},{9,8},{10,11... | collective-permute-start | bytes 1327112 | tf_op jit(solution)/shard_map/ppermute | solution.py:391
  6.3 6.1 %collective-permute-start.1 = (f32[6,144,128]{2,1,0:T(8,128)S(1)}, f32[6,144,128]{2,1,0:T(8,128)S(1)}, u32[]{:S(2)}, u32[]{:S(2)}) collective-permute-start(f32[6,144,128]{2,1,0:T(8,128)S(1)} %get-tuple-element.29), channel_id=1, source_target_pairs={{0,1},{1,0},{2,3},{3,2},{4,5},{5,4},{6,7},{7,6},{8,9},{9,8},{10,11... | collective-permute-start | bytes 1327112 | tf_op jit(solution)/shard_map/ppermute | solution.py:391
  6.8 19.1 %collective-permute-start.2 = (f32[6,144,128]{2,1,0:T(8,128)S(1)}, f32[6,144,128]{2,1,0:T(8,128)S(1)}, u32[]{:S(2)}, u32[]{:S(2)}) collective-permute-start(f32[6,144,128]{2,1,0:T(8,128)S(1)} %get-tuple-element.31), channel_id=1, source_target_pairs={{1,2},{2,1},{3,4},{4,3},{5,6},{6,5},{7,8},{8,7},{9,10},{10,9},{11,... | collective-permute-start | bytes 1327112 | tf_op jit(solution)/shard_map/ppermute | solution.py:391
  8.9 21.7 %collective-permute-start.3 = (f32[6,144,128]{2,1,0:T(8,128)S(1)}, f32[6,144,128]{2,1,0:T(8,128)S(1)}, u32[]{:S(2)}, u32[]{:S(2)}) collective-permute-start(f32[6,144,128]{2,1,0:T(8,128)S(1)} %get-tuple-element.34), channel_id=1, source_target_pairs={{1,2},{2,1},{3,4},{4,3},{5,6},{6,5},{7,8},{8,7},{9,10},{10,9},{11,... | collective-permute-start | bytes 1327112 | tf_op jit(solution)/shard_map/ppermute | solution.py:391
  15.5 23.2 %collective-permute-start.6 = (f32[7,144,128]{2,1,0:T(8,128)S(1)}, f32[7,144,128]{2,1,0:T(8,128)S(1)}, u32[]{:S(2)}, u32[]{:S(2)}) collective-permute-start(f32[7,144,128]{2,1,0:T(8,128)S(1)} %get-tuple-element.42), channel_id=1, source_target_pairs={{0,16},{1,17},{2,18},{3,19},{4,20},{5,21},{6,22},{7,23},{8,24},{9,... | collective-permute-start | bytes 1548296 | tf_op jit(solution)/shard_map/ppermute | solution.py:431
  32.5 16.1 %collective-permute-start.5 = (f32[7,144,128]{2,1,0:T(8,128)S(1)}, f32[7,144,128]{2,1,0:T(8,128)S(1)}, u32[]{:S(2)}, u32[]{:S(2)}) collective-permute-start(f32[7,144,128]{2,1,0:T(8,128)S(1)} %get-tuple-element.37), channel_id=1, source_target_pairs={{0,16},{1,17},{2,18},{3,19},{4,20},{5,21},{6,22},{7,23},{8,24},{9,... | collective-permute-start | bytes 1548296 | tf_op jit(solution)/shard_map/ppermute | solution.py:431

commit v7 on v6

--- a/solution.py
+++ b/solution.py
@@ -11,6 +11,7 @@
 RIM = WMAX + 1
 LANES = 128
 SUB = 8
+INNER_ROWS, FINAL_ROWS = 9, 4
 TOGETHER = 4
 PARTS = (3, 2, 2)
 BORDER_SHARES = (((0, 1),), ((0,), (1,)))
@@ -22,19 +23,30 @@
 
 
 def group_sizes(row_count):
-    return (row_count - 2 * RIM, RIM, RIM)
+    return (INNER_ROWS, row_count - 2 * RIM - INNER_ROWS, RIM, RIM)
+
+
+def is_even():
+    return lax.rem(lax.axis_index("sky"), 2) == 0
+
+
+def pieces_of(row_count):
+    sizes = group_sizes(row_count)
+    even = is_even()
+    split_last = [(jnp.where(even, FINAL_ROWS, 0), RIM - FINAL_ROWS), (jnp.where(even, 0, RIM - FINAL_ROWS), FINAL_ROWS)]
+    return [(part, 0, count) for part, count in enumerate(sizes[:-1])] + [(len(sizes) - 1, *one) for one in split_last]
 
 
 def side_starts(row_count):
     low, high = (0, -RIM), (row_count - RIM, row_count)
-    even = lax.rem(lax.axis_index("sky"), 2) == 0
+    even = is_even()
     paired = [jnp.where(even, b, a) for a, b in zip(low, high)]
     other = [jnp.where(even, a, b) for a, b in zip(low, high)]
     return paired, other
 
 
 def first_row(row_count, part):
-    return RIM if part == 0 else side_starts(row_count)[part - 1][0]
+    return (RIM, RIM + INNER_ROWS)[part] if part < 2 else side_starts(row_count)[part - 2][0]
 
 
 def split(value, parts):
@@ -85,9 +97,9 @@
                 left_ref[field, here, part * LANES:(part + 1) * LANES] = piece
 
 
-def multiply(half_width, field, band_ref, left_ref):
+def multiply(half_width, field, length, band_ref, left_ref):
     weight = jnp.concatenate([band_ref[half_width - 1, field]] * PARTS[field], axis=0)
-    return jnp.dot(left_ref[field, :, :PARTS[field] * LANES], weight, preferred_element_type=F32)
+    return jnp.dot(left_ref[field, :length, :PARTS[field] * LANES], weight, preferred_element_type=F32)
 
 
 def combine(k, field, near, scale, blocks, product, beside_ref, entry_ref):
@@ -104,12 +116,13 @@
         entry_ref[k, field, pl.ds(at * blocks, blocks), :] = value if field == 1 else value + near
 
 
-def sweep(planes, length, near_of, entry_ref, conv_ref, start, finish):
+def sweep(planes, base, length, near_of, entry_ref, conv_ref, start, finish):
     step = next(count * SUB for count in (4, 3, 2, 1) if length % (count * SUB) == 0)
 
     def part(index, carry):
-        where = pl.ds(pl.multiple_of(index * step, step), step)
-        now, then = (None, None) if start is None else start(where)
+        own = pl.ds(pl.multiple_of(index * step, SUB), step)
+        where = pl.ds(pl.multiple_of(base + index * step, SUB), step)
+        now, then = (None, None) if start is None else start(own)
         for k in range(planes):
             xx, xy, yy = [entry_ref[k, i, where, :] for i in range(3)]
             kept = 1.0 - near_of(k)
@@ -131,7 +144,7 @@
             now = new
             conv_ref[k, where, :] = 1.0 - 0.5 * (new[0] + new[3])
         if finish is not None:
-            finish(where, now + then)
+            finish(own, now + then)
         return carry
 
     lax.fori_loop(0, length // step, part, 0)
@@ -183,7 +196,7 @@
     return count // per, per
 
 
-def group_stage(sizes, part, scalars, x_ref, band_ref, scratch, entry_ref, conv_ref, state_ref, before_plane,
+def group_stage(sizes, part, scalars, x_ref, band_ref, scratch, entry_ref, before_plane=None,
                 shares=tuple(range(SHARES))):
     planes, rows, blocks = sizes
     widths, slots, near, lens = scalars
@@ -199,22 +212,33 @@
             for share in shares:
                 place = index * per + i
                 ks.append(place * SHARES + share)
-                before_plane(share, place, ks[-1])
+                if before_plane is not None:
+                    before_plane(share, place, ks[-1])
         for k, left_ref in zip(ks, left_refs):
             build(k, widths[k], first, count, blocks, x_ref, left_ref)
         for field in range(3):
             for k, left_ref, beside_ref in zip(ks, left_refs, beside_refs):
                 width = (2 * widths[k] + 1).astype(F32)
                 combine(k, field, near[slots[k]], lens[slots[k]] / (width * width), blocks,
-                        multiply(widths[k], field, band_ref, left_ref), beside_ref, entry_ref)
+                        multiply(widths[k], field, count * blocks, band_ref, left_ref), beside_ref, entry_ref)
         return carry
 
     lax.fori_loop(0, steps, step, 0)
-    if shares[-1] == SHARES - 1:
-
-        @pl.when(lax.axis_index("depth") == 0)
-        def _():
-            sweep(planes, group_sizes(rows)[part] * blocks, lambda k: near[slots[k]], entry_ref, conv_ref, None,
+
+
+def is_first():
+    return lax.axis_index("depth") == 0
+
+
+def first_sweep(sizes, part, scalars, entry_ref, conv_ref, state_refs):
+    planes, rows, blocks = sizes
+    widths, slots, near, lens = scalars
+    pieces = [(base, count) for group, base, count in pieces_of(rows) if group == part]
+
+    @pl.when(is_first())
+    def _():
+        for (base, count), state_ref in zip(pieces, state_refs):
+            sweep(planes, base * blocks, count * blocks, lambda k: near[slots[k]], entry_ref, conv_ref, None,
                   writer(state_ref))
 
 
@@ -248,53 +272,82 @@
         for i, side in enumerate(sides):
             sends[i * SHARES + share][place] = x_ref[k, pl.ds(pl.multiple_of(side, blocks), RIM * blocks), :]
 
-    group_stage(sizes, 0, (widths, slots, near, lens), x_ref, band_ref, scratch, entry_ref, conv_ref, state_ref, arrive)
-
-
-def border_kernel(sizes, part, shares, widths, slots, near, lens, band_ref, x_in, entry_in, *refs):
-    planes, rows, blocks = sizes
-    arrived, refs = refs[:len(shares)], refs[len(shares):]
-    last = shares[-1] == SHARES - 1
-    outputs = 4 if last else 2
-    scratch_count = 2 * len(shares) * steps_of(planes, shares)[1]
-    refs, scratch = refs[-outputs - scratch_count:-scratch_count], refs[-scratch_count:]
-    x_ref, entry_ref, conv_ref, state_ref = (*refs, None, None)[:4]
-    start = side_starts(rows)[part - 1][1] + RIM
+    scalars = (widths, slots, near, lens)
+
+    @pl.when(is_first())
+    def _():
+        group_stage(sizes, 0, scalars, x_ref, band_ref, scratch, entry_ref, arrive)
+
+    @pl.when(jnp.logical_not(is_first()))
+    def _():
+        def place(index, carry):
+            for share in range(SHARES):
+                arrive(share, index, index * SHARES + share)
+            return carry
+
+        lax.fori_loop(0, planes // SHARES, place, 0)
+
+    first_sweep(sizes, 0, scalars, entry_ref, conv_ref, [state_ref])
+
+
+def second_kernel(sizes, widths, slots, near, lens, band_ref, x_ref, entry_ref, conv_ref, state_ref, *scratch):
+    scalars = (widths, slots, near, lens)
+    group_stage(sizes, 1, scalars, x_ref, band_ref, scratch, entry_ref)
+    first_sweep(sizes, 1, scalars, entry_ref, conv_ref, [state_ref])
+
+
+def border_kernel(sizes, part, shares, counts, widths, slots, near, lens, band_ref, x_in, *refs):
+    planes, rows, blocks = sizes
+    handed, results, _ = counts
+    refs = refs[handed:]
+    arrived, refs = refs[:len(shares)], refs[len(shares) + counts[2]:]
+    (x_ref, entry_ref, *made), scratch = refs[:results], refs[results:]
+    start = side_starts(rows)[part - 2][1] + RIM
+    scalars = (widths, slots, near, lens)
 
     def arrive(share, place, k):
         x_ref[k, pl.ds(pl.multiple_of(start * blocks, blocks), RIM * blocks), :] = arrived[shares.index(share)][place]
 
-    group_stage(sizes, part, (widths, slots, near, lens), x_ref, band_ref, scratch, entry_ref, conv_ref, state_ref, arrive,
-                shares)
-
-
-def resume(sizes, part, turn, slots, near, entry_ref, incoming, conv_ref, finish):
-    planes, rows, blocks = sizes
+    group_stage(sizes, part, scalars, x_ref, band_ref, scratch, entry_ref, arrive, shares)
+    if shares[-1] == SHARES - 1:
+        first_sweep(sizes, part, scalars, entry_ref, made[0], made[1:])
+    elif shares[0] == 0:
+        @pl.when(jnp.logical_not(is_first()))
+        def _():
+            for share in range(SHARES):
+                group_stage(sizes, 0, scalars, x_ref, band_ref, scratch, made[0], None, (share,))
+
+
+def resume(sizes, piece, turn, slots, near, entry_ref, incoming, conv_ref, finish):
+    planes, rows, blocks = sizes
+    part, base, count = pieces_of(rows)[piece]
 
     @pl.when(lax.axis_index("depth") == turn)
     def _():
-        sweep(planes, group_sizes(rows)[part] * blocks, lambda k: near[slots[k]], entry_ref, conv_ref,
+        sweep(planes, base * blocks, count * blocks, lambda k: near[slots[k]], entry_ref, conv_ref,
               lambda where: unpacked_state([incoming[i, where, :] for i in range(SENT)]), finish)
 
 
-def resume_kernel(sizes, part, turn, slots, near, entry_ref, incoming, conv_in, conv_ref, *state_ref):
-    resume(sizes, part, turn, slots, near, entry_ref, incoming, conv_ref, writer(state_ref[0]) if state_ref else None)
-
-
-def place_rows(sizes, part, k, conv_ref, tiles_ref):
-    planes, rows, blocks = sizes
-    start = first_row(rows, part)
-    for i in range(group_sizes(rows)[part]):
+def resume_kernel(sizes, piece, turn, slots, near, entry_ref, incoming, conv_in, behind, conv_ref, *state_ref):
+    resume(sizes, piece, turn, slots, near, entry_ref, incoming, conv_ref, writer(state_ref[0]) if state_ref else None)
+
+
+def place_rows(sizes, piece, k, conv_ref, tiles_ref):
+    planes, rows, blocks = sizes
+    part, base, count = pieces_of(rows)[piece]
+    start = first_row(rows, part) + base
+    for i in range(count):
         row = start + i
         for half in range(blocks // SUB):
             to = lax.div(row, SUB) * SUB * blocks + half * SUB * SUB + lax.rem(row, SUB)
-            tiles_ref[k, pl.ds(to, SUB, stride=SUB), :] = conv_ref[k, pl.ds(i * blocks + half * SUB, SUB), :]
+            at = (base + i) * blocks + half * SUB
+            tiles_ref[k, pl.ds(to, SUB, stride=SUB), :] = conv_ref[k, pl.ds(pl.multiple_of(at, SUB), SUB), :]
 
 
 def write_out(sizes, late, tiles_ref, out_hbm, sems, before_plane):
     planes, rows, blocks = sizes
-    even = lax.rem(lax.axis_index("sky"), 2) == 0
-    tail = -(-RIM // SUB) * SUB
+    even = is_even()
+    tail = -(-FINAL_ROWS // SUB) * SUB
     if late:
         start, count = jnp.where(even, 0, rows - tail), tail
     else:
@@ -318,23 +371,25 @@
     *conv_refs, tiles_ref, out_hbm, sems = refs
 
     def place(k):
-        for part, conv_ref in enumerate(conv_refs):
-            place_rows(sizes, part, k, conv_ref, tiles_ref)
+        for piece, (part, _, _) in enumerate(pieces_of(sizes[1])[:-1]):
+            place_rows(sizes, piece, k, conv_refs[part], tiles_ref)
 
     write_out(sizes, False, tiles_ref, out_hbm, sems, place)
 
 
-def last_kernel(sizes, part, turn, slots, near, entry_ref, incoming, conv_in, tiles_in, out_in, conv_ref, tiles_ref,
+def last_kernel(sizes, piece, turn, slots, near, entry_ref, incoming, conv_in, tiles_in, out_in, conv_ref, tiles_ref,
                 out_hbm, sems):
-    resume(sizes, part, turn, slots, near, entry_ref, incoming, conv_ref, None)
-    write_out(sizes, True, tiles_ref, out_hbm, sems, lambda k: place_rows(sizes, part, k, conv_ref, tiles_ref))
+    resume(sizes, piece, turn, slots, near, entry_ref, incoming, conv_ref, None)
+    write_out(sizes, True, tiles_ref, out_hbm, sems, lambda k: place_rows(sizes, piece, k, conv_ref, tiles_ref))
 
 
 def per_device(potential, widths, plane_slot, ratio_near, ratio_lens):
     planes, rows, cols = potential.shape
     blocks = cols // LANES
     sizes = (planes, rows, blocks)
-    parts = len(group_sizes(rows))
+    counts = group_sizes(rows)
+    parts = len(counts)
+    pieces = [(part, count) for part, _, count in pieces_of(rows)]
     depth_count, sky_count = lax.axis_size("depth"), lax.axis_size("sky")
     swaps = [[pair for i in range(first, sky_count - 1, 2) for pair in ((i, i + 1), (i + 1, i))] for first in (0, 1)]
     ahead = [(i, i + 1) for i in range(depth_count - 1)]
@@ -363,19 +418,27 @@
     x_shape = held(planes, (rows + 2 * RIM) * blocks, LANES)
     band_shape = held(WMAX, 3, LANES, 2 * LANES, dtype=BF16)
 
+    def entry_shape(part):
+        return held(planes, 3, counts[part] * blocks, LANES)
+
+    def conv_shape(part):
+        return held(planes, counts[part] * blocks, LANES)
+
+    def state_shape(piece):
+        return moved(SENT, pieces[piece][1] * blocks, LANES)
+
     def group_shapes(part):
-        length = group_sizes(rows)[part] * blocks
-        return [held(planes, 3, length, LANES), held(planes, length, LANES), moved(SENT, length, LANES)]
+        return [conv_shape(part), *[state_shape(piece) for piece, (group, _) in enumerate(pieces) if group == part]]
 
     def group_scratch(part, shares):
-        count = group_sizes(rows)[part]
+        count = max(counts[0], counts[part]) if part > 1 else counts[part]
         return [held(3, count * blocks, max(PARTS) * LANES, dtype=BF16),
                 held(3, (count + 1) * (blocks + SUB), LANES)] * (len(shares) * steps_of(planes, shares)[1])
 
     side = moved(planes // SHARES, RIM * blocks, LANES)
     x, bands, *rest = pl.pallas_call(
         functools.partial(first_kernel, sizes),
-        out_shape=[x_shape, band_shape, *group_shapes(0), *[side] * (2 * SHARES)],
+        out_shape=[x_shape, band_shape, entry_shape(0), *group_shapes(0), *[side] * (2 * SHARES)],
         in_specs=[anywhere] * 5,
         out_specs=[vmem] * (5 + 2 * SHARES),
         scratch_shapes=[
@@ -385,66 +448,79 @@
         cost_estimate=cost,
         name="first",
     )(*[in_hbm(array) for array in (*scalars, tiled)])
-    group, sends = rest[:3], rest[3:]
-    made = [group]
-    arriving = [lax.ppermute(group[2], "depth", ahead)]
+    (entry, conv, state), sends = rest[:3], rest[3:]
+    convs, arriving = [conv], [lax.ppermute(state, "depth", ahead)]
     swapped = [[lax.ppermute(piece, "sky", swap) for piece in sends[i * SHARES:(i + 1) * SHARES]]
                for i, swap in enumerate(swaps)]
-    entries, convs = [group[0] for group in made], [group[1] for group in made]
-    out_shape = moved(planes, rows * blocks, LANES)
-
-    def resumed(part, turn):
-        last = turn == depth_count - 1
-        convs[part], *state = pl.pallas_call(
-            functools.partial(resume_kernel, sizes, part, turn),
-            out_shape=group_shapes(part)[1:2] + ([] if last else group_shapes(part)[2:3]),
-            in_specs=[smem] * 2 + [vmem] * 3,
-            out_specs=[vmem] * (1 if last else 2),
-            input_output_aliases={4: 0},
-            compiler_params=params,
-            cost_estimate=cost,
-            name="resume",
-        )(plane_slot, ratio_near, in_vmem(entries[part]), arriving[part], in_vmem(convs[part]))
-        if state:
-            arriving[part] = lax.ppermute(state[0], "depth", ahead)
-
-    for part in range(1, parts):
+    entries = [entry]
+    entry, conv, state = pl.pallas_call(
+        functools.partial(second_kernel, sizes),
+        out_shape=[entry_shape(1), *group_shapes(1)],
+        in_specs=[smem] * 4 + [vmem] * 2,
+        out_specs=[vmem] * 3,
+        scratch_shapes=group_scratch(1, range(SHARES)),
+        compiler_params=params,
+        cost_estimate=cost,
+        name="second",
+    )(*scalars, in_vmem(bands), in_vmem(x))
+    entries.append(entry)
+    convs.append(conv)
+    arriving.append(lax.ppermute(state, "depth", ahead))
+    for part in range(2, parts):
         entry = None
-        for shares in BORDER_SHARES[part - 1]:
+        for shares in BORDER_SHARES[part - 2]:
             last = shares[-1] == SHARES - 1
-            behind = arriving[:1] if last and part > 1 else []
+            behind = [] if part == 2 else [] if last else arriving[:2]
+            handed = ([] if entry is None else [entry]) + ([] if last else entries[:1])
+            shapes = [x_shape, entry_shape(part), *([] if last else [entry_shape(0)]), *(group_shapes(part) if last else [])]
             x, entry, *group = pl.pallas_call(
-                functools.partial(border_kernel, sizes, part, shares),
-                out_shape=[x_shape, *group_shapes(part)[:3 if last else 1]],
-                in_specs=[smem] * 4 + [vmem] * 2 + [anywhere if entry is None else vmem] + [vmem] * len(shares)
-                + [anywhere] * len(behind),
-                out_specs=[vmem] * (4 if last else 2),
+                functools.partial(border_kernel, sizes, part, shares, (len(handed), len(shapes), len(behind))),
+                out_shape=shapes,
+                in_specs=[smem] * 4 + [vmem] * (2 + len(handed) + len(shares)) + [anywhere] * len(behind),
+                out_specs=[vmem] * len(shapes),
                 scratch_shapes=group_scratch(part, shares),
-                input_output_aliases={5: 0} if entry is None else {5: 0, 6: 1},
+                input_output_aliases={5: 0} | ({} if entry is None else {6: 1}) | ({} if last else {5 + len(handed): 2}),
                 compiler_params=params,
                 cost_estimate=cost,
                 name="border",
-            )(*scalars, in_vmem(bands), in_vmem(x), plane_slot if entry is None else in_vmem(entry),
-              *[swapped[part - 1][share] for share in shares], *behind)
+            )(*scalars, in_vmem(bands), in_vmem(x), *map(in_vmem, handed), *[swapped[part - 2][share] for share in shares],
+              *behind)
+            if not last:
+                entries[0] = group[0]
         entries.append(entry)
         convs.append(group[0])
-        arriving.append(lax.ppermute(group[1], "depth", ahead))
+        arriving += [lax.ppermute(state, "depth", ahead) for state in group[1:]]
+
     for turn in range(1, depth_count):
-        for part in range(parts - (turn == depth_count - 1)):
-            resumed(part, turn)
+        last = turn == depth_count - 1
+        for piece, (part, _) in enumerate(pieces[:len(pieces) - last]):
+            convs[part], *state = pl.pallas_call(
+                functools.partial(resume_kernel, sizes, piece, turn),
+                out_shape=[conv_shape(part)] + ([] if last else [state_shape(piece)]),
+                in_specs=[smem] * 2 + [vmem] * 4,
+                out_specs=[vmem] * (1 if last else 2),
+                input_output_aliases={4: 0},
+                compiler_params=params,
+                cost_estimate=cost,
+                name="resume",
+            )(plane_slot, ratio_near, in_vmem(entries[part]), arriving[piece], in_vmem(convs[part]),
+              in_vmem(convs[part - 1]))
+            if state:
+                arriving[piece] = lax.ppermute(state[0], "depth", ahead)
+    out_shape = moved(planes, rows * blocks, LANES)
     tiles, out = pl.pallas_call(
         functools.partial(early_kernel, sizes),
         out_shape=[held(planes, rows * blocks, LANES), out_shape],
-        in_specs=[vmem] * (parts - 1),
+        in_specs=[vmem] * parts,
         out_specs=[vmem, anywhere],
         scratch_shapes=[dma((planes,))],
         compiler_params=params,
         cost_estimate=cost,
         name="early",
-    )(*[in_vmem(conv) for conv in convs[:-1]])
+    )(*[in_vmem(conv) for conv in convs])
     conv, tiles, out = pl.pallas_call(
-        functools.partial(last_kernel, sizes, parts - 1, depth_count - 1),
-        out_shape=[group_shapes(parts - 1)[1], held(planes, rows * blocks, LANES), out_shape],
+        functools.partial(last_kernel, sizes, len(pieces) - 1, depth_count - 1),
+        out_shape=[conv_shape(parts - 1), held(planes, rows * blocks, LANES), out_shape],
         in_specs=[smem] * 2 + [vmem] * 4 + [anywhere],
         out_specs=[vmem, vmem, anywhere],
         scratch_shapes=[dma((planes,))],

time: 51.6 us -> 49.7 us (0.963)
  waiting for transfers between devices: 22.2 us -> 14.9 us
  Pallas kernels: 18.9 us -> 21.8 us
  starting transfers between devices: 9.99 us -> 12.6 us
    ppermute x4, waiting for transfers between devices: 12.1 us -> 0.01 us  [per_device(): lax.ppermute(piece, 'sky', swap)]
    pallas_call x6 -> x9, Pallas kernels: 12.7 us -> 18.1 us  [the longest x3 8.91 us: per_device(): pl.pallas_call(functools.partial(border_kernel, sizes, part, shares, (len...]
    ppermute x3 -> x5, waiting for transfers between devices: 10.1 us -> 14.9 us  [the longest x1 8.32 us: per_device(): arriving.append(lax.ppermute(state, 'depth', ahead))]
    pallas_call x1, Pallas kernels: 4.93 us -> 2.06 us  [per_device(): pl.pallas_call(functools.partial(first_kernel, sizes), out_shape=[x_shape...]
    ppermute x3 -> x5, starting transfers between devices: 3.88 us -> 6.45 us  [the longest x3 3.88 us: per_device(): arriving += [lax.ppermute(state, 'depth', ahead) for state in group[1:]]]
  transfers between devices with their start and end apart: 7 -> 9, of which waited for: 4 -> 3; matrix products, arithmetic and copies ran while one was open for 0% -> 0% of each run, Pallas kernels for 22% -> 36%
where the time goes in v7:
time: 49.7 us; the launch traced here: 49.5 us
  Pallas kernels  21.8 us (44%)
  waiting for transfers between devices  14.9 us (30%)
  starting transfers between devices  12.6 us (25%)
    pallas_call x3, Pallas kernels, per_device(): pl.pallas_call(functools.partial(border_kernel, sizes, part, shares, (len...  8.91 us
    ppermute x1, waiting for transfers between devices, per_device(): arriving.append(lax.ppermute(state, 'depth', ahead))  8.32 us
    ppermute x3, waiting for transfers between devices, per_device(): arriving += [lax.ppermute(state, 'depth', ahead) for state in group[1:]]  6.56 us
    ppermute x4, starting transfers between devices, per_device(): lax.ppermute(piece, 'sky', swap)  6.13 us
    pallas_call x4, Pallas kernels, per_device(): pl.pallas_call(functools.partial(resume_kernel, sizes, piece, turn), out_...  5.01 us
    ppermute x3, starting transfers between devices, per_device(): arriving += [lax.ppermute(state, 'depth', ahead) for state in group[1:]]  3.88 us
    pallas_call x1, Pallas kernels, per_device(): pl.pallas_call(functools.partial(second_kernel, sizes), out_shape=[entry_...  2.25 us
    pallas_call x1, Pallas kernels, per_device(): pl.pallas_call(functools.partial(first_kernel, sizes), out_shape=[x_shape...  2.06 us
  transfers between devices with their start and end apart: 9, of which 3 were waited for; matrix products, arithmetic and copies ran while one was open for 0% of the time, Pallas kernels for 36%

profile of v7, /device:TPU:6, one launch (start us, length us, event | category | flops | bytes accessed | tf_op | source)
XLA Modules:
  0.0 49.5 jit_solution(9400615474187110791)
XLA Ops:
  0.0 0.0 copy-start.1
  0.0 0.0 copy-start
  0.0 0.0 copy-start.3
  0.0 0.0 copy-start.2
  0.0 2.1 %first.1 = (f32[12,800,128]{2,1,0:T(8,128)S(1)}, bf16[8,3,128,256]{3,2,1,0:T(8,128)(2,1)S(1)}, f32[12,3,144,128]{3,2,1,0:T(8,128)S(1)}, f32[12,144,128]{2,1,0:T(...) custom-call(s32[12]{0:T(128)} %widths.7, ...), custom_call_target="tpu_custom_call" | custom-call | flops 1 | bytes 1 | tf_op jit(solution)/shard_map/first/pallas_call | solution.py:439
  2.1 0.1 collective-permute-start
  2.2 0.5 %collective-permute-start.1 = (f32[6,144,128]{2,1,0:T(8,128)S(1)}, f32[6,144,128]{2,1,0:T(8,128)S(1)}, u32[]{:S(2)}, u32[]{:S(2)}) collective-permute-start(f32[6,144,128]{2,1,0:T(8,128)S(1)} %get-tuple-element.34), channel_id=1, source_target_pairs={{0,1},{1,0},{2,3},{3,2},{4,5},{5,4},{6,7},{7,6},{8,9},{9,8},{10,11... | collective-permute-start | bytes 1327112 | tf_op jit(solution)/shard_map/ppermute | solution.py:453
  2.7 1.3 %collective-permute-start.3 = (f32[7,144,128]{2,1,0:T(8,128)S(1)}, f32[7,144,128]{2,1,0:T(8,128)S(1)}, u32[]{:S(2)}, u32[]{:S(2)}) collective-permute-start(f32[7,144,128]{2,1,0:T(8,128)S(1)} %get-tuple-element.38), channel_id=1, source_target_pairs={{0,16},{1,17},{2,18},{3,19},{4,20},{5,21},{6,22},{7,23},{8,24},{9,... | collective-permute-start | bytes 1548296 | tf_op jit(solution)/shard_map/ppermute | solution.py:452
  4.0 2.1 %collective-permute-start.2 = (f32[6,144,128]{2,1,0:T(8,128)S(1)}, f32[6,144,128]{2,1,0:T(8,128)S(1)}, u32[]{:S(2)}, u32[]{:S(2)}) collective-permute-start(f32[6,144,128]{2,1,0:T(8,128)S(1)} %get-tuple-element.37), channel_id=1, source_target_pairs={{1,2},{2,1},{3,4},{4,3},{5,6},{6,5},{7,8},{8,7},{9,10},{10,9},{11,... | collective-permute-start | bytes 1327112 | tf_op jit(solution)/shard_map/ppermute | solution.py:453
  6.1 3.5 %collective-permute-start.5 = (f32[6,144,128]{2,1,0:T(8,128)S(1)}, f32[6,144,128]{2,1,0:T(8,128)S(1)}, u32[]{:S(2)}, u32[]{:S(2)}) collective-permute-start(f32[6,144,128]{2,1,0:T(8,128)S(1)} %get-tuple-element.42), channel_id=1, source_target_pairs={{1,2},{2,1},{3,4},{4,3},{5,6},{6,5},{7,8},{8,7},{9,10},{10,9},{11,... | collective-permute-start | bytes 1327112 | tf_op jit(solution)/shard_map/ppermute | solution.py:453
  9.5 0.0 copy-done.1
  9.5 0.0 copy-done
  9.6 0.0 copy-done.3
  9.6 0.0 copy-done.2
  9.6 2.3 %second.1 = (f32[12,3,80,128]{3,2,1,0:T(8,128)S(1)}, f32[12,80,128]{2,1,0:T(8,128)S(1)}, f32[7,80,128]{2,1,0:T(8,128)S(1)}) custom-call(s32[12]{0:T(128)S(1)} %copy-done.2, s32[12]{0:T(128)S(1)} %copy-done, f32[16]{0:T(128)S(1)} %copy-done.1, f32[16]{0:T(128)S(1)} %copy-done.3, bf16[8,3,128,256]{3,2,1,0:T(8,128)(2,1)S(1)} %get-tuple-element.31.band_ref, ...), custom_call_target="tpu_custom_call" | custom-call | flops 1 | bytes 1 | tf_op jit(solution)/shard_map/second/pallas_call | solution.py:456
  11.8 0.0 collective-permute-done.refs_0_
  11.8 1.3 %collective-permute-start.4 = (f32[7,80,128]{2,1,0:T(8,128)S(1)}, f32[7,80,128]{2,1,0:T(8,128)S(1)}, u32[]{:S(2)}, u32[]{:S(2)}) collective-permute-start(f32[7,80,128]{2,1,0:T(8,128)S(1)} %get-tuple-element.39), channel_id=1, source_target_pairs={{0,16},{1,17},{2,18},{3,19},{4,20},{5,21},{6,22},{7,23},{8,24},{9,... | collective-permute-start | bytes 860168 | tf_op jit(solution)/shard_map/ppermute | solution.py:468
  13.1 0.0 collective-permute-done.1.refs_1_
  13.2 3.0 %border.3 = (f32[12,800,128]{2,1,0:T(8,128)S(1)}, f32[12,3,144,128]{3,2,1,0:T(8,128)S(1)}, f32[12,144,128]{2,1,0:T(8,128)S(1)}, f32[7,144,128]{2,1,0:T(8,128)S(1)}) custom-call(s32[12]{0:T(128)S(1)} %copy-done.2, s32[12]{0:T(128)S(1)} %copy-done, f32[16]{0:T(128)S(1)} %copy-done.1, f32[16]{0:T(128)S(1)} %copy-done.3, ...), custom_call_target="tpu_custom_call", output_to_operand_aliasing={{0}: (5, {})} | custom-call | flops 1 | bytes 1 | tf_op jit(solution)/shard_map/border/pallas_call | solution.py:476
  16.2 1.3 %collective-permute-start.8 = (f32[7,144,128]{2,1,0:T(8,128)S(1)}, f32[7,144,128]{2,1,0:T(8,128)S(1)}, u32[]{:S(2)}, u32[]{:S(2)}) collective-permute-start(f32[7,144,128]{2,1,0:T(8,128)S(1)} %get-tuple-element.48), channel_id=1, source_target_pairs={{0,16},{1,17},{2,18},{3,19},{4,20},{5,21},{6,22},{7,23},{8,24},{9,... | collective-permute-start | bytes 1548296 | tf_op jit(solution)/shard_map/ppermute | solution.py:492
  17.5 8.3 %collective-permute-done.4.refs_3_.incoming = f32[7,80,128]{2,1,0:T(8,128)S(1)} collective-permute-done((f32[7,80,128]{2,1,0:T(8,128)S(1)}, f32[7,80,128]{2,1,0:T(8,128)S(1)}, u32[]{:S(2)}, u32[]{:S(2)}) %collective-permute-start.4) | collective-permute-done | bytes 286752 | tf_op jit(solution)/shard_map/ppermute | solution.py:468
  25.8 0.0 collective-permute-done.2.refs_1_
  25.8 0.0 collective-permute-done.3.refs_2_.incoming
  25.8 4.1 %border.4 = (f32[12,800,128]{2,1,0:T(8,128)S(1)}, f32[12,3,144,128]{3,2,1,0:T(8,128)S(1)}, f32[12,3,144,128]{3,2,1,0:T(8,128)S(1)}) custom-call(s32[12]{0:T(128)S(1)} %copy-done.2, s32[12]{0:T(128)S(1)} %copy-done, f32[16]{0:T(128)S(1)} %copy-done.1, f32[16]{0:T(128)S(1)} %copy-done.3, ...), custom_call_target="tpu_custom_call", output_to_operand_aliasing={{0}: (5, {}), {2}: (6, {})} | custom-call | flops 1 | bytes 1 | tf_op jit(solution)/shard_map/border/pallas_call | solution.py:476
  29.9 0.0 collective-permute-done.5.refs_1_
  29.9 1.8 %border.5 = (f32[12,800,128]{2,1,0:T(8,128)S(1)}, f32[12,3,144,128]{3,2,1,0:T(8,128)S(1)}, f32[12,144,128]{2,1,0:T(8,128)S(1)}, f32[7,80,128]{2,1,0:T(8,128)S(1)}, f32[7,64,128]{2,1,0:T(8,128)S(1)}) custom-call(s32[12]{0:T(128)S(1)} %copy-done.2, s32[12]{0:T(128)S(1)} %copy-done, f32[16]{0:T(128)S(1)} %copy-done.1, ...), custom_call_target="tpu_custom_call", output_to_operand_aliasing={{0}: (5, {}), {1}: (6, {})} | custom-call | flops 1 | bytes 1 | tf_op jit(solution)/shard_map/border/pallas_call | solution.py:476
  31.7 1.3 %collective-permute-start.7 = (f32[7,80,128]{2,1,0:T(8,128)S(1)}, f32[7,80,128]{2,1,0:T(8,128)S(1)}, u32[]{:S(2)}, u32[]{:S(2)}) collective-permute-start(f32[7,80,128]{2,1,0:T(8,128)S(1)} %get-tuple-element.45), channel_id=1, source_target_pairs={{0,16},{1,17},{2,18},{3,19},{4,20},{5,21},{6,22},{7,23},{8,24},{9,... | collective-permute-start | bytes 860168 | tf_op jit(solution)/shard_map/ppermute | solution.py:492
  33.0 1.3 %collective-permute-start.6 = (f32[7,64,128]{2,1,0:T(8,128)S(1)}, f32[7,64,128]{2,1,0:T(8,128)S(1)}, u32[]{:S(2)}, u32[]{:S(2)}) collective-permute-start(f32[7,64,128]{2,1,0:T(8,128)S(1)} %get-tuple-element.44), channel_id=1, source_target_pairs={{0,16},{1,17},{2,18},{3,19},{4,20},{5,21},{6,22},{7,23},{8,24},{9,... | collective-permute-start | bytes 688136 | tf_op jit(solution)/shard_map/ppermute | solution.py:492
  34.3 1.4 %resume.4.behind.refs_0_ = f32[12,144,128]{2,1,0:T(8,128)S(1)} custom-call(s32[12]{0:T(128)S(1)} %copy-done, f32[16]{0:T(128)S(1)} %copy-done.1, f32[12,3,144,128]{3,2,1,0:T(8,128)S(1)} %get-tuple-element.52.entry_ref, f32[7,144,128]{2,1,0:T(8,128)S(1)} %collective-permute-done.3.refs_2_.incoming, ...), custom_call_target="tpu_custom_call", output_to_operand_aliasing={{}: (4, {})} | custom-call | flops 1 | bytes 1 | tf_op jit(solution)/shard_map/resume/pallas_call | solution.py:497
  35.8 1.1 %resume.5.behind.refs_1_ = f32[12,80,128]{2,1,0:T(8,128)S(1)} custom-call(s32[12]{0:T(128)S(1)} %copy-done, f32[16]{0:T(128)S(1)} %copy-done.1, f32[12,3,80,128]{3,2,1,0:T(8,128)S(1)} %get-tuple-element.50.entry_ref, f32[7,80,128]{2,1,0:T(8,128)S(1)} %collective-permute-done.4.refs_3_.incoming, ...), custom_call_target="tpu_custom_call", output_to_operand_aliasing={{}: (4, {})} | custom-call | flops 1 | bytes 1 | tf_op jit(solution)/shard_map/resume/pallas_call | solution.py:497
  36.9 0.0 collective-permute-done.8.incoming
  36.9 1.4 %resume.6.behind.refs_2_ = f32[12,144,128]{2,1,0:T(8,128)S(1)} custom-call(s32[12]{0:T(128)S(1)} %copy-done, f32[16]{0:T(128)S(1)} %copy-done.1, f32[12,3,144,128]{3,2,1,0:T(8,128)S(1)} %get-tuple-element.47.entry_ref, f32[7,144,128]{2,1,0:T(8,128)S(1)} %collective-permute-done.8.incoming, ...), custom_call_target="tpu_custom_call", output_to_operand_aliasing={{}: (4, {})} | custom-call | flops 1 | bytes 1 | tf_op jit(solution)/shard_map/resume/pallas_call | solution.py:497
  38.3 5.1 %collective-permute-done.7.incoming = f32[7,80,128]{2,1,0:T(8,128)S(1)} collective-permute-done((f32[7,80,128]{2,1,0:T(8,128)S(1)}, f32[7,80,128]{2,1,0:T(8,128)S(1)}, u32[]{:S(2)}, u32[]{:S(2)}) %collective-permute-start.7) | collective-permute-done | bytes 286752 | tf_op jit(solution)/shard_map/ppermute | solution.py:492
  43.4 1.1 %resume.7.refs_3_.conv_in = f32[12,144,128]{2,1,0:T(8,128)S(1)} custom-call(s32[12]{0:T(128)S(1)} %copy-done, f32[16]{0:T(128)S(1)} %copy-done.1, f32[12,3,144,128]{3,2,1,0:T(8,128)S(1)} %get-tuple-element.43.entry_ref, f32[7,80,128]{2,1,0:T(8,128)S(1)} %collective-permute-done.7.incoming, ...), custom_call_target="tpu_custom_call", output_to_operand_aliasing={{}: (4, {})} | custom-call | flops 1 | bytes 1 | tf_op jit(solution)/shard_map/resume/pallas_call | solution.py:497
  44.5 1.6 %early.1 = (f32[12,512,128]{2,1,0:T(8,128)S(1)}, f32[12,512,128]{2,1,0:T(8,128)}) custom-call(f32[12,144,128]{2,1,0:T(8,128)S(1)} %resume.4.behind.refs_0_, f32[12,80,128]{2,1,0:T(8,128)S(1)} %resume.5.behind.refs_1_, f32[12,144,128]{2,1,0:T(8,128)S(1)} %resume.6.behind.refs_2_, f32[12,144,128]{2,1,0:T(8,128)S(1)} %resume.7.refs_3_.conv_in), custom_call_target="tpu_custom_call" | custom-call | flops 1 | bytes 1 | tf_op jit(solution)/shard_map/early/pallas_call | solution.py:511
  46.1 1.5 %collective-permute-done.6.incoming = f32[7,64,128]{2,1,0:T(8,128)S(1)} collective-permute-done((f32[7,64,128]{2,1,0:T(8,128)S(1)}, f32[7,64,128]{2,1,0:T(8,128)S(1)}, u32[]{:S(2)}, u32[]{:S(2)}) %collective-permute-start.6) | collective-permute-done | bytes 229408 | tf_op jit(solution)/shard_map/ppermute | solution.py:492
  47.6 1.9 %last.1 = (f32[12,144,128]{2,1,0:T(8,128)S(1)}, f32[12,512,128]{2,1,0:T(8,128)S(1)}, f32[12,512,128]{2,1,0:T(8,128)}) custom-call(s32[12]{0:T(128)S(1)} %copy-done, f32[16]{0:T(128)S(1)} %copy-done.1, f32[12,3,144,128]{3,2,1,0:T(8,128)S(1)} %get-tuple-element.43.entry_ref, ...), custom_call_target="tpu_custom_call", output_to_operand_aliasing={{0}: (4, {}), {1}: (5, {}), {2}: (6, {})} | custom-call | flops 1 | bytes 1 | tf_op jit(solution)/shard_map/last/pallas_call | solution.py:521
Async XLA Ops:
  0.0 9.5 %copy-start.1 = (f32[16]{0:T(128)S(1)}, f32[16]{0:T(128)}, u32[]{:S(2)}) copy-start(f32[16]{0:T(128)} %near.17) | copy-start | bytes 196
  0.0 9.5 %copy-start = (s32[12]{0:T(128)S(1)}, s32[12]{0:T(128)}, u32[]{:S(2)}) copy-start(s32[12]{0:T(128)} %slots.17) | copy-start | bytes 148
  0.0 9.5 %copy-start.3 = (f32[16]{0:T(128)S(1)}, f32[16]{0:T(128)}, u32[]{:S(2)}) copy-start(f32[16]{0:T(128)} %lens.7) | copy-start | bytes 196
  0.0 9.6 %copy-start.2 = (s32[12]{0:T(128)S(1)}, s32[12]{0:T(128)}, u32[]{:S(2)}) copy-start(s32[12]{0:T(128)} %widths.7) | copy-start | bytes 148
  2.1 9.7 %collective-permute-start = (f32[6,144,128]{2,1,0:T(8,128)S(1)}, f32[6,144,128]{2,1,0:T(8,128)S(1)}, u32[]{:S(2)}, u32[]{:S(2)}) collective-permute-start(f32[6,144,128]{2,1,0:T(8,128)S(1)} %get-tuple-element.33), channel_id=1, source_target_pairs={{0,1},{1,0},{2,3},{3,2},{4,5},{5,4},{6,7},{7,6},{8,9},{9,8},{10,11... | collective-permute-start | bytes 1327112 | tf_op jit(solution)/shard_map/ppermute | solution.py:453
  2.2 11.0 %collective-permute-start.1 = (f32[6,144,128]{2,1,0:T(8,128)S(1)}, f32[6,144,128]{2,1,0:T(8,128)S(1)}, u32[]{:S(2)}, u32[]{:S(2)}) collective-permute-start(f32[6,144,128]{2,1,0:T(8,128)S(1)} %get-tuple-element.34), channel_id=1, source_target_pairs={{0,1},{1,0},{2,3},{3,2},{4,5},{5,4},{6,7},{7,6},{8,9},{9,8},{10,11... | collective-permute-start | bytes 1327112 | tf_op jit(solution)/shard_map/ppermute | solution.py:453
  2.7 23.1 %collective-permute-start.3 = (f32[7,144,128]{2,1,0:T(8,128)S(1)}, f32[7,144,128]{2,1,0:T(8,128)S(1)}, u32[]{:S(2)}, u32[]{:S(2)}) collective-permute-start(f32[7,144,128]{2,1,0:T(8,128)S(1)} %get-tuple-element.38), channel_id=1, source_target_pairs={{0,16},{1,17},{2,18},{3,19},{4,20},{5,21},{6,22},{7,23},{8,24},{9,... | collective-permute-start | bytes 1548296 | tf_op jit(solution)/shard_map/ppermute | solution.py:452
  4.0 21.9 %collective-permute-start.2 = (f32[6,144,128]{2,1,0:T(8,128)S(1)}, f32[6,144,128]{2,1,0:T(8,128)S(1)}, u32[]{:S(2)}, u32[]{:S(2)}) collective-permute-start(f32[6,144,128]{2,1,0:T(8,128)S(1)} %get-tuple-element.37), channel_id=1, source_target_pairs={{1,2},{2,1},{3,4},{4,3},{5,6},{6,5},{7,8},{8,7},{9,10},{10,9},{11,... | collective-permute-start | bytes 1327112 | tf_op jit(solution)/shard_map/ppermute | solution.py:453
  6.1 23.9 %collective-permute-start.5 = (f32[6,144,128]{2,1,0:T(8,128)S(1)}, f32[6,144,128]{2,1,0:T(8,128)S(1)}, u32[]{:S(2)}, u32[]{:S(2)}) collective-permute-start(f32[6,144,128]{2,1,0:T(8,128)S(1)} %get-tuple-element.42), channel_id=1, source_target_pairs={{1,2},{2,1},{3,4},{4,3},{5,6},{6,5},{7,8},{8,7},{9,10},{10,9},{11,... | collective-permute-start | bytes 1327112 | tf_op jit(solution)/shard_map/ppermute | solution.py:453
  11.8 14.0 %collective-permute-start.4 = (f32[7,80,128]{2,1,0:T(8,128)S(1)}, f32[7,80,128]{2,1,0:T(8,128)S(1)}, u32[]{:S(2)}, u32[]{:S(2)}) collective-permute-start(f32[7,80,128]{2,1,0:T(8,128)S(1)} %get-tuple-element.39), channel_id=1, source_target_pairs={{0,16},{1,17},{2,18},{3,19},{4,20},{5,21},{6,22},{7,23},{8,24},{9,... | collective-permute-start | bytes 860168 | tf_op jit(solution)/shard_map/ppermute | solution.py:468
  16.2 20.7 %collective-permute-start.8 = (f32[7,144,128]{2,1,0:T(8,128)S(1)}, f32[7,144,128]{2,1,0:T(8,128)S(1)}, u32[]{:S(2)}, u32[]{:S(2)}) collective-permute-start(f32[7,144,128]{2,1,0:T(8,128)S(1)} %get-tuple-element.48), channel_id=1, source_target_pairs={{0,16},{1,17},{2,18},{3,19},{4,20},{5,21},{6,22},{7,23},{8,24},{9,... | collective-permute-start | bytes 1548296 | tf_op jit(solution)/shard_map/ppermute | solution.py:492
  31.7 11.7 %collective-permute-start.7 = (f32[7,80,128]{2,1,0:T(8,128)S(1)}, f32[7,80,128]{2,1,0:T(8,128)S(1)}, u32[]{:S(2)}, u32[]{:S(2)}) collective-permute-start(f32[7,80,128]{2,1,0:T(8,128)S(1)} %get-tuple-element.45), channel_id=1, source_target_pairs={{0,16},{1,17},{2,18},{3,19},{4,20},{5,21},{6,22},{7,23},{8,24},{9,... | collective-permute-start | bytes 860168 | tf_op jit(solution)/shard_map/ppermute | solution.py:492
  33.0 14.5 %collective-permute-start.6 = (f32[7,64,128]{2,1,0:T(8,128)S(1)}, f32[7,64,128]{2,1,0:T(8,128)S(1)}, u32[]{:S(2)}, u32[]{:S(2)}) collective-permute-start(f32[7,64,128]{2,1,0:T(8,128)S(1)} %get-tuple-element.44), channel_id=1, source_target_pairs={{0,16},{1,17},{2,18},{3,19},{4,20},{5,21},{6,22},{7,23},{8,24},{9,... | collective-permute-start | bytes 688136 | tf_op jit(solution)/shard_map/ppermute | solution.py:492

commit v8 on v7

--- a/solution.py
+++ b/solution.py
@@ -11,10 +11,11 @@
 RIM = WMAX + 1
 LANES = 128
 SUB = 8
-INNER_ROWS, FINAL_ROWS = 9, 4
+INNER_ROWS, FINAL_ROWS = 8, 3
 TOGETHER = 4
 PARTS = (3, 2, 2)
-BORDER_SHARES = (((0, 1),), ((0,), (1,)))
+MADE_UP = {3: 0, 4: 2}
+BEHIND = {2: 0, 3: 1}
 SHARES = 2
 SENT = 7
 TINY, POLE, FAR = 1e-30, 1e-20, 1e10
@@ -23,30 +24,43 @@
 
 
 def group_sizes(row_count):
-    return (INNER_ROWS, row_count - 2 * RIM - INNER_ROWS, RIM, RIM)
+    return (INNER_ROWS, row_count - 2 * RIM - INNER_ROWS, RIM, RIM - FINAL_ROWS, FINAL_ROWS)
 
 
 def is_even():
     return lax.rem(lax.axis_index("sky"), 2) == 0
 
 
-def pieces_of(row_count):
-    sizes = group_sizes(row_count)
-    even = is_even()
-    split_last = [(jnp.where(even, FINAL_ROWS, 0), RIM - FINAL_ROWS), (jnp.where(even, 0, RIM - FINAL_ROWS), FINAL_ROWS)]
-    return [(part, 0, count) for part, count in enumerate(sizes[:-1])] + [(len(sizes) - 1, *one) for one in split_last]
-
-
-def side_starts(row_count):
-    low, high = (0, -RIM), (row_count - RIM, row_count)
-    even = is_even()
-    paired = [jnp.where(even, b, a) for a, b in zip(low, high)]
-    other = [jnp.where(even, a, b) for a, b in zip(low, high)]
-    return paired, other
+def by_side(paired, low, high):
+    return jnp.where(is_even() != paired, low, high)
 
 
 def first_row(row_count, part):
-    return (RIM, RIM + INNER_ROWS)[part] if part < 2 else side_starts(row_count)[part - 2][0]
+    if part < 2:
+        return (RIM, RIM + INNER_ROWS)[part]
+    if part == 2:
+        return by_side(True, 0, row_count - RIM)
+    if part == 3:
+        return by_side(False, FINAL_ROWS, row_count - RIM)
+    return by_side(False, 0, row_count - FINAL_ROWS)
+
+
+def sent_rows(row_count, part):
+    near = RIM - FINAL_ROWS
+    if part == 2:
+        return by_side(True, 0, row_count - RIM), RIM
+    if part == 3:
+        return by_side(False, 0, row_count - near), near
+    return by_side(False, near, row_count - RIM), FINAL_ROWS
+
+
+def got_rows(row_count, part):
+    near = RIM - FINAL_ROWS
+    if part == 2:
+        return by_side(True, -RIM, row_count), RIM
+    if part == 3:
+        return by_side(False, -near, row_count), near
+    return by_side(False, -RIM, row_count + near), FINAL_ROWS
 
 
 def split(value, parts):
@@ -116,13 +130,12 @@
         entry_ref[k, field, pl.ds(at * blocks, blocks), :] = value if field == 1 else value + near
 
 
-def sweep(planes, base, length, near_of, entry_ref, conv_ref, start, finish):
+def sweep(planes, length, near_of, entry_ref, conv_ref, start, finish):
     step = next(count * SUB for count in (4, 3, 2, 1) if length % (count * SUB) == 0)
 
     def part(index, carry):
-        own = pl.ds(pl.multiple_of(index * step, SUB), step)
-        where = pl.ds(pl.multiple_of(base + index * step, SUB), step)
-        now, then = (None, None) if start is None else start(own)
+        where = pl.ds(pl.multiple_of(index * step, SUB), step)
+        now, then = (None, None) if start is None else start(where)
         for k in range(planes):
             xx, xy, yy = [entry_ref[k, i, where, :] for i in range(3)]
             kept = 1.0 - near_of(k)
@@ -144,7 +157,7 @@
             now = new
             conv_ref[k, where, :] = 1.0 - 0.5 * (new[0] + new[3])
         if finish is not None:
-            finish(own, now + then)
+            finish(where, now + then)
         return carry
 
     lax.fori_loop(0, length // step, part, 0)
@@ -230,22 +243,29 @@
     return lax.axis_index("depth") == 0
 
 
-def first_sweep(sizes, part, scalars, entry_ref, conv_ref, state_refs):
+def first_sweep(sizes, part, scalars, entry_ref, conv_ref, state_ref):
     planes, rows, blocks = sizes
     widths, slots, near, lens = scalars
-    pieces = [(base, count) for group, base, count in pieces_of(rows) if group == part]
 
     @pl.when(is_first())
     def _():
-        for (base, count), state_ref in zip(pieces, state_refs):
-            sweep(planes, base * blocks, count * blocks, lambda k: near[slots[k]], entry_ref, conv_ref, None,
-                  writer(state_ref))
+        sweep(planes, group_sizes(rows)[part] * blocks, lambda k: near[slots[k]], entry_ref, conv_ref, None,
+              writer(state_ref))
+
+
+def each_plane(planes, body):
+    def step(place, carry):
+        for share in range(SHARES):
+            body(share, place, place * SHARES + share)
+        return carry
+
+    lax.fori_loop(0, planes // SHARES, step, 0)
 
 
 def first_kernel(sizes, widths_hbm, slots_hbm, near_hbm, lens_hbm, potential_hbm, x_ref, band_ref, entry_ref, conv_ref,
-                 state_ref, *refs):
-    planes, rows, blocks = sizes
-    sends, scratch = refs[:2 * SHARES], refs[2 * SHARES:]
+                 state_ref, near_ref, far_ref, *rest):
+    planes, rows, blocks = sizes
+    paired_refs, scratch = rest[:SHARES], rest[SHARES:]
     scratch, (tiles_ref, widths, slots, near, lens, plane_sems, table_sems) = scratch[:-7], scratch[-7:]
     tables = ((widths_hbm, widths), (slots_hbm, slots), (near_hbm, near), (lens_hbm, lens))
     copies = [pltpu.make_async_copy(*pair, table_sems.at[i]) for i, pair in enumerate(tables)]
@@ -260,7 +280,6 @@
     make_bands(band_ref)
     for copy in copies:
         copy.wait()
-    sides = [(start + RIM) * blocks for start, _ in side_starts(rows)]
 
     def arrive(share, place, k):
         plane_copy(k).wait()
@@ -269,8 +288,9 @@
                 start = (row // SUB) * SUB * blocks + half * SUB * SUB + row % SUB
                 x_ref[k, pl.ds((row + RIM) * blocks + half * SUB, SUB), :] = tiles_ref[
                     k, pl.ds(start, SUB, stride=SUB), :]
-        for i, side in enumerate(sides):
-            sends[i * SHARES + share][place] = x_ref[k, pl.ds(pl.multiple_of(side, blocks), RIM * blocks), :]
+        for part, ref, at in ((2, paired_refs[share], place), (3, near_ref, k), (4, far_ref, k)):
+            start, count = sent_rows(rows, part)
+            ref[at] = x_ref[k, pl.ds(pl.multiple_of((start + RIM) * blocks, blocks), count * blocks), :]
 
     scalars = (widths, slots, near, lens)
 
@@ -280,68 +300,73 @@
 
     @pl.when(jnp.logical_not(is_first()))
     def _():
-        def place(index, carry):
-            for share in range(SHARES):
-                arrive(share, index, index * SHARES + share)
-            return carry
-
-        lax.fori_loop(0, planes // SHARES, place, 0)
-
-    first_sweep(sizes, 0, scalars, entry_ref, conv_ref, [state_ref])
+        each_plane(planes, arrive)
+
+    first_sweep(sizes, 0, scalars, entry_ref, conv_ref, state_ref)
 
 
 def second_kernel(sizes, widths, slots, near, lens, band_ref, x_ref, entry_ref, conv_ref, state_ref, *scratch):
     scalars = (widths, slots, near, lens)
     group_stage(sizes, 1, scalars, x_ref, band_ref, scratch, entry_ref)
-    first_sweep(sizes, 1, scalars, entry_ref, conv_ref, [state_ref])
-
-
-def border_kernel(sizes, part, shares, counts, widths, slots, near, lens, band_ref, x_in, *refs):
-    planes, rows, blocks = sizes
-    handed, results, _ = counts
-    refs = refs[handed:]
-    arrived, refs = refs[:len(shares)], refs[len(shares) + counts[2]:]
-    (x_ref, entry_ref, *made), scratch = refs[:results], refs[results:]
-    start = side_starts(rows)[part - 2][1] + RIM
+    first_sweep(sizes, 1, scalars, entry_ref, conv_ref, state_ref)
+
+
+def border_kernel(sizes, part, widths, slots, near, lens, band_ref, x_in, *refs):
+    planes, rows, blocks = sizes
+    made_up = part in MADE_UP
+    arrived, refs = refs[made_up:made_up + (SHARES if part == 2 else 1)], refs[made_up + (SHARES if part == 2 else 1) + (part in BEHIND):]
+    x_ref, entry_ref, conv_ref, state_ref, *scratch = refs
+    start, count = got_rows(rows, part)
     scalars = (widths, slots, near, lens)
 
     def arrive(share, place, k):
-        x_ref[k, pl.ds(pl.multiple_of(start * blocks, blocks), RIM * blocks), :] = arrived[shares.index(share)][place]
-
-    group_stage(sizes, part, scalars, x_ref, band_ref, scratch, entry_ref, arrive, shares)
-    if shares[-1] == SHARES - 1:
-        first_sweep(sizes, part, scalars, entry_ref, made[0], made[1:])
-    elif shares[0] == 0:
+        rows_in = arrived[share][place] if part == 2 else arrived[0][k]
+        x_ref[k, pl.ds(pl.multiple_of((start + RIM) * blocks, blocks), count * blocks), :] = rows_in
+
+    if made_up:
+        other_ref, scratch = scratch[0], scratch[1:]
+    if part in MADE_UP.values():
+
+        @pl.when(is_first())
+        def _():
+            group_stage(sizes, part, scalars, x_ref, band_ref, scratch, entry_ref, arrive)
+
         @pl.when(jnp.logical_not(is_first()))
         def _():
-            for share in range(SHARES):
-                group_stage(sizes, 0, scalars, x_ref, band_ref, scratch, made[0], None, (share,))
-
-
-def resume(sizes, piece, turn, slots, near, entry_ref, incoming, conv_ref, finish):
-    planes, rows, blocks = sizes
-    part, base, count = pieces_of(rows)[piece]
+            each_plane(planes, arrive)
+
+    else:
+        group_stage(sizes, part, scalars, x_ref, band_ref, scratch, entry_ref, arrive)
+    if made_up:
+
+        @pl.when(jnp.logical_not(is_first()))
+        def _():
+            group_stage(sizes, MADE_UP[part], scalars, x_ref, band_ref, scratch, other_ref)
+
+    first_sweep(sizes, part, scalars, entry_ref, conv_ref, state_ref)
+
+
+def resume(sizes, part, turn, slots, near, entry_ref, incoming, conv_ref, finish):
+    planes, rows, blocks = sizes
 
     @pl.when(lax.axis_index("depth") == turn)
     def _():
-        sweep(planes, base * blocks, count * blocks, lambda k: near[slots[k]], entry_ref, conv_ref,
+        sweep(planes, group_sizes(rows)[part] * blocks, lambda k: near[slots[k]], entry_ref, conv_ref,
               lambda where: unpacked_state([incoming[i, where, :] for i in range(SENT)]), finish)
 
 
-def resume_kernel(sizes, piece, turn, slots, near, entry_ref, incoming, conv_in, behind, conv_ref, *state_ref):
-    resume(sizes, piece, turn, slots, near, entry_ref, incoming, conv_ref, writer(state_ref[0]) if state_ref else None)
-
-
-def place_rows(sizes, piece, k, conv_ref, tiles_ref):
-    planes, rows, blocks = sizes
-    part, base, count = pieces_of(rows)[piece]
-    start = first_row(rows, part) + base
-    for i in range(count):
+def resume_kernel(sizes, part, turn, slots, near, entry_ref, incoming, conv_in, behind, conv_ref, *state_ref):
+    resume(sizes, part, turn, slots, near, entry_ref, incoming, conv_ref, writer(state_ref[0]) if state_ref else None)
+
+
+def place_rows(sizes, part, k, conv_ref, tiles_ref):
+    planes, rows, blocks = sizes
+    start = first_row(rows, part)
+    for i in range(group_sizes(rows)[part]):
         row = start + i
         for half in range(blocks // SUB):
             to = lax.div(row, SUB) * SUB * blocks + half * SUB * SUB + lax.rem(row, SUB)
-            at = (base + i) * blocks + half * SUB
-            tiles_ref[k, pl.ds(to, SUB, stride=SUB), :] = conv_ref[k, pl.ds(pl.multiple_of(at, SUB), SUB), :]
+            tiles_ref[k, pl.ds(to, SUB, stride=SUB), :] = conv_ref[k, pl.ds(i * blocks + half * SUB, SUB), :]
 
 
 def write_out(sizes, late, tiles_ref, out_hbm, sems, before_plane):
@@ -371,16 +396,16 @@
     *conv_refs, tiles_ref, out_hbm, sems = refs
 
     def place(k):
-        for piece, (part, _, _) in enumerate(pieces_of(sizes[1])[:-1]):
-            place_rows(sizes, piece, k, conv_refs[part], tiles_ref)
+        for part, conv_ref in enumerate(conv_refs):
+            place_rows(sizes, part, k, conv_ref, tiles_ref)
 
     write_out(sizes, False, tiles_ref, out_hbm, sems, place)
 
 
-def last_kernel(sizes, piece, turn, slots, near, entry_ref, incoming, conv_in, tiles_in, out_in, conv_ref, tiles_ref,
+def last_kernel(sizes, part, turn, slots, near, entry_ref, incoming, conv_in, tiles_in, out_in, conv_ref, tiles_ref,
                 out_hbm, sems):
-    resume(sizes, piece, turn, slots, near, entry_ref, incoming, conv_ref, None)
-    write_out(sizes, True, tiles_ref, out_hbm, sems, lambda k: place_rows(sizes, piece, k, conv_ref, tiles_ref))
+    resume(sizes, part, turn, slots, near, entry_ref, incoming, conv_ref, None)
+    write_out(sizes, True, tiles_ref, out_hbm, sems, lambda k: place_rows(sizes, part, k, conv_ref, tiles_ref))
 
 
 def per_device(potential, widths, plane_slot, ratio_near, ratio_lens):
@@ -389,7 +414,6 @@
     sizes = (planes, rows, blocks)
     counts = group_sizes(rows)
     parts = len(counts)
-    pieces = [(part, count) for part, _, count in pieces_of(rows)]
     depth_count, sky_count = lax.axis_size("depth"), lax.axis_size("sky")
     swaps = [[pair for i in range(first, sky_count - 1, 2) for pair in ((i, i + 1), (i + 1, i))] for first in (0, 1)]
     ahead = [(i, i + 1) for i in range(depth_count - 1)]
@@ -424,41 +448,39 @@
     def conv_shape(part):
         return held(planes, counts[part] * blocks, LANES)
 
-    def state_shape(piece):
-        return moved(SENT, pieces[piece][1] * blocks, LANES)
+    def state_shape(part):
+        return moved(SENT, counts[part] * blocks, LANES)
 
     def group_shapes(part):
-        return [conv_shape(part), *[state_shape(piece) for piece, (group, _) in enumerate(pieces) if group == part]]
-
-    def group_scratch(part, shares):
-        count = max(counts[0], counts[part]) if part > 1 else counts[part]
+        return [entry_shape(part), conv_shape(part), state_shape(part)]
+
+    def group_scratch(part):
+        count = max(counts[part], counts[MADE_UP[part]] if part in MADE_UP else 0)
         return [held(3, count * blocks, max(PARTS) * LANES, dtype=BF16),
-                held(3, (count + 1) * (blocks + SUB), LANES)] * (len(shares) * steps_of(planes, shares)[1])
-
-    side = moved(planes // SHARES, RIM * blocks, LANES)
-    x, bands, *rest = pl.pallas_call(
+                held(3, (count + 1) * (blocks + SUB), LANES)] * (SHARES * steps_of(planes, range(SHARES))[1])
+
+    def side_shape(part, shares=1):
+        return moved(planes // shares, sent_rows(rows, part)[1] * blocks, LANES)
+
+    x, bands, entry, conv, state, close, far, *paired = pl.pallas_call(
         functools.partial(first_kernel, sizes),
-        out_shape=[x_shape, band_shape, entry_shape(0), *group_shapes(0), *[side] * (2 * SHARES)],
+        out_shape=[x_shape, band_shape, *group_shapes(0), side_shape(3), side_shape(4), *[side_shape(2, SHARES)] * SHARES],
         in_specs=[anywhere] * 5,
-        out_specs=[vmem] * (5 + 2 * SHARES),
+        out_specs=[vmem] * (7 + SHARES),
         scratch_shapes=[
-            *group_scratch(0, range(SHARES)), held(planes, rows * blocks, LANES),
+            *group_scratch(0), held(planes, rows * blocks, LANES),
             *[pltpu.SMEM(array.shape, array.dtype) for array in scalars], dma((planes,)), dma((len(scalars),))],
         compiler_params=params,
         cost_estimate=cost,
         name="first",
     )(*[in_hbm(array) for array in (*scalars, tiled)])
-    (entry, conv, state), sends = rest[:3], rest[3:]
-    convs, arriving = [conv], [lax.ppermute(state, "depth", ahead)]
-    swapped = [[lax.ppermute(piece, "sky", swap) for piece in sends[i * SHARES:(i + 1) * SHARES]]
-               for i, swap in enumerate(swaps)]
-    entries = [entry]
+    entries, convs, arriving = [entry], [conv], [lax.ppermute(state, "depth", ahead)]
     entry, conv, state = pl.pallas_call(
         functools.partial(second_kernel, sizes),
-        out_shape=[entry_shape(1), *group_shapes(1)],
+        out_shape=group_shapes(1),
         in_specs=[smem] * 4 + [vmem] * 2,
         out_specs=[vmem] * 3,
-        scratch_shapes=group_scratch(1, range(SHARES)),
+        scratch_shapes=group_scratch(1),
         compiler_params=params,
         cost_estimate=cost,
         name="second",
@@ -466,60 +488,56 @@
     entries.append(entry)
     convs.append(conv)
     arriving.append(lax.ppermute(state, "depth", ahead))
+    swapped = {part: [lax.ppermute(piece, "sky", swaps[part > 2]) for piece in pieces]
+               for part, pieces in ((2, paired), (3, [close]), (4, [far]))}
     for part in range(2, parts):
-        entry = None
-        for shares in BORDER_SHARES[part - 2]:
-            last = shares[-1] == SHARES - 1
-            behind = [] if part == 2 else [] if last else arriving[:2]
-            handed = ([] if entry is None else [entry]) + ([] if last else entries[:1])
-            shapes = [x_shape, entry_shape(part), *([] if last else [entry_shape(0)]), *(group_shapes(part) if last else [])]
-            x, entry, *group = pl.pallas_call(
-                functools.partial(border_kernel, sizes, part, shares, (len(handed), len(shapes), len(behind))),
-                out_shape=shapes,
-                in_specs=[smem] * 4 + [vmem] * (2 + len(handed) + len(shares)) + [anywhere] * len(behind),
-                out_specs=[vmem] * len(shapes),
-                scratch_shapes=group_scratch(part, shares),
-                input_output_aliases={5: 0} | ({} if entry is None else {6: 1}) | ({} if last else {5 + len(handed): 2}),
-                compiler_params=params,
-                cost_estimate=cost,
-                name="border",
-            )(*scalars, in_vmem(bands), in_vmem(x), *map(in_vmem, handed), *[swapped[part - 2][share] for share in shares],
-              *behind)
-            if not last:
-                entries[0] = group[0]
+        other = [entries[MADE_UP[part]]] if part in MADE_UP else []
+        x, entry, conv, state, *again = pl.pallas_call(
+            functools.partial(border_kernel, sizes, part),
+            out_shape=[x_shape, *group_shapes(part), *[entry_shape(MADE_UP[part]) for _ in other]],
+            in_specs=[smem] * 4 + [vmem] * (2 + len(other) + len(swapped[part])) + [anywhere] * (part in BEHIND),
+            out_specs=[vmem] * (4 + len(other)),
+            scratch_shapes=group_scratch(part),
+            input_output_aliases={5: 0} | ({6: 4} if other else {}),
+            compiler_params=params,
+            cost_estimate=cost,
+            name="border",
+        )(*scalars, in_vmem(bands), in_vmem(x), *map(in_vmem, other), *swapped[part], *[arriving[BEHIND[part]] for _ in range(part in BEHIND)])
+        if other:
+            entries[MADE_UP[part]], = again
         entries.append(entry)
-        convs.append(group[0])
-        arriving += [lax.ppermute(state, "depth", ahead) for state in group[1:]]
+        convs.append(conv)
+        arriving.append(lax.ppermute(state, "depth", ahead))
 
     for turn in range(1, depth_count):
         last = turn == depth_count - 1
-        for piece, (part, _) in enumerate(pieces[:len(pieces) - last]):
+        for part in range(parts - last):
             convs[part], *state = pl.pallas_call(
-                functools.partial(resume_kernel, sizes, piece, turn),
-                out_shape=[conv_shape(part)] + ([] if last else [state_shape(piece)]),
+                functools.partial(resume_kernel, sizes, part, turn),
+                out_shape=[conv_shape(part)] + ([] if last else [state_shape(part)]),
                 in_specs=[smem] * 2 + [vmem] * 4,
                 out_specs=[vmem] * (1 if last else 2),
                 input_output_aliases={4: 0},
                 compiler_params=params,
                 cost_estimate=cost,
                 name="resume",
-            )(plane_slot, ratio_near, in_vmem(entries[part]), arriving[piece], in_vmem(convs[part]),
+            )(plane_slot, ratio_near, in_vmem(entries[part]), arriving[part], in_vmem(convs[part]),
               in_vmem(convs[part - 1]))
             if state:
-                arriving[piece] = lax.ppermute(state[0], "depth", ahead)
+                arriving[part] = lax.ppermute(state[0], "depth", ahead)
     out_shape = moved(planes, rows * blocks, LANES)
     tiles, out = pl.pallas_call(
         functools.partial(early_kernel, sizes),
         out_shape=[held(planes, rows * blocks, LANES), out_shape],
-        in_specs=[vmem] * parts,
+        in_specs=[vmem] * (parts - 1),
         out_specs=[vmem, anywhere],
         scratch_shapes=[dma((planes,))],
         compiler_params=params,
         cost_estimate=cost,
         name="early",
-    )(*[in_vmem(conv) for conv in convs])
+    )(*[in_vmem(conv) for conv in convs[:-1]])
     conv, tiles, out = pl.pallas_call(
-        functools.partial(last_kernel, sizes, len(pieces) - 1, depth_count - 1),
+        functools.partial(last_kernel, sizes, parts - 1, depth_count - 1),
         out_shape=[conv_shape(parts - 1), held(planes, rows * blocks, LANES), out_shape],
         in_specs=[smem] * 2 + [vmem] * 4 + [anywhere],
         out_specs=[vmem, vmem, anywhere],

time: 49.7 us -> 48.6 us (0.978)
  starting transfers between devices: 12.6 us -> 11 us
  Pallas kernels: 21.8 us -> 22.5 us
    ppermute x8 -> x5, starting transfers between devices: 11.3 us -> 5.87 us  [the longest x4 4.57 us: per_device(): lax.ppermute(piece, 'sky', swaps[part > 2])]
    ppermute x1 -> x4, starting transfers between devices: 1.29 us -> 5.17 us  [per_device(): arriving.append(lax.ppermute(state, 'depth', ahead))]
    ppermute x1 -> x4, waiting for transfers between devices: 8.32 us -> 6.48 us  [per_device(): arriving.append(lax.ppermute(state, 'depth', ahead))]
    ppermute x8 -> x5, waiting for transfers between devices: 6.57 us -> 8.11 us  [the longest x1 8.1 us: per_device(): lax.ppermute(state, 'depth', ahead)]
    pallas_call x9, Pallas kernels: 18.1 us -> 18.8 us  [the longest x3 9.57 us: per_device(): pl.pallas_call(functools.partial(border_kernel, sizes, part), out_shape=[...]
  transfers between devices with their start and end apart: 9 -> 9, of which waited for: 3 -> 3; matrix products, arithmetic and copies ran while one was open for 0% -> 0% of each run, Pallas kernels for 36% -> 38%
where the time goes in v8:
time: 48.6 us; the launch traced here: 48.3 us
  Pallas kernels  22.5 us (46%)
  waiting for transfers between devices  14.6 us (30%)
  starting transfers between devices  11 us (23%)
    pallas_call x3, Pallas kernels, per_device(): pl.pallas_call(functools.partial(border_kernel, sizes, part), out_shape=[...  9.57 us
    ppermute x1, waiting for transfers between devices, per_device(): lax.ppermute(state, 'depth', ahead)  8.1 us
    ppermute x4, waiting for transfers between devices, per_device(): arriving.append(lax.ppermute(state, 'depth', ahead))  6.48 us
    ppermute x4, starting transfers between devices, per_device(): arriving.append(lax.ppermute(state, 'depth', ahead))  5.17 us
    pallas_call x4, Pallas kernels, per_device(): pl.pallas_call(functools.partial(resume_kernel, sizes, part, turn), out_s...  5.04 us
    ppermute x4, starting transfers between devices, per_device(): lax.ppermute(piece, 'sky', swaps[part > 2])  4.57 us
    pallas_call x1, Pallas kernels, per_device(): pl.pallas_call(functools.partial(second_kernel, sizes), out_shape=group_s...  2.31 us
    pallas_call x1, Pallas kernels, per_device(): pl.pallas_call(functools.partial(first_kernel, sizes), out_shape=[x_shape...  2.06 us
  transfers between devices with their start and end apart: 9, of which 3 were waited for; matrix products, arithmetic and copies ran while one was open for 0% of the time, Pallas kernels for 38%

profile of v8, /device:TPU:6, one launch (start us, length us, event | category | flops | bytes accessed | tf_op | source)
XLA Modules:
  0.0 48.3 jit_solution(4640061371581224723)
XLA Ops:
  0.0 0.0 copy-start.1
  0.0 0.0 copy-start
  0.0 0.0 copy-start.3
  0.0 0.0 copy-start.2
  0.0 2.1 %first.1 = (f32[12,800,128]{2,1,0:T(8,128)S(1)}, bf16[8,3,128,256]{3,2,1,0:T(8,128)(2,1)S(1)}, f32[12,3,128,128]{3,2,1,0:T(8,128)S(1)}, f32[12,128,128]{2,1,0:T(...) custom-call(s32[12]{0:T(128)} %widths.7, ...), custom_call_target="tpu_custom_call" | custom-call | flops 1 | bytes 1 | tf_op jit(solution)/shard_map/first/pallas_call | solution.py:465
  2.1 1.3 %collective-permute-start.2 = (f32[7,128,128]{2,1,0:T(8,128)S(1)}, f32[7,128,128]{2,1,0:T(8,128)S(1)}, u32[]{:S(2)}, u32[]{:S(2)}) collective-permute-start(f32[7,128,128]{2,1,0:T(8,128)S(1)} %get-tuple-element.37), channel_id=1, source_target_pairs={{0,16},{1,17},{2,18},{3,19},{4,20},{5,21},{6,22},{7,23},{8,24},{9,... | collective-permute-start | bytes 1376264 | tf_op jit(solution)/shard_map/ppermute | solution.py:477
  3.4 0.1 collective-permute-start
  3.5 0.5 %collective-permute-start.1 = (f32[6,144,128]{2,1,0:T(8,128)S(1)}, f32[6,144,128]{2,1,0:T(8,128)S(1)}, u32[]{:S(2)}, u32[]{:S(2)}) collective-permute-start(f32[6,144,128]{2,1,0:T(8,128)S(1)} %get-tuple-element.36), channel_id=1, source_target_pairs={{0,1},{1,0},{2,3},{3,2},{4,5},{5,4},{6,7},{7,6},{8,9},{9,8},{10,11... | collective-permute-start | bytes 1327112 | tf_op jit(solution)/shard_map/ppermute | solution.py:491
  4.0 2.1 %collective-permute-start.3 = (f32[12,96,128]{2,1,0:T(8,128)S(1)}, f32[12,96,128]{2,1,0:T(8,128)S(1)}, u32[]{:S(2)}, u32[]{:S(2)}) collective-permute-start(f32[12,96,128]{2,1,0:T(8,128)S(1)} %get-tuple-element.40), channel_id=1, source_target_pairs={{1,2},{2,1},{3,4},{4,3},{5,6},{6,5},{7,8},{8,7},{9,10},{10,9},{11,... | collective-permute-start | bytes 1769480 | tf_op jit(solution)/shard_map/ppermute | solution.py:491
  6.1 0.0 copy-done.1
  6.1 0.0 copy-done
  6.1 0.0 copy-done.3
  6.1 0.0 copy-done.2
  6.1 2.3 %second.1 = (f32[12,3,96,128]{3,2,1,0:T(8,128)S(1)}, f32[12,96,128]{2,1,0:T(8,128)S(1)}, f32[7,96,128]{2,1,0:T(8,128)S(1)}) custom-call(s32[12]{0:T(128)S(1)} %copy-done.2, s32[12]{0:T(128)S(1)} %copy-done, f32[16]{0:T(128)S(1)} %copy-done.1, f32[16]{0:T(128)S(1)} %copy-done.3, bf16[8,3,128,256]{3,2,1,0:T(8,128)(2,1)S(1)} %get-tuple-element.33.band_ref, ...), custom_call_target="tpu_custom_call" | custom-call | flops 1 | bytes 1 | tf_op jit(solution)/shard_map/second/pallas_call | solution.py:478
  8.4 1.3 %collective-permute-start.4 = (f32[7,96,128]{2,1,0:T(8,128)S(1)}, f32[7,96,128]{2,1,0:T(8,128)S(1)}, u32[]{:S(2)}, u32[]{:S(2)}) collective-permute-start(f32[7,96,128]{2,1,0:T(8,128)S(1)} %get-tuple-element.41), channel_id=1, source_target_pairs={{0,16},{1,17},{2,18},{3,19},{4,20},{5,21},{6,22},{7,23},{8,24},{9,... | collective-permute-start | bytes 1032200 | tf_op jit(solution)/shard_map/ppermute | solution.py:490
  9.7 0.0 collective-permute-done.refs_0_
  9.7 0.0 collective-permute-done.1.refs_1_
  9.7 8.1 %collective-permute-done.2.refs_2_.incoming = f32[7,128,128]{2,1,0:T(8,128)S(1)} collective-permute-done((f32[7,128,128]{2,1,0:T(8,128)S(1)}, f32[7,128,128]{2,1,0:T(8,128)S(1)}, u32[]{:S(2)}, u32[]{:S(2)}) %collective-permute-start.2) | collective-permute-done | bytes 458784 | tf_op jit(solution)/shard_map/ppermute | solution.py:477
  17.8 0.7 %border.3 = (f32[12,800,128]{2,1,0:T(8,128)S(1)}, f32[12,3,144,128]{3,2,1,0:T(8,128)S(1)}, f32[12,144,128]{2,1,0:T(8,128)S(1)}, f32[7,144,128]{2,1,0:T(8,128)S(1)}) custom-call(s32[12]{0:T(128)S(1)} %copy-done.2, s32[12]{0:T(128)S(1)} %copy-done, f32[16]{0:T(128)S(1)} %copy-done.1, f32[16]{0:T(128)S(1)} %copy-done.3, ...), custom_call_target="tpu_custom_call", output_to_operand_aliasing={{0}: (5, {})} | custom-call | flops 1 | bytes 1 | tf_op jit(solution)/shard_map/border/pallas_call | solution.py:495
  18.5 1.3 %collective-permute-start.7 = (f32[7,144,128]{2,1,0:T(8,128)S(1)}, f32[7,144,128]{2,1,0:T(8,128)S(1)}, u32[]{:S(2)}, u32[]{:S(2)}) collective-permute-start(f32[7,144,128]{2,1,0:T(8,128)S(1)} %get-tuple-element.53), channel_id=1, source_target_pairs={{0,16},{1,17},{2,18},{3,19},{4,20},{5,21},{6,22},{7,23},{8,24},{9,... | collective-permute-start | bytes 1548296 | tf_op jit(solution)/shard_map/ppermute | solution.py:510
  19.8 1.9 %collective-permute-start.5 = (f32[12,48,128]{2,1,0:T(8,128)S(1)}, f32[12,48,128]{2,1,0:T(8,128)S(1)}, u32[]{:S(2)}, u32[]{:S(2)}) collective-permute-start(f32[12,48,128]{2,1,0:T(8,128)S(1)} %get-tuple-element.44), channel_id=1, source_target_pairs={{1,2},{2,1},{3,4},{4,3},{5,6},{6,5},{7,8},{8,7},{9,10},{10,9},{11,... | collective-permute-start | bytes 884744 | tf_op jit(solution)/shard_map/ppermute | solution.py:491
  21.7 3.5 %collective-permute-done.4.refs_2_.incoming = f32[7,96,128]{2,1,0:T(8,128)S(1)} collective-permute-done((f32[7,96,128]{2,1,0:T(8,128)S(1)}, f32[7,96,128]{2,1,0:T(8,128)S(1)}, u32[]{:S(2)}, u32[]{:S(2)}) %collective-permute-start.4) | collective-permute-done | bytes 344096 | tf_op jit(solution)/shard_map/ppermute | solution.py:490
  25.2 0.0 collective-permute-done.3.refs_1_
  25.2 4.5 %border.4 = (f32[12,800,128]{2,1,0:T(8,128)S(1)}, f32[12,3,96,128]{3,2,1,0:T(8,128)S(1)}, f32[12,96,128]{2,1,0:T(8,128)S(1)}, f32[7,96,128]{2,1,0:T(8,128)S(1)}, f32[12,3,128,128]{3,2,1,0:T(8,128)S(1)}) custom-call(s32[12]{0:T(128)S(1)} %copy-done.2, s32[12]{0:T(128)S(1)} %copy-done, f32[16]{0:T(128)S(1)} %copy-done.1, ...), custom_call_target="tpu_custom_call", output_to_operand_aliasing={{0}: (5, {}), {4}: (6, {})} | custom-call | flops 1 | bytes 1 | tf_op jit(solution)/shard_map/border/pallas_call | solution.py:495
  29.7 1.3 %collective-permute-start.8 = (f32[7,96,128]{2,1,0:T(8,128)S(1)}, f32[7,96,128]{2,1,0:T(8,128)S(1)}, u32[]{:S(2)}, u32[]{:S(2)}) collective-permute-start(f32[7,96,128]{2,1,0:T(8,128)S(1)} %get-tuple-element.56), channel_id=1, source_target_pairs={{0,16},{1,17},{2,18},{3,19},{4,20},{5,21},{6,22},{7,23},{8,24},{9,... | collective-permute-start | bytes 1032200 | tf_op jit(solution)/shard_map/ppermute | solution.py:510
  31.0 0.0 collective-permute-done.5.refs_1_
  31.1 4.4 %border.5 = (f32[12,800,128]{2,1,0:T(8,128)S(1)}, f32[12,3,48,128]{3,2,1,0:T(8,128)S(1)}, f32[12,48,128]{2,1,0:T(8,128)S(1)}, f32[7,48,128]{2,1,0:T(8,128)S(1)}, f32[12,3,144,128]{3,2,1,0:T(8,128)S(1)}) custom-call(s32[12]{0:T(128)S(1)} %copy-done.2, s32[12]{0:T(128)S(1)} %copy-done, f32[16]{0:T(128)S(1)} %copy-done.1, ...), custom_call_target="tpu_custom_call", output_to_operand_aliasing={{0}: (5, {}), {4}: (6, {})} | custom-call | flops 1 | bytes 1 | tf_op jit(solution)/shard_map/border/pallas_call | solution.py:495
  35.4 1.3 %collective-permute-start.6 = (f32[7,48,128]{2,1,0:T(8,128)S(1)}, f32[7,48,128]{2,1,0:T(8,128)S(1)}, u32[]{:S(2)}, u32[]{:S(2)}) collective-permute-start(f32[7,48,128]{2,1,0:T(8,128)S(1)} %get-tuple-element.46), channel_id=1, source_target_pairs={{0,16},{1,17},{2,18},{3,19},{4,20},{5,21},{6,22},{7,23},{8,24},{9,... | collective-permute-start | bytes 516104 | tf_op jit(solution)/shard_map/ppermute | solution.py:510
  36.7 1.3 %resume.4.behind.refs_0_ = f32[12,128,128]{2,1,0:T(8,128)S(1)} custom-call(s32[12]{0:T(128)S(1)} %copy-done, f32[16]{0:T(128)S(1)} %copy-done.1, f32[12,3,128,128]{3,2,1,0:T(8,128)S(1)} %get-tuple-element.48.entry_ref, f32[7,128,128]{2,1,0:T(8,128)S(1)} %collective-permute-done.2.refs_2_.incoming, ...), custom_call_target="tpu_custom_call", output_to_operand_aliasing={{}: (4, {})} | custom-call | flops 1 | bytes 1 | tf_op jit(solution)/shard_map/resume/pallas_call | solution.py:515
  38.1 1.1 %resume.5.behind.refs_1_ = f32[12,96,128]{2,1,0:T(8,128)S(1)} custom-call(s32[12]{0:T(128)S(1)} %copy-done, f32[16]{0:T(128)S(1)} %copy-done.1, f32[12,3,96,128]{3,2,1,0:T(8,128)S(1)} %get-tuple-element.50.entry_ref, f32[7,96,128]{2,1,0:T(8,128)S(1)} %collective-permute-done.4.refs_2_.incoming, ...), custom_call_target="tpu_custom_call", output_to_operand_aliasing={{}: (4, {})} | custom-call | flops 1 | bytes 1 | tf_op jit(solution)/shard_map/resume/pallas_call | solution.py:515
  39.2 0.0 collective-permute-done.7.incoming
  39.2 1.4 %resume.6.behind.refs_2_ = f32[12,144,128]{2,1,0:T(8,128)S(1)} custom-call(s32[12]{0:T(128)S(1)} %copy-done, f32[16]{0:T(128)S(1)} %copy-done.1, f32[12,3,144,128]{3,2,1,0:T(8,128)S(1)} %get-tuple-element.52.entry_ref, f32[7,144,128]{2,1,0:T(8,128)S(1)} %collective-permute-done.7.incoming, ...), custom_call_target="tpu_custom_call", output_to_operand_aliasing={{}: (4, {})} | custom-call | flops 1 | bytes 1 | tf_op jit(solution)/shard_map/resume/pallas_call | solution.py:515
  40.7 3.0 %collective-permute-done.8.incoming = f32[7,96,128]{2,1,0:T(8,128)S(1)} collective-permute-done((f32[7,96,128]{2,1,0:T(8,128)S(1)}, f32[7,96,128]{2,1,0:T(8,128)S(1)}, u32[]{:S(2)}, u32[]{:S(2)}) %collective-permute-start.8) | collective-permute-done | bytes 344096 | tf_op jit(solution)/shard_map/ppermute | solution.py:510
  43.6 1.1 %resume.7.refs_3_ = f32[12,96,128]{2,1,0:T(8,128)S(1)} custom-call(s32[12]{0:T(128)S(1)} %copy-done, f32[16]{0:T(128)S(1)} %copy-done.1, f32[12,3,96,128]{3,2,1,0:T(8,128)S(1)} %get-tuple-element.55.entry_ref, f32[7,96,128]{2,1,0:T(8,128)S(1)} %collective-permute-done.8.incoming, ...), custom_call_target="tpu_custom_call", output_to_operand_aliasing={{}: (4, {})} | custom-call | flops 1 | bytes 1 | tf_op jit(solution)/shard_map/resume/pallas_call | solution.py:515
  44.8 1.7 %early.1 = (f32[12,512,128]{2,1,0:T(8,128)S(1)}, f32[12,512,128]{2,1,0:T(8,128)}) custom-call(f32[12,128,128]{2,1,0:T(8,128)S(1)} %resume.4.behind.refs_0_, f32[12,96,128]{2,1,0:T(8,128)S(1)} %resume.5.behind.refs_1_, f32[12,144,128]{2,1,0:T(8,128)S(1)} %resume.6.behind.refs_2_, f32[12,96,128]{2,1,0:T(8,128)S(1)} %resume.7.refs_3_), custom_call_target="tpu_custom_call" | custom-call | flops 1 | bytes 1 | tf_op jit(solution)/shard_map/early/pallas_call | solution.py:529
  46.4 0.0 collective-permute-done.6.incoming
  46.5 1.8 %last.1 = (f32[12,48,128]{2,1,0:T(8,128)S(1)}, f32[12,512,128]{2,1,0:T(8,128)S(1)}, f32[12,512,128]{2,1,0:T(8,128)}) custom-call(s32[12]{0:T(128)S(1)} %copy-done, f32[16]{0:T(128)S(1)} %copy-done.1, f32[12,3,48,128]{3,2,1,0:T(8,128)S(1)} %get-tuple-element.45.entry_ref, ...), custom_call_target="tpu_custom_call", output_to_operand_aliasing={{0}: (4, {}), {1}: (5, {}), {2}: (6, {})} | custom-call | flops 1 | bytes 1 | tf_op jit(solution)/shard_map/last/pallas_call | solution.py:539
Async XLA Ops:
  0.0 6.1 %copy-start.1 = (f32[16]{0:T(128)S(1)}, f32[16]{0:T(128)}, u32[]{:S(2)}) copy-start(f32[16]{0:T(128)} %near.17) | copy-start | bytes 196
  0.0 6.1 %copy-start = (s32[12]{0:T(128)S(1)}, s32[12]{0:T(128)}, u32[]{:S(2)}) copy-start(s32[12]{0:T(128)} %slots.17) | copy-start | bytes 148
  0.0 6.1 %copy-start.3 = (f32[16]{0:T(128)S(1)}, f32[16]{0:T(128)}, u32[]{:S(2)}) copy-start(f32[16]{0:T(128)} %lens.7) | copy-start | bytes 196
  0.0 6.1 %copy-start.2 = (s32[12]{0:T(128)S(1)}, s32[12]{0:T(128)}, u32[]{:S(2)}) copy-start(s32[12]{0:T(128)} %widths.7) | copy-start | bytes 148
  2.1 15.8 %collective-permute-start.2 = (f32[7,128,128]{2,1,0:T(8,128)S(1)}, f32[7,128,128]{2,1,0:T(8,128)S(1)}, u32[]{:S(2)}, u32[]{:S(2)}) collective-permute-start(f32[7,128,128]{2,1,0:T(8,128)S(1)} %get-tuple-element.37), channel_id=1, source_target_pairs={{0,16},{1,17},{2,18},{3,19},{4,20},{5,21},{6,22},{7,23},{8,24},{9,... | collective-permute-start | bytes 1376264 | tf_op jit(solution)/shard_map/ppermute | solution.py:477
  3.4 6.3 %collective-permute-start = (f32[6,144,128]{2,1,0:T(8,128)S(1)}, f32[6,144,128]{2,1,0:T(8,128)S(1)}, u32[]{:S(2)}, u32[]{:S(2)}) collective-permute-start(f32[6,144,128]{2,1,0:T(8,128)S(1)} %get-tuple-element.35), channel_id=1, source_target_pairs={{0,1},{1,0},{2,3},{3,2},{4,5},{5,4},{6,7},{7,6},{8,9},{9,8},{10,11... | collective-permute-start | bytes 1327112 | tf_op jit(solution)/shard_map/ppermute | solution.py:491
  3.5 6.3 %collective-permute-start.1 = (f32[6,144,128]{2,1,0:T(8,128)S(1)}, f32[6,144,128]{2,1,0:T(8,128)S(1)}, u32[]{:S(2)}, u32[]{:S(2)}) collective-permute-start(f32[6,144,128]{2,1,0:T(8,128)S(1)} %get-tuple-element.36), channel_id=1, source_target_pairs={{0,1},{1,0},{2,3},{3,2},{4,5},{5,4},{6,7},{7,6},{8,9},{9,8},{10,11... | collective-permute-start | bytes 1327112 | tf_op jit(solution)/shard_map/ppermute | solution.py:491
  4.0 21.2 %collective-permute-start.3 = (f32[12,96,128]{2,1,0:T(8,128)S(1)}, f32[12,96,128]{2,1,0:T(8,128)S(1)}, u32[]{:S(2)}, u32[]{:S(2)}) collective-permute-start(f32[12,96,128]{2,1,0:T(8,128)S(1)} %get-tuple-element.40), channel_id=1, source_target_pairs={{1,2},{2,1},{3,4},{4,3},{5,6},{6,5},{7,8},{8,7},{9,10},{10,9},{11,... | collective-permute-start | bytes 1769480 | tf_op jit(solution)/shard_map/ppermute | solution.py:491
  8.4 16.8 %collective-permute-start.4 = (f32[7,96,128]{2,1,0:T(8,128)S(1)}, f32[7,96,128]{2,1,0:T(8,128)S(1)}, u32[]{:S(2)}, u32[]{:S(2)}) collective-permute-start(f32[7,96,128]{2,1,0:T(8,128)S(1)} %get-tuple-element.41), channel_id=1, source_target_pairs={{0,16},{1,17},{2,18},{3,19},{4,20},{5,21},{6,22},{7,23},{8,24},{9,... | collective-permute-start | bytes 1032200 | tf_op jit(solution)/shard_map/ppermute | solution.py:490
  18.5 20.7 %collective-permute-start.7 = (f32[7,144,128]{2,1,0:T(8,128)S(1)}, f32[7,144,128]{2,1,0:T(8,128)S(1)}, u32[]{:S(2)}, u32[]{:S(2)}) collective-permute-start(f32[7,144,128]{2,1,0:T(8,128)S(1)} %get-tuple-element.53), channel_id=1, source_target_pairs={{0,16},{1,17},{2,18},{3,19},{4,20},{5,21},{6,22},{7,23},{8,24},{9,... | collective-permute-start | bytes 1548296 | tf_op jit(solution)/shard_map/ppermute | solution.py:510
  19.8 11.2 %collective-permute-start.5 = (f32[12,48,128]{2,1,0:T(8,128)S(1)}, f32[12,48,128]{2,1,0:T(8,128)S(1)}, u32[]{:S(2)}, u32[]{:S(2)}) collective-permute-start(f32[12,48,128]{2,1,0:T(8,128)S(1)} %get-tuple-element.44), channel_id=1, source_target_pairs={{1,2},{2,1},{3,4},{4,3},{5,6},{6,5},{7,8},{8,7},{9,10},{10,9},{11,... | collective-permute-start | bytes 884744 | tf_op jit(solution)/shard_map/ppermute | solution.py:491
  29.7 13.9 %collective-permute-start.8 = (f32[7,96,128]{2,1,0:T(8,128)S(1)}, f32[7,96,128]{2,1,0:T(8,128)S(1)}, u32[]{:S(2)}, u32[]{:S(2)}) collective-permute-start(f32[7,96,128]{2,1,0:T(8,128)S(1)} %get-tuple-element.56), channel_id=1, source_target_pairs={{0,16},{1,17},{2,18},{3,19},{4,20},{5,21},{6,22},{7,23},{8,24},{9,... | collective-permute-start | bytes 1032200 | tf_op jit(solution)/shard_map/ppermute | solution.py:510
  35.4 11.1 %collective-permute-start.6 = (f32[7,48,128]{2,1,0:T(8,128)S(1)}, f32[7,48,128]{2,1,0:T(8,128)S(1)}, u32[]{:S(2)}, u32[]{:S(2)}) collective-permute-start(f32[7,48,128]{2,1,0:T(8,128)S(1)} %get-tuple-element.46), channel_id=1, source_target_pairs={{0,16},{1,17},{2,18},{3,19},{4,20},{5,21},{6,22},{7,23},{8,24},{9,... | collective-permute-start | bytes 516104 | tf_op jit(solution)/shard_map/ppermute | solution.py:510

commit v9 on v8

--- a/solution.py
+++ b/solution.py
@@ -12,7 +12,7 @@
 LANES = 128
 SUB = 8
 INNER_ROWS, FINAL_ROWS = 8, 3
-TOGETHER = 4
+TOGETHER = 6
 PARTS = (3, 2, 2)
 MADE_UP = {3: 0, 4: 2}
 BEHIND = {2: 0, 3: 1}
@@ -273,7 +273,7 @@
         copy.start()
 
     def plane_copy(k):
-        return pltpu.make_async_copy(potential_hbm.at[k], tiles_ref.at[k], plane_sems.at[k])
+        return pltpu.make_async_copy(potential_hbm.at[k], tiles_ref.at[k, pl.ds(0, rows * blocks)], plane_sems.at[k])
 
     for k in range(planes):
         plane_copy(k).start()
@@ -430,6 +430,8 @@
     def held(*shape, dtype=F32):
         return pltpu.VMEM(shape, dtype)
 
+    tiles_shape = held(planes, rows * blocks + SUB * SUB, LANES)
+
     def moved(*shape):
         return jax.ShapeDtypeStruct(shape, F32)
 
@@ -468,7 +470,7 @@
         in_specs=[anywhere] * 5,
         out_specs=[vmem] * (7 + SHARES),
         scratch_shapes=[
-            *group_scratch(0), held(planes, rows * blocks, LANES),
+            *group_scratch(0), tiles_shape,
             *[pltpu.SMEM(array.shape, array.dtype) for array in scalars], dma((planes,)), dma((len(scalars),))],
         compiler_params=params,
         cost_estimate=cost,
@@ -528,7 +530,7 @@
     out_shape = moved(planes, rows * blocks, LANES)
     tiles, out = pl.pallas_call(
         functools.partial(early_kernel, sizes),
-        out_shape=[held(planes, rows * blocks, LANES), out_shape],
+        out_shape=[tiles_shape, out_shape],
         in_specs=[vmem] * (parts - 1),
         out_specs=[vmem, anywhere],
         scratch_shapes=[dma((planes,))],
@@ -538,7 +540,7 @@
     )(*[in_vmem(conv) for conv in convs[:-1]])
     conv, tiles, out = pl.pallas_call(
         functools.partial(last_kernel, sizes, parts - 1, depth_count - 1),
-        out_shape=[conv_shape(parts - 1), held(planes, rows * blocks, LANES), out_shape],
+        out_shape=[conv_shape(parts - 1), tiles_shape, out_shape],
         in_specs=[smem] * 2 + [vmem] * 4 + [anywhere],
         out_specs=[vmem, vmem, anywhere],
         scratch_shapes=[dma((planes,))],

time: 48.6 us -> 48.5 us (level)
  transfers between devices with their start and end apart: 9 -> 9, of which waited for: 3 -> 5; matrix products, arithmetic and copies ran while one was open for 0% -> 0% of each run, Pallas kernels for 38% -> 38%
where the time goes in v9:
time: 48.5 us; the launch traced here: 48.3 us
  Pallas kernels  22.1 us (46%)
  waiting for transfers between devices  15 us (31%)
  starting transfers between devices  11 us (23%)
    pallas_call x3, Pallas kernels, per_device(): pl.pallas_call(functools.partial(border_kernel, sizes, part), out_shape=[...  9.22 us
    ppermute x1, waiting for transfers between devices, per_device(): lax.ppermute(state, 'depth', ahead)  8.09 us
    ppermute x4, waiting for transfers between devices, per_device(): arriving.append(lax.ppermute(state, 'depth', ahead))  6.68 us
    ppermute x4, starting transfers between devices, per_device(): arriving.append(lax.ppermute(state, 'depth', ahead))  5.17 us
    pallas_call x4, Pallas kernels, per_device(): pl.pallas_call(functools.partial(resume_kernel, sizes, part, turn), out_s...  5.04 us
    ppermute x4, starting transfers between devices, per_device(): lax.ppermute(piece, 'sky', swaps[part > 2])  4.57 us
    pallas_call x1, Pallas kernels, per_device(): pl.pallas_call(functools.partial(second_kernel, sizes), out_shape=group_s...  2.25 us
    pallas_call x1, Pallas kernels, per_device(): pl.pallas_call(functools.partial(first_kernel, sizes), out_shape=[x_shape...  2.06 us
  transfers between devices with their start and end apart: 9, of which 5 were waited for; matrix products, arithmetic and copies ran while one was open for 0% of the time, Pallas kernels for 38%

profile of v9, /device:TPU:6, one launch (start us, length us, event | category | flops | bytes accessed | tf_op | source)
XLA Modules:
  0.0 48.3 jit_solution(15662577332539217116)
XLA Ops:
  0.0 0.0 copy-start.1
  0.0 0.0 copy-start
  0.0 0.0 copy-start.3
  0.0 0.0 copy-start.2
  0.0 2.1 %first.1 = (f32[12,800,128]{2,1,0:T(8,128)S(1)}, bf16[8,3,128,256]{3,2,1,0:T(8,128)(2,1)S(1)}, f32[12,3,128,128]{3,2,1,0:T(8,128)S(1)}, f32[12,128,128]{2,1,0:T(...) custom-call(s32[12]{0:T(128)} %widths.7, ...), custom_call_target="tpu_custom_call" | custom-call | flops 1 | bytes 1 | tf_op jit(solution)/shard_map/first/pallas_call | solution.py:467
  2.1 1.3 %collective-permute-start.2 = (f32[7,128,128]{2,1,0:T(8,128)S(1)}, f32[7,128,128]{2,1,0:T(8,128)S(1)}, u32[]{:S(2)}, u32[]{:S(2)}) collective-permute-start(f32[7,128,128]{2,1,0:T(8,128)S(1)} %get-tuple-element.37), channel_id=1, source_target_pairs={{0,16},{1,17},{2,18},{3,19},{4,20},{5,21},{6,22},{7,23},{8,24},{9,... | collective-permute-start | bytes 1376264 | tf_op jit(solution)/shard_map/ppermute | solution.py:479
  3.4 0.1 collective-permute-start
  3.5 0.5 %collective-permute-start.1 = (f32[6,144,128]{2,1,0:T(8,128)S(1)}, f32[6,144,128]{2,1,0:T(8,128)S(1)}, u32[]{:S(2)}, u32[]{:S(2)}) collective-permute-start(f32[6,144,128]{2,1,0:T(8,128)S(1)} %get-tuple-element.36), channel_id=1, source_target_pairs={{0,1},{1,0},{2,3},{3,2},{4,5},{5,4},{6,7},{7,6},{8,9},{9,8},{10,11... | collective-permute-start | bytes 1327112 | tf_op jit(solution)/shard_map/ppermute | solution.py:493
  4.0 2.1 %collective-permute-start.3 = (f32[12,96,128]{2,1,0:T(8,128)S(1)}, f32[12,96,128]{2,1,0:T(8,128)S(1)}, u32[]{:S(2)}, u32[]{:S(2)}) collective-permute-start(f32[12,96,128]{2,1,0:T(8,128)S(1)} %get-tuple-element.40), channel_id=1, source_target_pairs={{1,2},{2,1},{3,4},{4,3},{5,6},{6,5},{7,8},{8,7},{9,10},{10,9},{11,... | collective-permute-start | bytes 1769480 | tf_op jit(solution)/shard_map/ppermute | solution.py:493
  6.1 0.0 copy-done.1
  6.1 0.0 copy-done
  6.1 0.0 copy-done.3
  6.1 0.0 copy-done.2
  6.1 2.3 %second.1 = (f32[12,3,96,128]{3,2,1,0:T(8,128)S(1)}, f32[12,96,128]{2,1,0:T(8,128)S(1)}, f32[7,96,128]{2,1,0:T(8,128)S(1)}) custom-call(s32[12]{0:T(128)S(1)} %copy-done.2, s32[12]{0:T(128)S(1)} %copy-done, f32[16]{0:T(128)S(1)} %copy-done.1, f32[16]{0:T(128)S(1)} %copy-done.3, bf16[8,3,128,256]{3,2,1,0:T(8,128)(2,1)S(1)} %get-tuple-element.33.band_ref, ...), custom_call_target="tpu_custom_call" | custom-call | flops 1 | bytes 1 | tf_op jit(solution)/shard_map/second/pallas_call | solution.py:480
  8.4 1.3 %collective-permute-start.4 = (f32[7,96,128]{2,1,0:T(8,128)S(1)}, f32[7,96,128]{2,1,0:T(8,128)S(1)}, u32[]{:S(2)}, u32[]{:S(2)}) collective-permute-start(f32[7,96,128]{2,1,0:T(8,128)S(1)} %get-tuple-element.41), channel_id=1, source_target_pairs={{0,16},{1,17},{2,18},{3,19},{4,20},{5,21},{6,22},{7,23},{8,24},{9,... | collective-permute-start | bytes 1032200 | tf_op jit(solution)/shard_map/ppermute | solution.py:492
  9.7 0.0 collective-permute-done.refs_0_
  9.7 0.0 collective-permute-done.1.refs_1_
  9.7 8.1 %collective-permute-done.2.refs_2_.incoming = f32[7,128,128]{2,1,0:T(8,128)S(1)} collective-permute-done((f32[7,128,128]{2,1,0:T(8,128)S(1)}, f32[7,128,128]{2,1,0:T(8,128)S(1)}, u32[]{:S(2)}, u32[]{:S(2)}) %collective-permute-start.2) | collective-permute-done | bytes 458784 | tf_op jit(solution)/shard_map/ppermute | solution.py:479
  17.8 0.7 %border.3 = (f32[12,800,128]{2,1,0:T(8,128)S(1)}, f32[12,3,144,128]{3,2,1,0:T(8,128)S(1)}, f32[12,144,128]{2,1,0:T(8,128)S(1)}, f32[7,144,128]{2,1,0:T(8,128)S(1)}) custom-call(s32[12]{0:T(128)S(1)} %copy-done.2, s32[12]{0:T(128)S(1)} %copy-done, f32[16]{0:T(128)S(1)} %copy-done.1, f32[16]{0:T(128)S(1)} %copy-done.3, ...), custom_call_target="tpu_custom_call", output_to_operand_aliasing={{0}: (5, {})} | custom-call | flops 1 | bytes 1 | tf_op jit(solution)/shard_map/border/pallas_call | solution.py:497
  18.5 1.3 %collective-permute-start.7 = (f32[7,144,128]{2,1,0:T(8,128)S(1)}, f32[7,144,128]{2,1,0:T(8,128)S(1)}, u32[]{:S(2)}, u32[]{:S(2)}) collective-permute-start(f32[7,144,128]{2,1,0:T(8,128)S(1)} %get-tuple-element.53), channel_id=1, source_target_pairs={{0,16},{1,17},{2,18},{3,19},{4,20},{5,21},{6,22},{7,23},{8,24},{9,... | collective-permute-start | bytes 1548296 | tf_op jit(solution)/shard_map/ppermute | solution.py:512
  19.8 1.9 %collective-permute-start.5 = (f32[12,48,128]{2,1,0:T(8,128)S(1)}, f32[12,48,128]{2,1,0:T(8,128)S(1)}, u32[]{:S(2)}, u32[]{:S(2)}) collective-permute-start(f32[12,48,128]{2,1,0:T(8,128)S(1)} %get-tuple-element.44), channel_id=1, source_target_pairs={{1,2},{2,1},{3,4},{4,3},{5,6},{6,5},{7,8},{8,7},{9,10},{10,9},{11,... | collective-permute-start | bytes 884744 | tf_op jit(solution)/shard_map/ppermute | solution.py:493
  21.7 3.5 %collective-permute-done.4.refs_2_.incoming = f32[7,96,128]{2,1,0:T(8,128)S(1)} collective-permute-done((f32[7,96,128]{2,1,0:T(8,128)S(1)}, f32[7,96,128]{2,1,0:T(8,128)S(1)}, u32[]{:S(2)}, u32[]{:S(2)}) %collective-permute-start.4) | collective-permute-done | bytes 344096 | tf_op jit(solution)/shard_map/ppermute | solution.py:492
  25.1 0.0 collective-permute-done.3.refs_1_
  25.1 4.3 %border.4 = (f32[12,800,128]{2,1,0:T(8,128)S(1)}, f32[12,3,96,128]{3,2,1,0:T(8,128)S(1)}, f32[12,96,128]{2,1,0:T(8,128)S(1)}, f32[7,96,128]{2,1,0:T(8,128)S(1)}, f32[12,3,128,128]{3,2,1,0:T(8,128)S(1)}) custom-call(s32[12]{0:T(128)S(1)} %copy-done.2, s32[12]{0:T(128)S(1)} %copy-done, f32[16]{0:T(128)S(1)} %copy-done.1, ...), custom_call_target="tpu_custom_call", output_to_operand_aliasing={{0}: (5, {}), {4}: (6, {})} | custom-call | flops 1 | bytes 1 | tf_op jit(solution)/shard_map/border/pallas_call | solution.py:497
  29.5 1.3 %collective-permute-start.8 = (f32[7,96,128]{2,1,0:T(8,128)S(1)}, f32[7,96,128]{2,1,0:T(8,128)S(1)}, u32[]{:S(2)}, u32[]{:S(2)}) collective-permute-start(f32[7,96,128]{2,1,0:T(8,128)S(1)} %get-tuple-element.56), channel_id=1, source_target_pairs={{0,16},{1,17},{2,18},{3,19},{4,20},{5,21},{6,22},{7,23},{8,24},{9,... | collective-permute-start | bytes 1032200 | tf_op jit(solution)/shard_map/ppermute | solution.py:512
  30.8 0.2 collective-permute-done.5.refs_1_
  31.0 4.2 %border.5 = (f32[12,800,128]{2,1,0:T(8,128)S(1)}, f32[12,3,48,128]{3,2,1,0:T(8,128)S(1)}, f32[12,48,128]{2,1,0:T(8,128)S(1)}, f32[7,48,128]{2,1,0:T(8,128)S(1)}, f32[12,3,144,128]{3,2,1,0:T(8,128)S(1)}) custom-call(s32[12]{0:T(128)S(1)} %copy-done.2, s32[12]{0:T(128)S(1)} %copy-done, f32[16]{0:T(128)S(1)} %copy-done.1, ...), custom_call_target="tpu_custom_call", output_to_operand_aliasing={{0}: (5, {}), {4}: (6, {})} | custom-call | flops 1 | bytes 1 | tf_op jit(solution)/shard_map/border/pallas_call | solution.py:497
  35.2 1.3 %collective-permute-start.6 = (f32[7,48,128]{2,1,0:T(8,128)S(1)}, f32[7,48,128]{2,1,0:T(8,128)S(1)}, u32[]{:S(2)}, u32[]{:S(2)}) collective-permute-start(f32[7,48,128]{2,1,0:T(8,128)S(1)} %get-tuple-element.46), channel_id=1, source_target_pairs={{0,16},{1,17},{2,18},{3,19},{4,20},{5,21},{6,22},{7,23},{8,24},{9,... | collective-permute-start | bytes 516104 | tf_op jit(solution)/shard_map/ppermute | solution.py:512
  36.5 1.3 %resume.4.behind.refs_0_ = f32[12,128,128]{2,1,0:T(8,128)S(1)} custom-call(s32[12]{0:T(128)S(1)} %copy-done, f32[16]{0:T(128)S(1)} %copy-done.1, f32[12,3,128,128]{3,2,1,0:T(8,128)S(1)} %get-tuple-element.48.entry_ref, f32[7,128,128]{2,1,0:T(8,128)S(1)} %collective-permute-done.2.refs_2_.incoming, ...), custom_call_target="tpu_custom_call", output_to_operand_aliasing={{}: (4, {})} | custom-call | flops 1 | bytes 1 | tf_op jit(solution)/shard_map/resume/pallas_call | solution.py:517
  37.8 1.1 %resume.5.behind.refs_1_ = f32[12,96,128]{2,1,0:T(8,128)S(1)} custom-call(s32[12]{0:T(128)S(1)} %copy-done, f32[16]{0:T(128)S(1)} %copy-done.1, f32[12,3,96,128]{3,2,1,0:T(8,128)S(1)} %get-tuple-element.50.entry_ref, f32[7,96,128]{2,1,0:T(8,128)S(1)} %collective-permute-done.4.refs_2_.incoming, ...), custom_call_target="tpu_custom_call", output_to_operand_aliasing={{}: (4, {})} | custom-call | flops 1 | bytes 1 | tf_op jit(solution)/shard_map/resume/pallas_call | solution.py:517
  39.0 0.0 collective-permute-done.7.incoming
  39.0 1.4 %resume.6.behind.refs_2_ = f32[12,144,128]{2,1,0:T(8,128)S(1)} custom-call(s32[12]{0:T(128)S(1)} %copy-done, f32[16]{0:T(128)S(1)} %copy-done.1, f32[12,3,144,128]{3,2,1,0:T(8,128)S(1)} %get-tuple-element.52.entry_ref, f32[7,144,128]{2,1,0:T(8,128)S(1)} %collective-permute-done.7.incoming, ...), custom_call_target="tpu_custom_call", output_to_operand_aliasing={{}: (4, {})} | custom-call | flops 1 | bytes 1 | tf_op jit(solution)/shard_map/resume/pallas_call | solution.py:517
  40.4 3.2 %collective-permute-done.8.incoming = f32[7,96,128]{2,1,0:T(8,128)S(1)} collective-permute-done((f32[7,96,128]{2,1,0:T(8,128)S(1)}, f32[7,96,128]{2,1,0:T(8,128)S(1)}, u32[]{:S(2)}, u32[]{:S(2)}) %collective-permute-start.8) | collective-permute-done | bytes 344096 | tf_op jit(solution)/shard_map/ppermute | solution.py:512
  43.6 1.1 %resume.7.refs_3_ = f32[12,96,128]{2,1,0:T(8,128)S(1)} custom-call(s32[12]{0:T(128)S(1)} %copy-done, f32[16]{0:T(128)S(1)} %copy-done.1, f32[12,3,96,128]{3,2,1,0:T(8,128)S(1)} %get-tuple-element.55.entry_ref, f32[7,96,128]{2,1,0:T(8,128)S(1)} %collective-permute-done.8.incoming, ...), custom_call_target="tpu_custom_call", output_to_operand_aliasing={{}: (4, {})} | custom-call | flops 1 | bytes 1 | tf_op jit(solution)/shard_map/resume/pallas_call | solution.py:517
  44.7 1.6 %early.1 = (f32[12,576,128]{2,1,0:T(8,128)S(1)}, f32[12,512,128]{2,1,0:T(8,128)}) custom-call(f32[12,128,128]{2,1,0:T(8,128)S(1)} %resume.4.behind.refs_0_, f32[12,96,128]{2,1,0:T(8,128)S(1)} %resume.5.behind.refs_1_, f32[12,144,128]{2,1,0:T(8,128)S(1)} %resume.6.behind.refs_2_, f32[12,96,128]{2,1,0:T(8,128)S(1)} %resume.7.refs_3_), custom_call_target="tpu_custom_call" | custom-call | flops 1 | bytes 1 | tf_op jit(solution)/shard_map/early/pallas_call | solution.py:531
  46.4 0.1 collective-permute-done.6.incoming
  46.4 1.8 %last.1 = (f32[12,48,128]{2,1,0:T(8,128)S(1)}, f32[12,576,128]{2,1,0:T(8,128)S(1)}, f32[12,512,128]{2,1,0:T(8,128)}) custom-call(s32[12]{0:T(128)S(1)} %copy-done, f32[16]{0:T(128)S(1)} %copy-done.1, f32[12,3,48,128]{3,2,1,0:T(8,128)S(1)} %get-tuple-element.45.entry_ref, ...), custom_call_target="tpu_custom_call", output_to_operand_aliasing={{0}: (4, {}), {1}: (5, {}), {2}: (6, {})} | custom-call | flops 1 | bytes 1 | tf_op jit(solution)/shard_map/last/pallas_call | solution.py:541
Async XLA Ops:
  0.0 6.1 %copy-start.1 = (f32[16]{0:T(128)S(1)}, f32[16]{0:T(128)}, u32[]{:S(2)}) copy-start(f32[16]{0:T(128)} %near.17) | copy-start | bytes 196
  0.0 6.1 %copy-start = (s32[12]{0:T(128)S(1)}, s32[12]{0:T(128)}, u32[]{:S(2)}) copy-start(s32[12]{0:T(128)} %slots.17) | copy-start | bytes 148
  0.0 6.1 %copy-start.3 = (f32[16]{0:T(128)S(1)}, f32[16]{0:T(128)}, u32[]{:S(2)}) copy-start(f32[16]{0:T(128)} %lens.7) | copy-start | bytes 196
  0.0 6.1 %copy-start.2 = (s32[12]{0:T(128)S(1)}, s32[12]{0:T(128)}, u32[]{:S(2)}) copy-start(s32[12]{0:T(128)} %widths.7) | copy-start | bytes 148
  2.1 15.7 %collective-permute-start.2 = (f32[7,128,128]{2,1,0:T(8,128)S(1)}, f32[7,128,128]{2,1,0:T(8,128)S(1)}, u32[]{:S(2)}, u32[]{:S(2)}) collective-permute-start(f32[7,128,128]{2,1,0:T(8,128)S(1)} %get-tuple-element.37), channel_id=1, source_target_pairs={{0,16},{1,17},{2,18},{3,19},{4,20},{5,21},{6,22},{7,23},{8,24},{9,... | collective-permute-start | bytes 1376264 | tf_op jit(solution)/shard_map/ppermute | solution.py:479
  3.4 6.3 %collective-permute-start = (f32[6,144,128]{2,1,0:T(8,128)S(1)}, f32[6,144,128]{2,1,0:T(8,128)S(1)}, u32[]{:S(2)}, u32[]{:S(2)}) collective-permute-start(f32[6,144,128]{2,1,0:T(8,128)S(1)} %get-tuple-element.35), channel_id=1, source_target_pairs={{0,1},{1,0},{2,3},{3,2},{4,5},{5,4},{6,7},{7,6},{8,9},{9,8},{10,11... | collective-permute-start | bytes 1327112 | tf_op jit(solution)/shard_map/ppermute | solution.py:493
  3.5 6.2 %collective-permute-start.1 = (f32[6,144,128]{2,1,0:T(8,128)S(1)}, f32[6,144,128]{2,1,0:T(8,128)S(1)}, u32[]{:S(2)}, u32[]{:S(2)}) collective-permute-start(f32[6,144,128]{2,1,0:T(8,128)S(1)} %get-tuple-element.36), channel_id=1, source_target_pairs={{0,1},{1,0},{2,3},{3,2},{4,5},{5,4},{6,7},{7,6},{8,9},{9,8},{10,11... | collective-permute-start | bytes 1327112 | tf_op jit(solution)/shard_map/ppermute | solution.py:493
  4.0 21.2 %collective-permute-start.3 = (f32[12,96,128]{2,1,0:T(8,128)S(1)}, f32[12,96,128]{2,1,0:T(8,128)S(1)}, u32[]{:S(2)}, u32[]{:S(2)}) collective-permute-start(f32[12,96,128]{2,1,0:T(8,128)S(1)} %get-tuple-element.40), channel_id=1, source_target_pairs={{1,2},{2,1},{3,4},{4,3},{5,6},{6,5},{7,8},{8,7},{9,10},{10,9},{11,... | collective-permute-start | bytes 1769480 | tf_op jit(solution)/shard_map/ppermute | solution.py:493
  8.4 16.8 %collective-permute-start.4 = (f32[7,96,128]{2,1,0:T(8,128)S(1)}, f32[7,96,128]{2,1,0:T(8,128)S(1)}, u32[]{:S(2)}, u32[]{:S(2)}) collective-permute-start(f32[7,96,128]{2,1,0:T(8,128)S(1)} %get-tuple-element.41), channel_id=1, source_target_pairs={{0,16},{1,17},{2,18},{3,19},{4,20},{5,21},{6,22},{7,23},{8,24},{9,... | collective-permute-start | bytes 1032200 | tf_op jit(solution)/shard_map/ppermute | solution.py:492
  18.5 20.5 %collective-permute-start.7 = (f32[7,144,128]{2,1,0:T(8,128)S(1)}, f32[7,144,128]{2,1,0:T(8,128)S(1)}, u32[]{:S(2)}, u32[]{:S(2)}) collective-permute-start(f32[7,144,128]{2,1,0:T(8,128)S(1)} %get-tuple-element.53), channel_id=1, source_target_pairs={{0,16},{1,17},{2,18},{3,19},{4,20},{5,21},{6,22},{7,23},{8,24},{9,... | collective-permute-start | bytes 1548296 | tf_op jit(solution)/shard_map/ppermute | solution.py:512
  19.8 11.2 %collective-permute-start.5 = (f32[12,48,128]{2,1,0:T(8,128)S(1)}, f32[12,48,128]{2,1,0:T(8,128)S(1)}, u32[]{:S(2)}, u32[]{:S(2)}) collective-permute-start(f32[12,48,128]{2,1,0:T(8,128)S(1)} %get-tuple-element.44), channel_id=1, source_target_pairs={{1,2},{2,1},{3,4},{4,3},{5,6},{6,5},{7,8},{8,7},{9,10},{10,9},{11,... | collective-permute-start | bytes 884744 | tf_op jit(solution)/shard_map/ppermute | solution.py:493
  29.5 14.1 %collective-permute-start.8 = (f32[7,96,128]{2,1,0:T(8,128)S(1)}, f32[7,96,128]{2,1,0:T(8,128)S(1)}, u32[]{:S(2)}, u32[]{:S(2)}) collective-permute-start(f32[7,96,128]{2,1,0:T(8,128)S(1)} %get-tuple-element.56), channel_id=1, source_target_pairs={{0,16},{1,17},{2,18},{3,19},{4,20},{5,21},{6,22},{7,23},{8,24},{9,... | collective-permute-start | bytes 1032200 | tf_op jit(solution)/shard_map/ppermute | solution.py:512
  35.2 11.2 %collective-permute-start.6 = (f32[7,48,128]{2,1,0:T(8,128)S(1)}, f32[7,48,128]{2,1,0:T(8,128)S(1)}, u32[]{:S(2)}, u32[]{:S(2)}) collective-permute-start(f32[7,48,128]{2,1,0:T(8,128)S(1)} %get-tuple-element.46), channel_id=1, source_target_pairs={{0,16},{1,17},{2,18},{3,19},{4,20},{5,21},{6,22},{7,23},{8,24},{9,... | collective-permute-start | bytes 516104 | tf_op jit(solution)/shard_map/ppermute | solution.py:512

commit v10 on v9

--- a/solution.py
+++ b/solution.py
@@ -217,7 +217,8 @@
     first, count = first_row(rows, part) + RIM, group_sizes(rows)[part]
     steps, per = steps_of(planes, shares)
     for beside_ref in beside_refs:
-        beside_ref[...] = jnp.zeros(beside_ref.shape, F32)
+        for at in range(count + 1):
+            beside_ref[:, pl.ds(at * (blocks + SUB), SUB), :] = jnp.zeros((3, SUB, LANES), F32)
 
     def step(index, carry):
         ks = []

time: 48.5 us -> 48.5 us (level)
  transfers between devices with their start and end apart: 9 -> 9, of which waited for: 5 -> 5; matrix products, arithmetic and copies ran while one was open for 0% -> 0% of each run, Pallas kernels for 38% -> 37%
where the time goes in v10:
time: 48.5 us; the launch traced here: 48.3 us
  Pallas kernels  21.7 us (45%)
  waiting for transfers between devices  15.4 us (32%)
  starting transfers between devices  11 us (23%)
    pallas_call x3, Pallas kernels, per_device(): pl.pallas_call(functools.partial(border_kernel, sizes, part), out_shape=[...  8.88 us
    ppermute x1, waiting for transfers between devices, per_device(): lax.ppermute(state, 'depth', ahead)  8.15 us
    ppermute x4, waiting for transfers between devices, per_device(): arriving.append(lax.ppermute(state, 'depth', ahead))  6.88 us
    ppermute x4, starting transfers between devices, per_device(): arriving.append(lax.ppermute(state, 'depth', ahead))  5.17 us
    pallas_call x4, Pallas kernels, per_device(): pl.pallas_call(functools.partial(resume_kernel, sizes, part, turn), out_s...  5.04 us
    ppermute x4, starting transfers between devices, per_device(): lax.ppermute(piece, 'sky', swaps[part > 2])  4.57 us
    pallas_call x1, Pallas kernels, per_device(): pl.pallas_call(functools.partial(second_kernel, sizes), out_shape=group_s...  2.2 us
    pallas_call x1, Pallas kernels, per_device(): pl.pallas_call(functools.partial(first_kernel, sizes), out_shape=[x_shape...  2.06 us
  transfers between devices with their start and end apart: 9, of which 5 were waited for; matrix products, arithmetic and copies ran while one was open for 0% of the time, Pallas kernels for 37%

profile of v10, /device:TPU:6, one launch (start us, length us, event | category | flops | bytes accessed | tf_op | source)
XLA Modules:
  0.0 48.3 jit_solution(4558760575282330643)
XLA Ops:
  0.0 0.0 copy-start.1
  0.0 0.0 copy-start
  0.0 0.0 copy-start.3
  0.0 0.0 copy-start.2
  0.0 2.1 %first.1 = (f32[12,800,128]{2,1,0:T(8,128)S(1)}, bf16[8,3,128,256]{3,2,1,0:T(8,128)(2,1)S(1)}, f32[12,3,128,128]{3,2,1,0:T(8,128)S(1)}, f32[12,128,128]{2,1,0:T(...) custom-call(s32[12]{0:T(128)} %widths.7, ...), custom_call_target="tpu_custom_call" | custom-call | flops 1 | bytes 1 | tf_op jit(solution)/shard_map/first/pallas_call | solution.py:468
  2.1 1.3 %collective-permute-start.2 = (f32[7,128,128]{2,1,0:T(8,128)S(1)}, f32[7,128,128]{2,1,0:T(8,128)S(1)}, u32[]{:S(2)}, u32[]{:S(2)}) collective-permute-start(f32[7,128,128]{2,1,0:T(8,128)S(1)} %get-tuple-element.37), channel_id=1, source_target_pairs={{0,16},{1,17},{2,18},{3,19},{4,20},{5,21},{6,22},{7,23},{8,24},{9,... | collective-permute-start | bytes 1376264 | tf_op jit(solution)/shard_map/ppermute | solution.py:480
  3.4 0.1 collective-permute-start
  3.5 0.5 %collective-permute-start.1 = (f32[6,144,128]{2,1,0:T(8,128)S(1)}, f32[6,144,128]{2,1,0:T(8,128)S(1)}, u32[]{:S(2)}, u32[]{:S(2)}) collective-permute-start(f32[6,144,128]{2,1,0:T(8,128)S(1)} %get-tuple-element.36), channel_id=1, source_target_pairs={{0,1},{1,0},{2,3},{3,2},{4,5},{5,4},{6,7},{7,6},{8,9},{9,8},{10,11... | collective-permute-start | bytes 1327112 | tf_op jit(solution)/shard_map/ppermute | solution.py:494
  4.0 2.1 %collective-permute-start.3 = (f32[12,96,128]{2,1,0:T(8,128)S(1)}, f32[12,96,128]{2,1,0:T(8,128)S(1)}, u32[]{:S(2)}, u32[]{:S(2)}) collective-permute-start(f32[12,96,128]{2,1,0:T(8,128)S(1)} %get-tuple-element.40), channel_id=1, source_target_pairs={{1,2},{2,1},{3,4},{4,3},{5,6},{6,5},{7,8},{8,7},{9,10},{10,9},{11,... | collective-permute-start | bytes 1769480 | tf_op jit(solution)/shard_map/ppermute | solution.py:494
  6.1 0.0 copy-done.1
  6.1 0.0 copy-done
  6.1 0.0 copy-done.3
  6.1 0.0 copy-done.2
  6.1 2.2 %second.1 = (f32[12,3,96,128]{3,2,1,0:T(8,128)S(1)}, f32[12,96,128]{2,1,0:T(8,128)S(1)}, f32[7,96,128]{2,1,0:T(8,128)S(1)}) custom-call(s32[12]{0:T(128)S(1)} %copy-done.2, s32[12]{0:T(128)S(1)} %copy-done, f32[16]{0:T(128)S(1)} %copy-done.1, f32[16]{0:T(128)S(1)} %copy-done.3, bf16[8,3,128,256]{3,2,1,0:T(8,128)(2,1)S(1)} %get-tuple-element.33.band_ref, ...), custom_call_target="tpu_custom_call" | custom-call | flops 1 | bytes 1 | tf_op jit(solution)/shard_map/second/pallas_call | solution.py:481
  8.3 1.3 %collective-permute-start.4 = (f32[7,96,128]{2,1,0:T(8,128)S(1)}, f32[7,96,128]{2,1,0:T(8,128)S(1)}, u32[]{:S(2)}, u32[]{:S(2)}) collective-permute-start(f32[7,96,128]{2,1,0:T(8,128)S(1)} %get-tuple-element.41), channel_id=1, source_target_pairs={{0,16},{1,17},{2,18},{3,19},{4,20},{5,21},{6,22},{7,23},{8,24},{9,... | collective-permute-start | bytes 1032200 | tf_op jit(solution)/shard_map/ppermute | solution.py:493
  9.6 0.0 collective-permute-done.refs_0_
  9.6 0.0 collective-permute-done.1.refs_1_
  9.6 8.1 %collective-permute-done.2.refs_2_.incoming = f32[7,128,128]{2,1,0:T(8,128)S(1)} collective-permute-done((f32[7,128,128]{2,1,0:T(8,128)S(1)}, f32[7,128,128]{2,1,0:T(8,128)S(1)}, u32[]{:S(2)}, u32[]{:S(2)}) %collective-permute-start.2) | collective-permute-done | bytes 458784 | tf_op jit(solution)/shard_map/ppermute | solution.py:480
  17.8 0.7 %border.3 = (f32[12,800,128]{2,1,0:T(8,128)S(1)}, f32[12,3,144,128]{3,2,1,0:T(8,128)S(1)}, f32[12,144,128]{2,1,0:T(8,128)S(1)}, f32[7,144,128]{2,1,0:T(8,128)S(1)}) custom-call(s32[12]{0:T(128)S(1)} %copy-done.2, s32[12]{0:T(128)S(1)} %copy-done, f32[16]{0:T(128)S(1)} %copy-done.1, f32[16]{0:T(128)S(1)} %copy-done.3, ...), custom_call_target="tpu_custom_call", output_to_operand_aliasing={{0}: (5, {})} | custom-call | flops 1 | bytes 1 | tf_op jit(solution)/shard_map/border/pallas_call | solution.py:498
  18.5 1.3 %collective-permute-start.7 = (f32[7,144,128]{2,1,0:T(8,128)S(1)}, f32[7,144,128]{2,1,0:T(8,128)S(1)}, u32[]{:S(2)}, u32[]{:S(2)}) collective-permute-start(f32[7,144,128]{2,1,0:T(8,128)S(1)} %get-tuple-element.53), channel_id=1, source_target_pairs={{0,16},{1,17},{2,18},{3,19},{4,20},{5,21},{6,22},{7,23},{8,24},{9,... | collective-permute-start | bytes 1548296 | tf_op jit(solution)/shard_map/ppermute | solution.py:513
  19.8 1.9 %collective-permute-start.5 = (f32[12,48,128]{2,1,0:T(8,128)S(1)}, f32[12,48,128]{2,1,0:T(8,128)S(1)}, u32[]{:S(2)}, u32[]{:S(2)}) collective-permute-start(f32[12,48,128]{2,1,0:T(8,128)S(1)} %get-tuple-element.44), channel_id=1, source_target_pairs={{1,2},{2,1},{3,4},{4,3},{5,6},{6,5},{7,8},{8,7},{9,10},{10,9},{11,... | collective-permute-start | bytes 884744 | tf_op jit(solution)/shard_map/ppermute | solution.py:494
  21.7 3.5 %collective-permute-done.4.refs_2_.incoming = f32[7,96,128]{2,1,0:T(8,128)S(1)} collective-permute-done((f32[7,96,128]{2,1,0:T(8,128)S(1)}, f32[7,96,128]{2,1,0:T(8,128)S(1)}, u32[]{:S(2)}, u32[]{:S(2)}) %collective-permute-start.4) | collective-permute-done | bytes 344096 | tf_op jit(solution)/shard_map/ppermute | solution.py:493
  25.1 0.0 collective-permute-done.3.refs_1_
  25.2 4.2 %border.4 = (f32[12,800,128]{2,1,0:T(8,128)S(1)}, f32[12,3,96,128]{3,2,1,0:T(8,128)S(1)}, f32[12,96,128]{2,1,0:T(8,128)S(1)}, f32[7,96,128]{2,1,0:T(8,128)S(1)}, f32[12,3,128,128]{3,2,1,0:T(8,128)S(1)}) custom-call(s32[12]{0:T(128)S(1)} %copy-done.2, s32[12]{0:T(128)S(1)} %copy-done, f32[16]{0:T(128)S(1)} %copy-done.1, ...), custom_call_target="tpu_custom_call", output_to_operand_aliasing={{0}: (5, {}), {4}: (6, {})} | custom-call | flops 1 | bytes 1 | tf_op jit(solution)/shard_map/border/pallas_call | solution.py:498
  29.3 1.3 %collective-permute-start.8 = (f32[7,96,128]{2,1,0:T(8,128)S(1)}, f32[7,96,128]{2,1,0:T(8,128)S(1)}, u32[]{:S(2)}, u32[]{:S(2)}) collective-permute-start(f32[7,96,128]{2,1,0:T(8,128)S(1)} %get-tuple-element.56), channel_id=1, source_target_pairs={{0,16},{1,17},{2,18},{3,19},{4,20},{5,21},{6,22},{7,23},{8,24},{9,... | collective-permute-start | bytes 1032200 | tf_op jit(solution)/shard_map/ppermute | solution.py:513
  30.6 0.3 collective-permute-done.5.refs_1_
  31.0 4.0 %border.5 = (f32[12,800,128]{2,1,0:T(8,128)S(1)}, f32[12,3,48,128]{3,2,1,0:T(8,128)S(1)}, f32[12,48,128]{2,1,0:T(8,128)S(1)}, f32[7,48,128]{2,1,0:T(8,128)S(1)}, f32[12,3,144,128]{3,2,1,0:T(8,128)S(1)}) custom-call(s32[12]{0:T(128)S(1)} %copy-done.2, s32[12]{0:T(128)S(1)} %copy-done, f32[16]{0:T(128)S(1)} %copy-done.1, ...), custom_call_target="tpu_custom_call", output_to_operand_aliasing={{0}: (5, {}), {4}: (6, {})} | custom-call | flops 1 | bytes 1 | tf_op jit(solution)/shard_map/border/pallas_call | solution.py:498
  35.0 1.3 %collective-permute-start.6 = (f32[7,48,128]{2,1,0:T(8,128)S(1)}, f32[7,48,128]{2,1,0:T(8,128)S(1)}, u32[]{:S(2)}, u32[]{:S(2)}) collective-permute-start(f32[7,48,128]{2,1,0:T(8,128)S(1)} %get-tuple-element.46), channel_id=1, source_target_pairs={{0,16},{1,17},{2,18},{3,19},{4,20},{5,21},{6,22},{7,23},{8,24},{9,... | collective-permute-start | bytes 516104 | tf_op jit(solution)/shard_map/ppermute | solution.py:513
  36.3 1.3 %resume.4.behind.refs_0_ = f32[12,128,128]{2,1,0:T(8,128)S(1)} custom-call(s32[12]{0:T(128)S(1)} %copy-done, f32[16]{0:T(128)S(1)} %copy-done.1, f32[12,3,128,128]{3,2,1,0:T(8,128)S(1)} %get-tuple-element.48.entry_ref, f32[7,128,128]{2,1,0:T(8,128)S(1)} %collective-permute-done.2.refs_2_.incoming, ...), custom_call_target="tpu_custom_call", output_to_operand_aliasing={{}: (4, {})} | custom-call | flops 1 | bytes 1 | tf_op jit(solution)/shard_map/resume/pallas_call | solution.py:518
  37.6 1.1 %resume.5.behind.refs_1_ = f32[12,96,128]{2,1,0:T(8,128)S(1)} custom-call(s32[12]{0:T(128)S(1)} %copy-done, f32[16]{0:T(128)S(1)} %copy-done.1, f32[12,3,96,128]{3,2,1,0:T(8,128)S(1)} %get-tuple-element.50.entry_ref, f32[7,96,128]{2,1,0:T(8,128)S(1)} %collective-permute-done.4.refs_2_.incoming, ...), custom_call_target="tpu_custom_call", output_to_operand_aliasing={{}: (4, {})} | custom-call | flops 1 | bytes 1 | tf_op jit(solution)/shard_map/resume/pallas_call | solution.py:518
  38.8 0.0 collective-permute-done.7.incoming
  38.8 1.4 %resume.6.behind.refs_2_ = f32[12,144,128]{2,1,0:T(8,128)S(1)} custom-call(s32[12]{0:T(128)S(1)} %copy-done, f32[16]{0:T(128)S(1)} %copy-done.1, f32[12,3,144,128]{3,2,1,0:T(8,128)S(1)} %get-tuple-element.52.entry_ref, f32[7,144,128]{2,1,0:T(8,128)S(1)} %collective-permute-done.7.incoming, ...), custom_call_target="tpu_custom_call", output_to_operand_aliasing={{}: (4, {})} | custom-call | flops 1 | bytes 1 | tf_op jit(solution)/shard_map/resume/pallas_call | solution.py:518
  40.2 3.4 %collective-permute-done.8.incoming = f32[7,96,128]{2,1,0:T(8,128)S(1)} collective-permute-done((f32[7,96,128]{2,1,0:T(8,128)S(1)}, f32[7,96,128]{2,1,0:T(8,128)S(1)}, u32[]{:S(2)}, u32[]{:S(2)}) %collective-permute-start.8) | collective-permute-done | bytes 344096 | tf_op jit(solution)/shard_map/ppermute | solution.py:513
  43.6 1.1 %resume.7.refs_3_ = f32[12,96,128]{2,1,0:T(8,128)S(1)} custom-call(s32[12]{0:T(128)S(1)} %copy-done, f32[16]{0:T(128)S(1)} %copy-done.1, f32[12,3,96,128]{3,2,1,0:T(8,128)S(1)} %get-tuple-element.55.entry_ref, f32[7,96,128]{2,1,0:T(8,128)S(1)} %collective-permute-done.8.incoming, ...), custom_call_target="tpu_custom_call", output_to_operand_aliasing={{}: (4, {})} | custom-call | flops 1 | bytes 1 | tf_op jit(solution)/shard_map/resume/pallas_call | solution.py:518
  44.7 1.6 %early.1 = (f32[12,576,128]{2,1,0:T(8,128)S(1)}, f32[12,512,128]{2,1,0:T(8,128)}) custom-call(f32[12,128,128]{2,1,0:T(8,128)S(1)} %resume.4.behind.refs_0_, f32[12,96,128]{2,1,0:T(8,128)S(1)} %resume.5.behind.refs_1_, f32[12,144,128]{2,1,0:T(8,128)S(1)} %resume.6.behind.refs_2_, f32[12,96,128]{2,1,0:T(8,128)S(1)} %resume.7.refs_3_), custom_call_target="tpu_custom_call" | custom-call | flops 1 | bytes 1 | tf_op jit(solution)/shard_map/early/pallas_call | solution.py:532
  46.4 0.1 collective-permute-done.6.incoming
  46.4 1.8 %last.1 = (f32[12,48,128]{2,1,0:T(8,128)S(1)}, f32[12,576,128]{2,1,0:T(8,128)S(1)}, f32[12,512,128]{2,1,0:T(8,128)}) custom-call(s32[12]{0:T(128)S(1)} %copy-done, f32[16]{0:T(128)S(1)} %copy-done.1, f32[12,3,48,128]{3,2,1,0:T(8,128)S(1)} %get-tuple-element.45.entry_ref, ...), custom_call_target="tpu_custom_call", output_to_operand_aliasing={{0}: (4, {}), {1}: (5, {}), {2}: (6, {})} | custom-call | flops 1 | bytes 1 | tf_op jit(solution)/shard_map/last/pallas_call | solution.py:542
Async XLA Ops:
  0.0 6.1 %copy-start.1 = (f32[16]{0:T(128)S(1)}, f32[16]{0:T(128)}, u32[]{:S(2)}) copy-start(f32[16]{0:T(128)} %near.17) | copy-start | bytes 196
  0.0 6.1 %copy-start = (s32[12]{0:T(128)S(1)}, s32[12]{0:T(128)}, u32[]{:S(2)}) copy-start(s32[12]{0:T(128)} %slots.17) | copy-start | bytes 148
  0.0 6.1 %copy-start.3 = (f32[16]{0:T(128)S(1)}, f32[16]{0:T(128)}, u32[]{:S(2)}) copy-start(f32[16]{0:T(128)} %lens.7) | copy-start | bytes 196
  0.0 6.1 %copy-start.2 = (s32[12]{0:T(128)S(1)}, s32[12]{0:T(128)}, u32[]{:S(2)}) copy-start(s32[12]{0:T(128)} %widths.7) | copy-start | bytes 148
  2.1 15.7 %collective-permute-start.2 = (f32[7,128,128]{2,1,0:T(8,128)S(1)}, f32[7,128,128]{2,1,0:T(8,128)S(1)}, u32[]{:S(2)}, u32[]{:S(2)}) collective-permute-start(f32[7,128,128]{2,1,0:T(8,128)S(1)} %get-tuple-element.37), channel_id=1, source_target_pairs={{0,16},{1,17},{2,18},{3,19},{4,20},{5,21},{6,22},{7,23},{8,24},{9,... | collective-permute-start | bytes 1376264 | tf_op jit(solution)/shard_map/ppermute | solution.py:480
  3.4 6.2 %collective-permute-start = (f32[6,144,128]{2,1,0:T(8,128)S(1)}, f32[6,144,128]{2,1,0:T(8,128)S(1)}, u32[]{:S(2)}, u32[]{:S(2)}) collective-permute-start(f32[6,144,128]{2,1,0:T(8,128)S(1)} %get-tuple-element.35), channel_id=1, source_target_pairs={{0,1},{1,0},{2,3},{3,2},{4,5},{5,4},{6,7},{7,6},{8,9},{9,8},{10,11... | collective-permute-start | bytes 1327112 | tf_op jit(solution)/shard_map/ppermute | solution.py:494
  3.5 6.2 %collective-permute-start.1 = (f32[6,144,128]{2,1,0:T(8,128)S(1)}, f32[6,144,128]{2,1,0:T(8,128)S(1)}, u32[]{:S(2)}, u32[]{:S(2)}) collective-permute-start(f32[6,144,128]{2,1,0:T(8,128)S(1)} %get-tuple-element.36), channel_id=1, source_target_pairs={{0,1},{1,0},{2,3},{3,2},{4,5},{5,4},{6,7},{7,6},{8,9},{9,8},{10,11... | collective-permute-start | bytes 1327112 | tf_op jit(solution)/shard_map/ppermute | solution.py:494
  4.0 21.2 %collective-permute-start.3 = (f32[12,96,128]{2,1,0:T(8,128)S(1)}, f32[12,96,128]{2,1,0:T(8,128)S(1)}, u32[]{:S(2)}, u32[]{:S(2)}) collective-permute-start(f32[12,96,128]{2,1,0:T(8,128)S(1)} %get-tuple-element.40), channel_id=1, source_target_pairs={{1,2},{2,1},{3,4},{4,3},{5,6},{6,5},{7,8},{8,7},{9,10},{10,9},{11,... | collective-permute-start | bytes 1769480 | tf_op jit(solution)/shard_map/ppermute | solution.py:494
  8.3 16.8 %collective-permute-start.4 = (f32[7,96,128]{2,1,0:T(8,128)S(1)}, f32[7,96,128]{2,1,0:T(8,128)S(1)}, u32[]{:S(2)}, u32[]{:S(2)}) collective-permute-start(f32[7,96,128]{2,1,0:T(8,128)S(1)} %get-tuple-element.41), channel_id=1, source_target_pairs={{0,16},{1,17},{2,18},{3,19},{4,20},{5,21},{6,22},{7,23},{8,24},{9,... | collective-permute-start | bytes 1032200 | tf_op jit(solution)/shard_map/ppermute | solution.py:493
  18.5 20.3 %collective-permute-start.7 = (f32[7,144,128]{2,1,0:T(8,128)S(1)}, f32[7,144,128]{2,1,0:T(8,128)S(1)}, u32[]{:S(2)}, u32[]{:S(2)}) collective-permute-start(f32[7,144,128]{2,1,0:T(8,128)S(1)} %get-tuple-element.53), channel_id=1, source_target_pairs={{0,16},{1,17},{2,18},{3,19},{4,20},{5,21},{6,22},{7,23},{8,24},{9,... | collective-permute-start | bytes 1548296 | tf_op jit(solution)/shard_map/ppermute | solution.py:513
  19.8 11.2 %collective-permute-start.5 = (f32[12,48,128]{2,1,0:T(8,128)S(1)}, f32[12,48,128]{2,1,0:T(8,128)S(1)}, u32[]{:S(2)}, u32[]{:S(2)}) collective-permute-start(f32[12,48,128]{2,1,0:T(8,128)S(1)} %get-tuple-element.44), channel_id=1, source_target_pairs={{1,2},{2,1},{3,4},{4,3},{5,6},{6,5},{7,8},{8,7},{9,10},{10,9},{11,... | collective-permute-start | bytes 884744 | tf_op jit(solution)/shard_map/ppermute | solution.py:494
  29.3 14.2 %collective-permute-start.8 = (f32[7,96,128]{2,1,0:T(8,128)S(1)}, f32[7,96,128]{2,1,0:T(8,128)S(1)}, u32[]{:S(2)}, u32[]{:S(2)}) collective-permute-start(f32[7,96,128]{2,1,0:T(8,128)S(1)} %get-tuple-element.56), channel_id=1, source_target_pairs={{0,16},{1,17},{2,18},{3,19},{4,20},{5,21},{6,22},{7,23},{8,24},{9,... | collective-permute-start | bytes 1032200 | tf_op jit(solution)/shard_map/ppermute | solution.py:513
  35.0 11.4 %collective-permute-start.6 = (f32[7,48,128]{2,1,0:T(8,128)S(1)}, f32[7,48,128]{2,1,0:T(8,128)S(1)}, u32[]{:S(2)}, u32[]{:S(2)}) collective-permute-start(f32[7,48,128]{2,1,0:T(8,128)S(1)} %get-tuple-element.46), channel_id=1, source_target_pairs={{0,16},{1,17},{2,18},{3,19},{4,20},{5,21},{6,22},{7,23},{8,24},{9,... | collective-permute-start | bytes 516104 | tf_op jit(solution)/shard_map/ppermute | solution.py:513
